TPU v7x, 32 devices: a whole 2x2x4 slice. The times are simulated.
32 devices in a mesh: role: 2 (over core), dp: 16 (over z, y, x).
Axes of the slice: x: 2, y: 2, z: 4, core: 2. Of those that a mesh axis runs over, the one named last changes fastest.
Arguments:
- frames: bfloat16 [32, 384, 512], P('dp'), may hold values from -6 to 6
- step_lengths: int32 [32], P('dp'), may hold values from 48 to 192, as said below
- characters: int32 [16, 2, 72], P('dp', 'role'), may hold values from 0 to 29
- char_lengths: int32 [16, 2], P('dp', 'role'), may hold values from 18 to 72, as said below
- listen_input: bfloat16 [2, 1024, 1024], P('role'), may hold values from -0.1875 to 0.1875
- listen_hidden: bfloat16 [2, 256, 1024], P('role'), may hold values from -0.375 to 0.375
- listen_bias: bfloat16 [2, 1024], P('role'), may hold values from -3 to 7
- lower_input: bfloat16 [768, 2048], replicated, may hold values from -0.21875 to 0.21875
- lower_hidden: bfloat16 [512, 2048], replicated, may hold values from -0.25 to 0.25
- lower_bias: bfloat16 [2048], replicated, may hold values from -3 to 7
- upper_input: bfloat16 [512, 2048], replicated, may hold values from -0.25 to 0.25
- upper_hidden: bfloat16 [512, 2048], replicated, may hold values from -0.25 to 0.25
- upper_bias: bfloat16 [2048], replicated, may hold values from -3 to 7
- key_proj: bfloat16 [512, 512], replicated, may hold values from -0.5 to 0.5
- query_proj: bfloat16 [512, 512], replicated, may hold values from -0.5 to 0.5
- score_vector: bfloat16 [512], replicated, may hold values from -1 to 1
- output_proj: bfloat16 [1024, 30], replicated, may hold values from -1.5 to 1.5
- output_bias: bfloat16 [30], replicated, may hold values from -4 to 4
- char_table: bfloat16 [30, 256], replicated, may hold values from -5 to 5
Outputs:
- loss: float32 [16, 2], P('dp', 'role')
- frames_grad: float32 [32, 384, 512], P('dp', 'role')
- grad_listen_input: float32 [2, 1024, 1024], P('role')
- grad_listen_hidden: float32 [2, 256, 1024], P('role')
- grad_listen_bias: float32 [2, 1024], P('role')
- grad_lower_input: float32 [768, 2048], replicated
- grad_lower_hidden: float32 [512, 2048], replicated
- grad_lower_bias: float32 [2048], replicated
- grad_upper_input: float32 [512, 2048], replicated
- grad_upper_hidden: float32 [512, 2048], replicated
- grad_upper_bias: float32 [2048], replicated
- grad_key_proj: float32 [512, 512], replicated
- grad_query_proj: float32 [512, 512], replicated
- grad_score_vector: float32 [512], replicated
- grad_output_proj: float32 [1024, 30], replicated
- grad_output_bias: float32 [30], replicated
- grad_char_table: float32 [30, 256], replicated
Inputs may be any that keep to these rules, and one draw needn't show every extreme that they name: `step_lengths`: every draw has an utterance of 192 frame pairs. `char_lengths`: every draw has a transcript of 72 characters.
All inputs are finite; a program needn't handle non-finite values.
Results may differ from a plain program's by a relative error of at most 0.008.
Values may be sent and summed in bfloat16 or wider, within the bound.
A program may use at most 192 MiB of HBM per device.

v0:
```python
import jax
import jax.numpy as jnp
from jax import lax
from jax.sharding import PartitionSpec as P


def product(left, right):
    return jnp.dot(left, right, preferred_element_type=jnp.float32)


def lstm_cell(preact, cell_prev):
    quarter = preact.shape[-1] // 4
    in_gate = jax.nn.sigmoid(preact[..., :quarter])
    forget = jax.nn.sigmoid(preact[..., quarter : 2 * quarter])
    candid = jnp.tanh(preact[..., 2 * quarter : 3 * quarter])
    out_gate = jax.nn.sigmoid(preact[..., 3 * quarter :])
    cell_new = forget * cell_prev + in_gate * candid
    gate_acts = jnp.concatenate([in_gate, forget, candid, out_gate], -1)
    return (gate_acts, cell_new, out_gate * jnp.tanh(cell_new))


def lstm_back(gate_acts, cell_prev, cell_new, grad_hidden, grad_cell):
    quarter = gate_acts.shape[-1] // 4
    in_gate = gate_acts[..., :quarter]
    forget = gate_acts[..., quarter : 2 * quarter]
    candid = gate_acts[..., 2 * quarter : 3 * quarter]
    out_gate = gate_acts[..., 3 * quarter :]
    tanh_cell = jnp.tanh(cell_new)
    grad_total = grad_cell + grad_hidden * out_gate * (1.0 - tanh_cell * tanh_cell)
    grad_preact = jnp.concatenate(
        [
            grad_total * candid * in_gate * (1.0 - in_gate),
            grad_total * cell_prev * forget * (1.0 - forget),
            grad_total * in_gate * (1.0 - candid * candid),
            grad_hidden * tanh_cell * out_gate * (1.0 - out_gate),
        ],
        -1,
    )
    return (grad_preact, grad_total * forget)


def flatten_rows(array):
    return array.reshape(-1, array.shape[-1])


def spell(
    key_feats,
    own_lengths,
    chars_local,
    text_len,
    lower_input,
    lower_hidden,
    lower_bias,
    upper_input,
    upper_hidden,
    upper_bias,
    key_proj,
    query_proj,
    score_vector,
    output_proj,
    output_bias,
    char_table,
):
    batch_rows, time_len, _ = key_feats.shape
    text_steps = chars_local.shape[1]
    vocab_size, embed_width = char_table.shape
    units = lower_hidden.shape[0]
    keys_proj = jnp.einsum("btd,da->bta", key_feats, key_proj, preferred_element_type=jnp.float32)
    frame_ok = jnp.arange(time_len)[None, :] < own_lengths[:, None]
    previous = jnp.concatenate([jnp.zeros((batch_rows, 1), jnp.int32), chars_local[:, :-1]], 1)
    prev_onehot = (previous.T[..., None] == jnp.arange(vocab_size)[None, None, :]).astype(
        jnp.bfloat16
    )
    embedded = jnp.einsum(
        "cbv,ve->cbe", prev_onehot, char_table, preferred_element_type=jnp.float32
    ).astype(jnp.bfloat16)
    target_onehot = (chars_local.T[..., None] == jnp.arange(vocab_size)[None, None, :]).astype(
        jnp.float32
    )
    text_lengths = text_len.astype(jnp.float32)
    text_mask = (jnp.arange(text_steps)[:, None] < text_len[None, :]).astype(jnp.float32)
    scale_cols = text_mask / text_lengths[None, :]
    vector = score_vector.astype(jnp.float32)
    bias_lower = lower_bias.astype(jnp.float32)
    bias_upper = upper_bias.astype(jnp.float32)
    bias_output = output_bias.astype(jnp.float32)

    def forward_step(carried, inputs):
        hidden_one, cell_one, hidden_two, cell_two, context_low = carried
        emb_t, target_t = inputs
        joined = jnp.concatenate([emb_t, context_low], -1)
        one_low = hidden_one.astype(jnp.bfloat16)
        preact_one = product(joined, lower_input) + product(one_low, lower_hidden) + bias_lower
        acts_one, cell_one_new, hidden_one_new = lstm_cell(preact_one, cell_one)
        lower_out = hidden_one_new.astype(jnp.bfloat16)
        two_low = hidden_two.astype(jnp.bfloat16)
        preact_two = product(lower_out, upper_input) + product(two_low, upper_hidden) + bias_upper
        acts_two, cell_two_new, hidden_two_new = lstm_cell(preact_two, cell_two)
        upper_out = hidden_two_new.astype(jnp.bfloat16)
        query_vec = product(upper_out, query_proj)
        energy = jnp.tanh(keys_proj + query_vec[:, None, :])
        scores = jnp.dot(energy, vector, precision=lax.Precision.HIGHEST)
        scores = jnp.where(frame_ok, scores, -1000000000.0)
        weights = jax.nn.softmax(scores, axis=-1)
        weights_low = weights.astype(jnp.bfloat16)
        context = jnp.einsum(
            "bt,btd->bd", weights_low, key_feats, preferred_element_type=jnp.float32
        )
        context_new = context.astype(jnp.bfloat16)
        out_feat = jnp.concatenate([upper_out, context_new], -1)
        logits = product(out_feat, output_proj) + bias_output
        log_total = jax.nn.logsumexp(logits, axis=-1)
        char_probs = jnp.exp(logits - log_total[:, None])
        cross = log_total - jnp.sum(logits * target_t, -1)
        saved = (
            joined,
            one_low,
            acts_one,
            cell_one,
            cell_one_new,
            lower_out,
            two_low,
            acts_two,
            cell_two,
            cell_two_new,
            upper_out,
            query_vec,
            weights,
            weights_low,
            out_feat,
            char_probs,
        )
        return (
            (hidden_one_new, cell_one_new, hidden_two_new, cell_two_new, context_new),
            (saved, cross),
        )

    zeros_state = jnp.zeros((batch_rows, units), jnp.float32)
    zeros_ctx = jnp.zeros((batch_rows, key_feats.shape[-1]), jnp.bfloat16)
    _, (saved, crosses) = lax.scan(
        forward_step,
        (zeros_state, zeros_state, zeros_state, zeros_state, zeros_ctx),
        (embedded, target_onehot),
    )
    losses = jnp.sum(crosses * text_mask, 0) / text_lengths

    def backward_step(carried, inputs):
        grad_one, gcell_one, grad_two, gcell_two, grad_ctx, grad_keys_acc, grad_vector = carried
        (
            (
                joined,
                one_low,
                acts_one,
                cell_one,
                cell_one_new,
                lower_out,
                two_low,
                acts_two,
                cell_two,
                cell_two_new,
                upper_out,
                query_vec,
                weights,
                weights_low,
                out_feat,
                char_probs,
            ),
            target_t,
            scale_t,
        ) = inputs
        logit_grad = (scale_t[:, None] * (char_probs - target_t)).astype(jnp.bfloat16)
        grad_feat = product(logit_grad, output_proj.T)
        grad_top = grad_feat[:, :units]
        context_grad = (grad_feat[:, units:] + grad_ctx).astype(jnp.bfloat16)
        grad_weights = jnp.einsum(
            "bd,btd->bt", context_grad, key_feats, preferred_element_type=jnp.float32
        )
        grad_scores = weights * (grad_weights - jnp.sum(weights * grad_weights, -1, keepdims=True))
        energy = jnp.tanh(keys_proj + query_vec[:, None, :])
        grad_vector = grad_vector + jnp.einsum(
            "bt,bta->a", grad_scores, energy, precision=lax.Precision.HIGHEST
        )
        grad_energy = grad_scores[..., None] * vector * (1.0 - energy * energy)
        grad_keys_acc = grad_keys_acc + grad_energy
        query_grad = jnp.sum(grad_energy, 1).astype(jnp.bfloat16)
        grad_two_total = grad_two + grad_top + product(query_grad, query_proj.T)
        preact_two_grad, gcell_two_prev = lstm_back(
            acts_two, cell_two, cell_two_new, grad_two_total, gcell_two
        )
        two_grad_low = preact_two_grad.astype(jnp.bfloat16)
        grad_one_total = grad_one + product(two_grad_low, upper_input.T)
        grad_two_prev = product(two_grad_low, upper_hidden.T)
        preact_one_grad, gcell_one_prev = lstm_back(
            acts_one, cell_one, cell_one_new, grad_one_total, gcell_one
        )
        one_grad_low = preact_one_grad.astype(jnp.bfloat16)
        grad_joined = product(one_grad_low, lower_input.T)
        grad_one_prev = product(one_grad_low, lower_hidden.T)
        new_carry = (
            grad_one_prev,
            gcell_one_prev,
            grad_two_prev,
            gcell_two_prev,
            grad_joined[:, embed_width:],
            grad_keys_acc,
            grad_vector,
        )
        return (
            new_carry,
            (
                logit_grad,
                context_grad,
                query_grad,
                two_grad_low,
                one_grad_low,
                grad_joined[:, :embed_width],
            ),
        )

    zeros_grad_ctx = jnp.zeros((batch_rows, key_feats.shape[-1]), jnp.float32)
    init = (
        zeros_state,
        zeros_state,
        zeros_state,
        zeros_state,
        zeros_grad_ctx,
        jnp.zeros_like(keys_proj),
        jnp.zeros_like(vector),
    )
    final, outputs = lax.scan(backward_step, init, (saved, target_onehot, scale_cols), reverse=True)
    grad_keys_acc, grad_vector = (final[5], final[6])
    logit_grad, context_grad, query_grad, two_grad_low, one_grad_low, grad_emb = outputs
    (
        joined,
        one_low,
        _,
        _,
        _,
        lower_out,
        two_low,
        _,
        _,
        _,
        upper_out,
        _,
        _,
        weights_low,
        out_feat,
        _,
    ) = saved
    grad_lower_in = product(flatten_rows(joined).T, flatten_rows(one_grad_low))
    grad_lower_rec = product(flatten_rows(one_low).T, flatten_rows(one_grad_low))
    grad_lower_bias = jnp.sum(flatten_rows(one_grad_low).astype(jnp.float32), 0)
    grad_upper_in = product(flatten_rows(lower_out).T, flatten_rows(two_grad_low))
    grad_upper_rec = product(flatten_rows(two_low).T, flatten_rows(two_grad_low))
    grad_upper_bias = jnp.sum(flatten_rows(two_grad_low).astype(jnp.float32), 0)
    grad_query_w = product(flatten_rows(upper_out).T, flatten_rows(query_grad))
    grad_out_w = product(flatten_rows(out_feat).T, flatten_rows(logit_grad))
    grad_out_bias = jnp.sum(flatten_rows(logit_grad).astype(jnp.float32), 0)
    grad_table = jnp.dot(
        flatten_rows(prev_onehot).astype(jnp.float32).T,
        flatten_rows(grad_emb),
        precision=lax.Precision.HIGHEST,
    )
    key_grad_low = grad_keys_acc.astype(jnp.bfloat16)
    grad_key_w = jnp.einsum(
        "btd,bta->da", key_feats, key_grad_low, preferred_element_type=jnp.float32
    )
    grad_keys = jnp.einsum(
        "bta,da->btd", key_grad_low, key_proj, preferred_element_type=jnp.float32
    )
    grad_keys = grad_keys + jnp.einsum(
        "cbt,cbd->btd", weights_low, context_grad, preferred_element_type=jnp.float32
    )
    grads = (
        grad_lower_in,
        grad_lower_rec,
        grad_lower_bias,
        grad_upper_in,
        grad_upper_rec,
        grad_upper_bias,
        grad_key_w,
        grad_query_w,
        grad_vector,
        grad_out_w,
        grad_out_bias,
        grad_table,
    )
    return (losses, grads, grad_keys)


def shards(
    frames,
    step_lengths,
    characters,
    char_lengths,
    listen_input,
    listen_hidden,
    listen_bias,
    lower_input,
    lower_hidden,
    lower_bias,
    upper_input,
    upper_hidden,
    upper_bias,
    key_proj,
    query_proj,
    score_vector,
    output_proj,
    output_bias,
    char_table,
):
    groups = lax.axis_size("role")
    role_index = lax.axis_index("role")
    reverse = role_index == 1
    utt_local, frame_len, feat_width = frames.shape
    time_len = frame_len // 2
    frame_pairs = frames.reshape(utt_local, time_len, 2 * feat_width)
    frame_mask = (jnp.arange(time_len)[None, :] < step_lengths[:, None]).astype(jnp.float32)
    pairs_dir = jnp.where(reverse, jnp.flip(frame_pairs, 1), frame_pairs)
    mask_dir = jnp.where(reverse, jnp.flip(frame_mask, 1), frame_mask)
    weight_in = listen_input[0]
    weight_rec = listen_hidden[0]
    units = weight_rec.shape[0]
    flat_pairs = pairs_dir.reshape(utt_local * time_len, 2 * feat_width)
    projected = product(flat_pairs, weight_in) + listen_bias[0].astype(jnp.float32)
    projected = projected.reshape(utt_local, time_len, 4 * units)

    def listen_step(carried, inputs):
        hidden, cell_state = carried
        proj_t, mask_t = inputs
        hidden_low = hidden.astype(jnp.bfloat16)
        preact = proj_t + product(hidden_low, weight_rec)
        gate_acts, cell_new, hidden_new = lstm_cell(preact, cell_state)
        mask_col = mask_t[:, None]
        hidden_next = mask_col * hidden_new + (1.0 - mask_col) * hidden
        cell_next = mask_col * cell_new + (1.0 - mask_col) * cell_state
        emitted = hidden_next.astype(jnp.bfloat16) * mask_col.astype(jnp.bfloat16)
        return ((hidden_next, cell_next), (emitted, hidden_low, gate_acts, cell_state, cell_new))

    zeros_state = jnp.zeros((utt_local, units), jnp.float32)
    _, (emitted, hidden_prev, gate_acts, cell_prev, cell_new) = lax.scan(
        listen_step, (zeros_state, zeros_state), (jnp.swapaxes(projected, 0, 1), mask_dir.T)
    )
    listen_out = jnp.swapaxes(jnp.where(reverse, jnp.flip(emitted, 0), emitted), 0, 1)
    spell_rows = utt_local // groups
    gathered = lax.all_gather(listen_out, "role", axis=2, tiled=True)
    key_feats = lax.dynamic_slice_in_dim(gathered, role_index * spell_rows, spell_rows, 0)
    own_lengths = lax.dynamic_slice_in_dim(step_lengths, role_index * spell_rows, spell_rows, 0)
    losses, speller_grads, grad_keys = spell(
        key_feats,
        own_lengths,
        characters[0],
        char_lengths[0],
        lower_input,
        lower_hidden,
        lower_bias,
        upper_input,
        upper_hidden,
        upper_bias,
        key_proj,
        query_proj,
        score_vector,
        output_proj,
        output_bias,
        char_table,
    )
    grad_keys_low = grad_keys.astype(jnp.bfloat16)
    padded = jnp.zeros((utt_local, time_len, 2 * units), jnp.float32)
    padded = lax.dynamic_update_slice_in_dim(
        padded, grad_keys_low.astype(jnp.float32), role_index * spell_rows, 0
    )
    grad_out = lax.psum_scatter(
        padded.astype(jnp.bfloat16), "role", scatter_dimension=2, tiled=True
    )
    grad_dir = jnp.where(reverse, jnp.flip(grad_out, 1), grad_out)

    def listen_back(carried, inputs):
        grad_hidden, grad_cell = carried
        acts_t, cprev_t, cnew_t, mask_t, gout_t = inputs
        mask_col = mask_t[:, None]
        grad_total = grad_hidden + mask_col * gout_t.astype(jnp.float32)
        grad_preact, cell_grad = lstm_back(
            acts_t, cprev_t, cnew_t, mask_col * grad_total, mask_col * grad_cell
        )
        preact_low = grad_preact.astype(jnp.bfloat16)
        hidden_prev_grad = (1.0 - mask_col) * grad_total + product(preact_low, weight_rec.T)
        cell_prev_grad = cell_grad + (1.0 - mask_col) * grad_cell
        return ((hidden_prev_grad, cell_prev_grad), preact_low)

    _, grad_pre = lax.scan(
        listen_back,
        (zeros_state, zeros_state),
        (gate_acts, cell_prev, cell_new, mask_dir.T, jnp.swapaxes(grad_dir, 0, 1)),
        reverse=True,
    )
    grad_rows = flatten_rows(jnp.swapaxes(grad_pre, 0, 1))
    hidden_rows = flatten_rows(jnp.swapaxes(hidden_prev, 0, 1))
    grad_in_w = product(flat_pairs.T, grad_rows)
    grad_rec_w = product(hidden_rows.T, grad_rows)
    grad_bias = jnp.sum(grad_rows.astype(jnp.float32), 0)
    grad_pairs = product(grad_rows, weight_in.T).reshape(utt_local, time_len, 2 * feat_width)
    grad_pairs = jnp.where(reverse, jnp.flip(grad_pairs, 1), grad_pairs)
    frame_grad = lax.psum_scatter(
        grad_pairs.reshape(utt_local, frame_len, feat_width),
        "role",
        scatter_dimension=1,
        tiled=True,
    )
    sum_in, sum_rec, sum_bias = lax.psum((grad_in_w, grad_rec_w, grad_bias), "dp")
    summed = lax.psum(
        (
            speller_grads[0],
            speller_grads[1],
            speller_grads[2],
            speller_grads[3],
            speller_grads[4],
            speller_grads[5],
            speller_grads[6],
            speller_grads[7],
            speller_grads[8],
            speller_grads[9],
            speller_grads[10],
            speller_grads[11],
        ),
        ("role", "dp"),
    )
    return (
        losses[None, :],
        frame_grad,
        sum_in[None],
        sum_rec[None],
        sum_bias[None],
        summed[0],
        summed[1],
        summed[2],
        summed[3],
        summed[4],
        summed[5],
        summed[6],
        summed[7],
        summed[8],
        summed[9],
        summed[10],
        summed[11],
    )


def solution(mesh):
    return jax.shard_map(
        shards,
        mesh=mesh,
        in_specs=(
            P("dp", None, None),
            P("dp"),
            P("dp", "role", None),
            P("dp", "role"),
            P("role", None, None),
            P("role", None, None),
            P("role", None),
            P(),
            P(),
            P(),
            P(),
            P(),
            P(),
            P(),
            P(),
            P(),
            P(),
            P(),
            P(),
        ),
        out_specs=(
            P("dp", "role"),
            P("dp", "role", None),
            P("role", None, None),
            P("role", None, None),
            P("role", None),
            P(),
            P(),
            P(),
            P(),
            P(),
            P(),
            P(),
            P(),
            P(),
            P(),
            P(),
            P(),
        ),
        check_vma=False,
    )
```

profile of v0, /device:TPU:0, one launch (start us, length us, event | category | flops | bytes accessed | tf_op | source)
XLA Modules:
  0.0 6359.3 jit_solution(769463236187959002)
XLA Ops:
  11.2 10.2 rev.21
  25.6 674.7 %while.138 = (s32[]{:T(128)}, f32[2,256]{1,0:T(2,128)S(1)}, f32[2,256]{1,0:T(2,128)S(1)}, bf16[192,2,256]{2,1,0:T(2,128)(2,1)}, bf16[192,2,256]{2,1,0:T(2,128)(2...) while((s32[]{:T(128)}, f32[2,256]{1,0:T(2,128)S(1)}, ...), condition=%wide.region_1.2_spmd.clone.clone, body=%wide.region_0.1_spmd.clone.sunk.clone | while | flops 1071623 | bytes 600286 | solution.py:342
  703.1 3.5 all_gather.3
  713.3 2381.2 %while.139 = (s32[]{:T(128)}, bf16[1,512]{1,0:T(2,128)(2,1)S(1)}, f32[1,512]{1,0:T(1,128)S(1)}, bf16[1,512]{1,0:T(2,128)(2,1)S(1)}, f32[1,512]{1,0:T(1,128)S(1)}...) while((s32[]{:T(128)}, bf16[1,512]{1,0:T(2,128)(2,1)S(1)}, ...), condition=%wide.region_8.9_spmd.clone.clone, body=%wide.region_2.8_spmd.clone.sunk.clone | while | flops 11552341 | bytes 36819692 | solution.py:140
  3099.8 1808.8 %while.140 = (s32[]{:T(128)}, f32[1,512]{1,0:T(1,128)S(1)}, f32[1,512]{1,0:T(1,128)}, f32[1,512]{1,0:T(1,128)S(1)}, f32[1,512]{1,0:T(1,128)}, /*index=5*/f32[1,5...) while((s32[]{:T(128)}, f32[1,512]{1,0:T(1,128)S(1)}, ...), condition=%wide.region_13.14_spmd.clone.clone, body=%wide.region_10.13_spmd.clone.sunk.clone | while | flops 12382135 | bytes 41453140 | solution.py:230
  4911.6 3.4 dynamic_update_slice.148
  4915.1 18.6 copy.65
  4933.7 35.1 reshape.1187
  4969.2 9.8 reduce-scatter.7.cloned.1.call-done
  4978.9 28.4 reshape.1188
  5007.4 12.2 copy.66
  5021.1 710.6 %while.141 = (s32[]{:T(128)}, f32[2,256]{1,0:T(2,128)S(1)}, f32[2,256]{1,0:T(2,128)S(1)}, bf16[192,2,1024]{2,1,0:T(2,128)(2,1)}, f32[192,2]{1,0:T(8,128)}, /*ind...) while((s32[]{:T(128)}, f32[2,256]{1,0:T(2,128)S(1)}, ...), condition=%wide.region_16.17_spmd.clone.clone, body=%wide.region_15.16_spmd.clone.sunk.clone | while | flops 1102342 | bytes 587988 | solution.py:391
  5731.6 3.3 fusion.123
  5734.9 16.1 rev.24
  5751.0 2.9 broadcast_select_fusion.10
  5759.0 4.5 convolution_bitcast_fusion.1
  5770.9 2.7 fusion.137
  5776.4 3.7 fusion.143
  5784.4 46.5 all-reduce
  5831.6 40.0 psum.107
  5871.6 94.6 %all-reduce.8.cloned.1.call-done = (f32[1,1024,1024]{2,1,0:T(8,128)}, f32[1,256,1024]{2,1,0:T(8,128)}) async-done(((f32[1,1024,1024]{2,1,0:T(8,128)}, f32[1,256,1024]{2,1,0:T(8,128)}), (f32[1,1024,1024]{2,1,0:T(8,128)}, f32[1,256,1024]{2,1,0:T(8,128)})) %all-reduce.8.cloned.1.call-update) | async-done | bytes 5242896 | tf_op jit(solution)/shard_map/psum | solution.py:410
  5966.3 362.4 %all-reduce.6.cloned.1.call-done = (f32[768,2048]{1,0:T(8,128)}, f32[512,2048]{1,0:T(8,128)}, f32[512,2048]{1,0:T(8,128)}, f32[512,2048]{1,0:T(8,128)}, f32[512,...) async-done(((f32[768,2048]{1,0:T(8,128)}, f32[512,2048]{1,0:T(8,128)}, f32[512,2048]{1,0:T(8,128)}, f32[512,2048]{1,0:T(8,128)}, f32[512,512]{1,0:T(8,128)}, ...) | async-done | bytes 21094416 | tf_op jit(solution)/shard_map/psum | solution.py:411
  6328.6 4.9 copy.309
  6334.5 3.2 copy.311
  (9995 shorter events, 5432.5 us)
Async XLA Ops:
  7.2 15.0 copy-start
  7.2 14.2 copy-start.44
  7.2 4971.7 %reduce-scatter.7.cloned.1.call-start = ((), (), s32[]{:S(2)}) async-start(), calls=%async_computation.3 | async-start | bytes 589824
  11.2 11.0 copy-start.43
  25.6 681.6 %copy-start.45 = (bf16[512]{0:T(512)(128)(2,1)S(1)}, bf16[512]{0:T(512)(128)(2,1)}, u32[]{:S(2)}) copy-start(bf16[512]{0:T(512)(128)(2,1)} %param.42) | copy-start | bytes 3076
  25.6 682.2 %copy-start.46 = (s32[1,1,72]{2,1,0:T(1,128)S(1)}, s32[1,1,72]{2,1,0:T(1,128)}, u32[]{:S(2)}) copy-start(s32[1,1,72]{2,1,0:T(1,128)} %param.29) | copy-start | bytes 868
  700.3 13.0 copy-start.7
  700.3 13.0 copy-start.15
  3150.1 9.9 copy-start.40
  3426.3 9.9 copy-start.40
  3677.6 9.9 copy-start.40
  3753.2 9.9 copy-start.40
  3778.4 9.9 copy-start.40
  3903.8 9.9 copy-start.40
  3954.2 9.9 copy-start.40
  4079.6 9.9 copy-start.40
  4431.0 9.9 copy-start.40
  4456.2 9.9 copy-start.40
  4732.7 9.9 copy-start.40
  4968.9 902.8 %reduce-scatter.5.cloned.1.call-start = ((), (), s32[]{:S(2)}) async-start(), calls=%async_computation.2 | async-start | bytes 2359296 | tf_op jit(solution)/shard_map/reduce_scatter | solution.py:404
  5007.4 13.7 copy-start.9
  5756.6 209.7 %all-reduce.8.cloned.1.call-start = ((), (), s32[]{:S(2)}) async-start(), calls=%async_computation.5 | async-start | bytes 10485760 | tf_op jit(solution)/shard_map/psum | solution.py:410
  5763.6 565.0 %all-reduce.6.cloned.1.call-start = ((), (), s32[]{:S(2)}) async-start(), calls=%async_computation.4 | async-start | bytes 42205184 | tf_op jit(solution)/shard_map/psum | solution.py:411
  5780.1 50.8 copy-start.14
  (883 other events, 4376.6 us)
Sparse Core Ops, SparseCore 0:
  4969.0 9.8 reduce-scatter.6
  5756.7 10.1 reduce-scatter.4
  5773.2 193.0 all-reduce.7
  5973.7 354.8 all-reduce.5
where the time goes:
time: 6490 us; the launch traced here: 6360 us
  other arithmetic  2150 us (33%)
  local copies, waits for them, and re-layouts  2020 us (31%)
  matrix products  1420 us (22%)
  waiting for transfers between devices  467 us (7%)
  loops' own time  204 us (3%)
  blocking collectives  90 us (1%)
    dot_general x1258, matrix products, product(): return jnp.dot(left, right, preferred_element_type=jnp.float32)  1260 us
    dynamic_update_slice x936, local copies, waits for them, and re-layouts, spell(): lax.scan(forward_step, (zeros_state, zeros_state, zeros_state, zeros_stat...  1080 us
    psum x1, waiting for transfers between devices, shards(): lax.psum((speller_grads[0], speller_grads[1], speller_grads[2], speller_g...  362 us
    dynamic_update_slice x576, other arithmetic, shards(): lax.scan(listen_step, (zeros_state, zeros_state), (jnp.swapaxes(projected...  355 us
    dynamic_update_slice x288, local copies, waits for them, and re-layouts, spell(): lax.scan(backward_step, init, (saved, target_onehot, scale_cols), reverse...  297 us
    dynamic_update_slice x576, other arithmetic, spell(): lax.scan(forward_step, (zeros_state, zeros_state, zeros_state, zeros_stat...  268 us
    another operation x347, other arithmetic  237 us
    dynamic_slice x216, local copies, waits for them, and re-layouts, spell(): lax.scan(backward_step, init, (saved, target_onehot, scale_cols), reverse...  197 us

commit v1 on v0

v1 whole, which is shorter than its diff:
```python
import functools

import jax
import jax.numpy as jnp
from jax import lax
from jax.experimental import pallas as pl
from jax.experimental.pallas import tpu as pltpu
from jax.sharding import PartitionSpec as P

F32 = jnp.float32
BF16 = jnp.bfloat16
VMEM_BYTES = 60 * 1024 * 1024
SAFE_SCORE = 80.0


def mm(left, right):
    return jnp.dot(left, right, preferred_element_type=F32)


def mm_nt(left, right):
    return lax.dot_general(left, right, (((1,), (1,)), ((), ())), preferred_element_type=F32)


def mm_tn(left, right):
    return lax.dot_general(left, right, (((0,), (0,)), ((), ())), preferred_element_type=F32)


def sigmoid(x):
    return 0.5 * jnp.tanh(0.5 * x) + 0.5


def cell_forward(preact, cell_prev):
    n = preact.shape[-1] // 4
    in_gate = sigmoid(preact[:, :n])
    forget = sigmoid(preact[:, n : 2 * n])
    candid = jnp.tanh(preact[:, 2 * n : 3 * n])
    out_gate = sigmoid(preact[:, 3 * n :])
    cell_new = forget * cell_prev + in_gate * candid
    tanh_cell = jnp.tanh(cell_new)
    hidden = out_gate * tanh_cell
    factors = (
        candid * in_gate * (1.0 - in_gate),
        cell_prev * forget * (1.0 - forget),
        in_gate * (1.0 - candid * candid),
        tanh_cell * out_gate * (1.0 - out_gate),
        out_gate * (1.0 - tanh_cell * tanh_cell),
        forget,
    )
    return cell_new, hidden, factors


def cell_backward(factors, grad_hidden, grad_cell):
    n = factors.shape[-1] // 6
    part = lambda k: factors[:, k * n : (k + 1) * n]
    total = grad_cell + grad_hidden * part(4)
    grad_preact = jnp.concatenate(
        [total * part(0), total * part(1), total * part(2), grad_hidden * part(3)], -1
    )
    return grad_preact, total * part(5)


def listen_forward_kernel(
    lengths, frames, w_in, w_rec, bias, pairs_out, factors_out, hprev_out, mine_out, other_out,
    proj, emit,
):
    role = lax.axis_index("role")
    utts, time_len, width4 = proj.shape
    units = width4 // 4
    feat = frames.shape[-1]
    rows = lax.broadcasted_iota(jnp.int32, (time_len, 2 * time_len), 0)
    cols = lax.broadcasted_iota(jnp.int32, (time_len, 2 * time_len), 1)
    for half in range(2):
        pick = jnp.where(cols == 2 * rows + half, 1.0, 0.0).astype(BF16)
        for u in range(utts):
            pairs_out[u, :, half * feat : (half + 1) * feat] = mm(pick, frames[u]).astype(BF16)
    bias_row = bias[...].astype(F32)
    for u in range(utts):
        proj[u] = mm(pairs_out[u], w_in[...]) + bias_row
    first = lax.broadcasted_iota(jnp.int32, (8, 1), 0) == 0
    row_lengths = jnp.where(first, lengths[0], lengths[1])

    def step(s, carry):
        hidden, cell = carry
        t = jnp.where(role == 1, time_len - 1 - s, s)
        at = pl.ds(t, 1)
        pre_in = jnp.where(first, proj[0, at, :], proj[1, at, :])
        low = hidden.astype(BF16)
        cell_new, hidden_new, factors = cell_forward(pre_in + mm(low, w_rec[...]), cell)
        live = t < row_lengths
        hidden_next = jnp.where(live, hidden_new, hidden)
        cell_next = jnp.where(live, cell_new, cell)
        emitted = jnp.where(live, hidden_new, 0.0)
        for u in range(2):
            for k in range(6):
                factors_out[u, at, k * units : (k + 1) * units] = factors[k][u : u + 1]
            hprev_out[u, at, :] = hidden[u : u + 1]
            emit[u, at, :] = emitted[u : u + 1]
        return hidden_next, cell_next

    zero = jnp.zeros((8, units), F32)
    lax.fori_loop(0, time_len, step, (zero, zero))
    mine_out[...] = emit[role].astype(BF16)
    other_out[...] = emit[1 - role].astype(BF16)


def listen_forward(lengths, frames, w_in, w_rec, bias):
    utts, frame_len, feat = frames.shape
    time_len = frame_len // 2
    units = w_rec.shape[0]
    vmem = pl.BlockSpec(memory_space=pltpu.VMEM)
    shape = jax.ShapeDtypeStruct
    return pl.pallas_call(
        listen_forward_kernel,
        out_shape=(
            shape((utts, time_len, 2 * feat), BF16),
            shape((utts, time_len, 6 * units), F32),
            shape((utts, time_len, units), F32),
            shape((time_len, units), BF16),
            shape((time_len, units), BF16),
        ),
        in_specs=[pl.BlockSpec(memory_space=pltpu.SMEM)] + [vmem] * 4,
        out_specs=(vmem,) * 5,
        scratch_shapes=[
            pltpu.VMEM((utts, time_len, 4 * units), F32),
            pltpu.VMEM((utts, time_len, units), F32),
        ],
        compiler_params=pltpu.CompilerParams(vmem_limit_bytes=VMEM_BYTES),
    )(lengths, frames, w_in, w_rec, bias)


def listen_backward_kernel(
    lengths, pairs, factors, hprev, grad_mine, grad_other, w_in, w_rec,
    grad_in, grad_rec, grad_bias, grad_pairs, grad_pre, grad_out,
):
    role = lax.axis_index("role")
    utts, time_len, width4 = grad_pre.shape
    units = width4 // 4
    grad_out[role] = grad_mine[...].astype(F32)
    grad_out[1 - role] = grad_other[...].astype(F32)
    first = lax.broadcasted_iota(jnp.int32, (8, 1), 0) == 0
    row_lengths = jnp.where(first, lengths[0], lengths[1])

    def step(s, carry):
        grad_hidden, grad_cell = carry
        t = jnp.where(role == 1, s, time_len - 1 - s)
        at = pl.ds(t, 1)
        live = t < row_lengths
        fact = jnp.where(first, factors[0, at, :], factors[1, at, :])
        arrived = jnp.where(first, grad_out[0, at, :], grad_out[1, at, :])
        fact = jnp.where(live, fact, 0.0)
        total = grad_hidden + jnp.where(live, arrived, 0.0)
        pre, cell_back = cell_backward(fact, total, grad_cell)
        pre_low = pre.astype(BF16)
        for u in range(2):
            grad_pre[u, at, :] = pre[u : u + 1]
        back = mm_nt(pre_low, w_rec[...])
        return jnp.where(live, back, total), jnp.where(live, cell_back, grad_cell)

    zero = jnp.zeros((8, units), F32)
    lax.fori_loop(0, time_len, step, (zero, zero))
    in_sum = None
    for u in range(utts):
        low = grad_pre[u].astype(BF16)
        grad_pairs[u] = mm_nt(low, w_in[...])
        bias_part = jnp.sum(low.astype(F32), 0, keepdims=True)
        if u == 0:
            grad_in[...] = mm_tn(pairs[u], low)
            grad_rec[...] = mm_tn(hprev[u].astype(BF16), low)
            grad_bias[...] = bias_part
        else:
            grad_in[...] += mm_tn(pairs[u], low)
            grad_rec[...] += mm_tn(hprev[u].astype(BF16), low)
            grad_bias[...] += bias_part


def listen_backward(lengths, pairs, factors, hprev, grad_mine, grad_other, w_in, w_rec):
    utts, time_len, width = pairs.shape
    units = w_rec.shape[0]
    vmem = pl.BlockSpec(memory_space=pltpu.VMEM)
    shape = jax.ShapeDtypeStruct
    return pl.pallas_call(
        listen_backward_kernel,
        out_shape=(
            shape((width, 4 * units), F32),
            shape((units, 4 * units), F32),
            shape((1, 4 * units), F32),
            shape((utts, time_len, width), F32),
        ),
        in_specs=[pl.BlockSpec(memory_space=pltpu.SMEM)] + [vmem] * 7,
        out_specs=(vmem,) * 4,
        scratch_shapes=[
            pltpu.VMEM((utts, time_len, 4 * units), F32),
            pltpu.VMEM((utts, time_len, units), F32),
        ],
        compiler_params=pltpu.CompilerParams(vmem_limit_bytes=VMEM_BYTES),
    )(lengths, pairs, factors, hprev, grad_mine, grad_other, w_in, w_rec)


def shift_down(rows):
    rolled = pltpu.roll(rows, 1, 0)
    at = lax.broadcasted_iota(jnp.int32, rows.shape, 0)
    return jnp.where(at == 0, 0.0, rolled)


def shift_up(rows):
    count = rows.shape[0]
    rolled = pltpu.roll(rows, count - 1, 0)
    at = lax.broadcasted_iota(jnp.int32, rows.shape, 0)
    return jnp.where(at == count - 1, 0.0, rolled)


def speller_kernel(
    lengths, text_lens,
    mine, other, prev_onehot, target_onehot,
    w_lin, w_lhid, b_low, w_uin, w_uhid, b_up, w_key, w_query, vec, w_out, b_out, table,
    loss, grad_mine, grad_other,
    g_lin, g_lhid, g_lbias, g_uin, g_uhid, g_ubias, g_key, g_query, g_vec, g_out, g_obias, g_table,
    key, keys_proj, key_low, key_low_t, emb_proj,
    fact1, fact2, s1_rows, s2_rows, q_rows, w_rows, feat_rows, dw_rows,
    dp1_rows, dp2_rows, dq_rows, m_scr, keys_acc, vec_acc,
):
    role = lax.axis_index("role")
    time_len, units = mine.shape
    steps = emb_proj.shape[0]
    cells = w_lhid.shape[0]
    embed = table.shape[1]
    pad_time = key.shape[0]
    length = lengths[role]
    text_len = text_lens[0, 0]

    key[time_len:, :] = jnp.zeros((pad_time - time_len, 2 * units), BF16)
    key[:time_len, :units] = jnp.where(role == 0, mine[...], other[...])
    key[:time_len, units:] = jnp.where(role == 0, other[...], mine[...])
    keys_proj[...] = mm(key[:time_len, :], w_key[...])
    key_low_f32 = mm(key[...], w_lin[embed:, :])
    key_low[...] = key_low_f32.astype(BF16)
    key_low_t[...] = jnp.transpose(key_low_f32).astype(BF16)
    emb = mm(prev_onehot[...], table[...]).astype(BF16)
    emb_proj[...] = mm(emb, w_lin[:embed, :]) + b_low[...].astype(F32)
    bias_up = b_up[...].astype(F32)
    vec_row = vec[...].astype(F32)
    lane = lax.broadcasted_iota(jnp.int32, (1, pad_time), 1)
    frame_ok = lane < length
    ones = jnp.ones((1, 256), BF16)
    tail = jnp.zeros((pad_time - time_len, 256), BF16)

    def forward_step(shift_by_max, i, carry):
        cell1, cell2, hid1, hid2, expw, rinv = carry
        at = pl.ds(i, 1)
        pre1 = emb_proj[at, :] + hid1 + mm(expw, key_low[...]) * rinv
        cell1, s1, factors = cell_forward(pre1, cell1)
        for k in range(6):
            fact1[at, k * cells : (k + 1) * cells] = factors[k]
        s1_rows[at, :] = s1
        s1_low = s1.astype(BF16)
        pre2 = hid2 + bias_up + mm(s1_low, w_uin[...])
        hid1 = mm(s1_low, w_lhid[...])
        cell2, s2, factors = cell_forward(pre2, cell2)
        for k in range(6):
            fact2[at, k * cells : (k + 1) * cells] = factors[k]
        s2_rows[at, :] = s2
        s2_low = s2.astype(BF16)
        query = mm(s2_low, w_query[...])
        hid2 = mm(s2_low, w_uhid[...])
        q_rows[at, :] = query
        part = None
        for j in range(query.shape[1] // 128):
            cut = slice(j * 128, (j + 1) * 128)
            term = jnp.tanh(keys_proj[:, cut] + query[:, cut]) * vec_row[:, cut]
            part = term if part is None else part + term
        high = part.astype(BF16)
        low = (part - high.astype(F32)).astype(BF16)
        split = jnp.concatenate([jnp.concatenate([high, low], 1), tail], 0)
        scores = mm_nt(ones, split)
        if shift_by_max:
            scores = jnp.where(frame_ok, scores, -1000000000.0)
            scores = scores - jnp.max(scores, -1, keepdims=True)
        expf = jnp.where(frame_ok, jnp.exp(scores), 0.0)
        rinv = 1.0 / jnp.sum(expf, -1, keepdims=True)
        w_rows[at, :] = expf * rinv
        return cell1, cell2, hid1, hid2, expf.astype(BF16), rinv

    zero = jnp.zeros((1, cells), F32)
    wide = jnp.zeros((1, 4 * cells), F32)
    start = (zero, zero, wide, wide, jnp.zeros((1, pad_time), BF16), jnp.ones((1, 1), F32))
    bound = jnp.sum(jnp.abs(vec_row))

    @pl.when(bound <= SAFE_SCORE)
    def _():
        lax.fori_loop(0, steps, functools.partial(forward_step, False), start)

    @pl.when(bound > SAFE_SCORE)
    def _():
        lax.fori_loop(0, steps, functools.partial(forward_step, True), start)

    w_low = w_rows[...].astype(BF16)
    ctx = mm(w_low, key[...]).astype(BF16)
    s2_low = s2_rows[...].astype(BF16)
    logits = mm(s2_low, w_out[:cells, :]) + mm(ctx, w_out[cells:, :]) + b_out[...].astype(F32)
    top = jnp.max(logits, -1, keepdims=True)
    log_total = top + jnp.log(jnp.sum(jnp.exp(logits - top), -1, keepdims=True))
    target = target_onehot[...]
    cross = log_total - jnp.sum(logits * target, -1, keepdims=True)
    text = text_len.astype(F32)
    alive = lax.broadcasted_iota(jnp.int32, (steps, 1), 0) < text_len
    loss[...] = jnp.sum(jnp.where(alive, cross, 0.0), 0, keepdims=True) / text
    scale = jnp.where(alive, 1.0 / text, 0.0)
    logit_grad = (scale * (jnp.exp(logits - log_total) - target)).astype(BF16)
    feat_rows[...] = mm_nt(logit_grad, w_out[...])
    dw_rows[...] = mm_nt(feat_rows[:, cells:].astype(BF16), key[...])
    keys_acc[...] = jnp.zeros_like(keys_acc)
    vec_acc[...] = jnp.zeros_like(vec_acc)
    m_scr[time_len:, :] = jnp.zeros((pad_time - time_len, m_scr.shape[1]), BF16)

    def backward_step(s, carry):
        dp1, back1, back2, dcell1, dcell2 = carry
        i = steps - 1 - s
        at = pl.ds(i, 1)
        query = q_rows[at, :]
        weights = w_rows[at, :]
        dweights = dw_rows[at, :] + mm(dp1, key_low_t[...])
        dscore = weights * (dweights - jnp.sum(weights * dweights, -1, keepdims=True))
        dcol = jnp.transpose(jnp.broadcast_to(dscore, (8, pad_time)))[:time_len, :1]
        for j in range(query.shape[1] // 128):
            cut = slice(j * 128, (j + 1) * 128)
            energy = jnp.tanh(keys_proj[:, cut] + query[:, cut])
            slope = 1.0 - energy * energy
            m_scr[:time_len, cut] = slope.astype(BF16)
            keys_acc[:, cut] += dcol * slope
            vec_acc[:, cut] += jnp.sum((dcol * energy).reshape(time_len // 8, 8, 128), 0)
        dquery = (mm(dscore.astype(BF16), m_scr[...]) * vec_row).astype(BF16)
        dq_rows[at, :] = dquery.astype(F32)
        ds2 = back2 + feat_rows[at, :cells] + mm_nt(dquery, w_query[...])
        pre2, dcell2 = cell_backward(fact2[at, :], ds2, dcell2)
        dp2_rows[at, :] = pre2
        dp2 = pre2.astype(BF16)
        ds1 = back1 + mm_nt(dp2, w_uin[...])
        back2 = mm_nt(dp2, w_uhid[...])
        pre1, dcell1 = cell_backward(fact1[at, :], ds1, dcell1)
        dp1_rows[at, :] = pre1
        dp1 = pre1.astype(BF16)
        back1 = mm_nt(dp1, w_lhid[...])
        return dp1, back1, back2, dcell1, dcell2

    lax.fori_loop(0, steps, backward_step, (wide.astype(BF16), zero, zero, zero, zero))

    dp1 = dp1_rows[...].astype(BF16)
    dp2 = dp2_rows[...].astype(BF16)
    dq = dq_rows[...].astype(BF16)
    s1 = s1_rows[...].astype(BF16)
    next_dp1 = shift_up(dp1.astype(F32)).astype(BF16)
    ctx_grad = (feat_rows[:, cells:] + mm_nt(next_dp1, w_lin[embed:, :])).astype(BF16)
    keys_grad = (keys_acc[...] * vec_row).astype(BF16)
    key_grad = mm_nt(keys_grad, w_key[...]) + mm_tn(w_low, ctx_grad)[:time_len, :]
    key_grad = key_grad.astype(BF16)
    grad_mine[...] = jnp.where(role == 0, key_grad[:, :units], key_grad[:, units:])
    grad_other[...] = jnp.where(role == 0, key_grad[:, units:], key_grad[:, :units])
    g_lin[:embed, :] = mm_tn(emb, dp1)
    g_lin[embed:, :] = mm_tn(shift_down(ctx.astype(F32)).astype(BF16), dp1)
    g_lhid[...] = mm_tn(shift_down(s1.astype(F32)).astype(BF16), dp1)
    g_lbias[...] = jnp.sum(dp1.astype(F32), 0, keepdims=True)
    g_uin[...] = mm_tn(s1, dp2)
    g_uhid[...] = mm_tn(shift_down(s2_low.astype(F32)).astype(BF16), dp2)
    g_ubias[...] = jnp.sum(dp2.astype(F32), 0, keepdims=True)
    g_key[...] = mm_tn(key[:time_len, :], keys_grad)
    g_query[...] = mm_tn(s2_low, dq)
    g_vec[...] = jnp.sum(vec_acc[...], 0, keepdims=True)
    g_out[:cells, :] = mm_tn(s2_low, logit_grad)
    g_out[cells:, :] = mm_tn(ctx, logit_grad)
    g_obias[...] = jnp.sum(logit_grad.astype(F32), 0, keepdims=True)
    emb_grad = mm_nt(dp1, w_lin[:embed, :])
    hot = prev_onehot[...]
    total = None
    for _ in range(3):
        low = emb_grad.astype(BF16)
        emb_grad = emb_grad - low.astype(F32)
        total = mm_tn(hot, low) if total is None else total + mm_tn(hot, low)
    g_table[...] = total


def speller(
    lengths, text_lens, mine, other, prev_onehot, target_onehot,
    w_lin, w_lhid, b_low, w_uin, w_uhid, b_up, w_key, w_query, vec, w_out, b_out, table,
):
    time_len, units = mine.shape
    steps, vocab = prev_onehot.shape
    cells = w_lhid.shape[0]
    att = w_key.shape[1]
    embed = table.shape[1]
    pad_time = -(-time_len // 256) * 256
    vmem = pl.BlockSpec(memory_space=pltpu.VMEM)
    smem = pl.BlockSpec(memory_space=pltpu.SMEM)
    shape = jax.ShapeDtypeStruct
    outs = (
        shape((1, 1), F32),
        shape((time_len, units), BF16),
        shape((time_len, units), BF16),
        shape(w_lin.shape, F32),
        shape(w_lhid.shape, F32),
        shape(b_low.shape, F32),
        shape(w_uin.shape, F32),
        shape(w_uhid.shape, F32),
        shape(b_up.shape, F32),
        shape(w_key.shape, F32),
        shape(w_query.shape, F32),
        shape(vec.shape, F32),
        shape(w_out.shape, F32),
        shape(b_out.shape, F32),
        shape(table.shape, F32),
    )
    return pl.pallas_call(
        speller_kernel,
        out_shape=outs,
        in_specs=[smem] * 2 + [vmem] * 16,
        out_specs=(vmem,) * len(outs),
        scratch_shapes=[
            pltpu.VMEM((pad_time, 2 * units), BF16),
            pltpu.VMEM((time_len, att), F32),
            pltpu.VMEM((pad_time, 4 * cells), BF16),
            pltpu.VMEM((4 * cells, pad_time), BF16),
            pltpu.VMEM((steps, 4 * cells), F32),
            pltpu.VMEM((steps, 6 * cells), F32),
            pltpu.VMEM((steps, 6 * cells), F32),
            pltpu.VMEM((steps, cells), F32),
            pltpu.VMEM((steps, cells), F32),
            pltpu.VMEM((steps, att), F32),
            pltpu.VMEM((steps, pad_time), F32),
            pltpu.VMEM((steps, w_out.shape[0]), F32),
            pltpu.VMEM((steps, pad_time), F32),
            pltpu.VMEM((steps, 4 * cells), F32),
            pltpu.VMEM((steps, 4 * cells), F32),
            pltpu.VMEM((steps, att), F32),
            pltpu.VMEM((pad_time, att), BF16),
            pltpu.VMEM((time_len, att), F32),
            pltpu.VMEM((8, att), F32),
        ],
        compiler_params=pltpu.CompilerParams(vmem_limit_bytes=VMEM_BYTES),
    )(
        lengths, text_lens, mine, other, prev_onehot, target_onehot,
        w_lin, w_lhid, b_low, w_uin, w_uhid, b_up, w_key, w_query, vec, w_out, b_out, table,
    )


def shards(
    frames,
    step_lengths,
    characters,
    char_lengths,
    listen_input,
    listen_hidden,
    listen_bias,
    lower_input,
    lower_hidden,
    lower_bias,
    upper_input,
    upper_hidden,
    upper_bias,
    key_proj,
    query_proj,
    score_vector,
    output_proj,
    output_bias,
    char_table,
):
    utts, frame_len, feat = frames.shape
    time_len = frame_len // 2
    swap = [(0, 1), (1, 0)]
    w_in, w_rec = listen_input[0], listen_hidden[0]
    pairs, factors, hprev, mine, other = listen_forward(
        step_lengths, frames, w_in, w_rec, listen_bias
    )
    other = lax.ppermute(other, "role", swap)
    chars = characters[0, 0]
    vocab = char_table.shape[0]
    previous = jnp.concatenate([jnp.zeros((1,), jnp.int32), chars[:-1]])
    ids = jnp.arange(vocab)[None, :]
    prev_onehot = (previous[:, None] == ids).astype(BF16)
    target_onehot = (chars[:, None] == ids).astype(F32)
    loss, grad_mine, grad_other, *grads = speller(
        step_lengths, char_lengths, mine, other, prev_onehot, target_onehot,
        lower_input, lower_hidden, lower_bias[None], upper_input, upper_hidden, upper_bias[None],
        key_proj, query_proj, score_vector[None], output_proj, output_bias[None], char_table,
    )
    grad_other = lax.ppermute(grad_other, "role", swap)
    grad_in, grad_rec, grad_bias, grad_pairs = listen_backward(
        step_lengths, pairs, factors, hprev, grad_mine, grad_other, w_in, w_rec
    )
    frame_grad = lax.psum_scatter(
        grad_pairs.reshape(utts, frame_len, feat), "role", scatter_dimension=1, tiled=True
    )
    summed = lax.psum(tuple(grads), ("role", "dp"))
    sum_in, sum_rec, sum_bias = lax.psum((grad_in, grad_rec, grad_bias), "dp")
    flat = {2: lower_bias, 5: upper_bias, 8: score_vector, 10: output_bias}
    summed = [item.reshape(flat[k].shape) if k in flat else item for k, item in enumerate(summed)]
    return (loss, frame_grad, sum_in[None], sum_rec[None], sum_bias, *summed)


def solution(mesh):
    whole = P()
    return jax.shard_map(
        shards,
        mesh=mesh,
        in_specs=(
            P("dp", None, None),
            P("dp"),
            P("dp", "role", None),
            P("dp", "role"),
            P("role", None, None),
            P("role", None, None),
            P("role", None),
        )
        + (whole,) * 12,
        out_specs=(
            P("dp", "role"),
            P("dp", "role", None),
            P("role", None, None),
            P("role", None, None),
            P("role", None),
        )
        + (whole,) * 12,
        check_vma=False,
    )
```

time: 6490 us -> 952 us (0.15)
  the two profiles are of different devices: /device:TPU:0 before, /device:TPU:9 now
where the time goes in v1:
time: 952 us; the launch traced here: 948 us
  waiting for transfers between devices  424 us (45%)
  Pallas kernels  400 us (42%)
  blocking collectives  70.9 us (7%)
  local copies, waits for them, and re-layouts  34.5 us (4%)
  between operations  16.3 us (2%)
    pallas_call x1, Pallas kernels, speller(): pl.pallas_call(speller_kernel, out_shape=outs, in_specs=[smem] * 2 + [vme...  298 us
    psum x1, waiting for transfers between devices, shards(): summed = lax.psum(tuple(grads), ('role', 'dp'))  227 us
    psum x1, waiting for transfers between devices, shards(): sum_in, sum_rec, sum_bias = lax.psum((grad_in, grad_rec, grad_bias), 'dp')  195 us
    pallas_call x1, Pallas kernels, listen_backward(): pl.pallas_call(listen_backward_kernel, out_shape=(shape((width, 4 * units...  56.8 us
    pallas_call x1, Pallas kernels, listen_forward(): pl.pallas_call(listen_forward_kernel, out_shape=(shape((utts, time_len, 2...  44.6 us
    psum x1, blocking collectives, shards(): summed = lax.psum(tuple(grads), ('role', 'dp'))  42.5 us
    psum x1, blocking collectives, shards(): sum_in, sum_rec, sum_bias = lax.psum((grad_in, grad_rec, grad_bias), 'dp')  28.4 us
    unnamed x42, local copies, waits for them, and re-layouts  27.4 us
  transfers between devices with their start and end apart: 5, of which 3 were waited for; matrix products, arithmetic and copies ran while one was open for 1% of the time, Pallas kernels for 6%

profile of v1, /device:TPU:9, one launch (start us, length us, event | category | flops | bytes accessed | tf_op | source)
XLA Modules:
  0.0 948.1 jit_solution(15262309333153113541)
XLA Ops:
  8.1 44.6 %shard_map.314 = (bf16[2,192,1024]{2,1,0:T(8,128)(2,1)}, f32[2,192,1536]{2,1,0:T(8,128)}, f32[2,192,256]{2,1,0:T(8,128)}, bf16[192,256]{1,0:T(8,128)(2,1)}, bf16[192,256]{1,0:T(8,128)(2,1)}) custom-call(s32[2]{0:T(128)} %lengths.5, bf16[2,384,512]{2,1,0:T(8,128)(2,1)} %frames.1, bf16[1024,1024]{1,0:T(8,128)(2,1)} %bitcast.12, bf16[256,1024]{1,0:T(8,128)(2,1)} %bitcast.15, ...), custom_call_target="tpu_custom_call" | custom-call | tf_op jit(solution)/shard_map/pallas_call | solution.py:112
  54.1 1.4 fusion
  56.1 1.3 broadcast_in_dim.22.vec
  57.4 1.3 broadcast_in_dim.20.b_low
  58.7 1.3 broadcast_in_dim.21.b_up
  59.9 1.7 copy.36.w_out
  62.3 298.2 %shard_map.315 = (f32[1,1]{1,0:T(1,128)}, bf16[192,256]{1,0:T(8,128)(2,1)}, bf16[192,256]{1,0:T(8,128)(2,1)}, f32[768,2048]{1,0:T(8,128)}, f32[512,2048]{1,0:T(8...) custom-call(s32[2]{0:T(128)} %lengths.5, ...), custom_call_target="tpu_custom_call" | custom-call | tf_op jit(solution)/shard_map/pallas_call | solution.py:411
  361.4 1.3 collective-permute-done.1.grad_other
  363.3 56.8 %shard_map.316 = (f32[1024,1024]{1,0:T(8,128)}, f32[256,1024]{1,0:T(8,128)}, f32[1,1024]{1,0:T(1,128)}, f32[2,192,1024]{2,1,0:T(8,128)}) custom-call(s32[2]{0:T(128)} %lengths.5, bf16[2,192,1024]{2,1,0:T(8,128)(2,1)} %get-tuple-element.44.pairs, f32[2,192,1536]{2,1,0:T(8,128)} %get-tuple-element.45.factors, f32[2,192,256]{2,1,0:T(8,128)} %get-tuple-element.46.hprev, ...), custom_call_target="tpu_custom_call" | custom-call | tf_op jit(solution)/shard_map/pallas_call | solution.py:181
  420.2 2.6 reshape.52
  423.6 42.5 %all-reduce = (f32[2048]{0:T(1024)}, f32[2048]{0:T(1024)}, f32[512]{0:T(512)}, f32[30]{0:T(128)}, f32[30,256]{1,0:T(8,128)}) all-reduce(f32[2048]{0:T(1024)S(1)} %bitcast.18, f32[2048]{0:T(1024)S(1)} %bitcast.19, f32[512]{0:T(512)S(1)} %bitcast.20, f32[30]{0:T(128)S(1)} %bitcast.23, ...), channel_id=1, replica_groups=mesh['role'=2,'dp'=16] {'role','dp'}, use_global_device_ids=true, to_apply=%region_6.0 | all-reduce | flops 12318 | bytes 98544 | tf_op jit(solution)/shard_map/psum | solution.py:491
  466.1 28.4 %psum.107 = f32[1,1024]{1,0:T(1,128)} all-reduce(f32[1,1024]{1,0:T(1,128)S(1)} %copy-done.12), channel_id=1, replica_groups=mesh['role'=2,'dp'=16] {'dp'}, use_global_device_ids=true, to_apply=%region_3.0 | all-reduce | flops 1024 | bytes 8192 | tf_op jit(solution)/shard_map/psum | solution.py:492
  494.5 227.2 %all-reduce.6.cloned.1.call-done = (f32[768,2048]{1,0:T(8,128)}, f32[512,2048]{1,0:T(8,128)}, f32[512,2048]{1,0:T(8,128)}, f32[512,2048]{1,0:T(8,128)}, f32[512,...) async-done(((f32[768,2048]{1,0:T(8,128)}, f32[512,2048]{1,0:T(8,128)}, f32[512,2048]{1,0:T(8,128)}, f32[512,2048]{1,0:T(8,128)}, f32[512,512]{1,0:T(8,128)}, ...) | async-done | bytes 21094416 | tf_op jit(solution)/shard_map/psum | solution.py:491
  721.7 1.9 copy.37
  723.5 195.2 %all-reduce.8.cloned.1.call-done = (f32[1,1024,1024]{2,1,0:T(8,128)}, f32[1,256,1024]{2,1,0:T(8,128)}) async-done(((f32[1,1024,1024]{2,1,0:T(8,128)}, f32[1,256,1024]{2,1,0:T(8,128)}), (f32[1,1024,1024]{2,1,0:T(8,128)}, f32[1,256,1024]{2,1,0:T(8,128)})) %all-reduce.8.cloned.1.call-update) | async-done | bytes 5242896 | tf_op jit(solution)/shard_map/psum | solution.py:492
  918.8 4.9 copy.48
  923.7 1.0 copy.49
  924.7 3.2 copy.50
  927.9 1.3 copy-done.3
  929.1 2.1 copy.51
  931.3 1.6 copy-done.2
  932.8 2.1 copy.52
  935.0 1.6 copy-done.1
  936.5 2.1 copy.53
  (43 shorter events, 6.3 us)
Async XLA Ops:
  8.0 713.6 %all-reduce.6.cloned.1.call-start = ((), (), s32[]{:S(2)}) async-start(), calls=%async_computation.2 | async-start | bytes 42991616 | tf_op jit(solution)/shard_map/psum | solution.py:491
  52.7 9.0 collective-permute-start
  61.7 0.6 copy-start.7
  360.5 0.9 copy-start.15
  360.5 363.0 %reduce-scatter.2.cloned.1.call-start = ((), (), s32[]{:S(2)}) async-start(), calls=%async_computation.1 | async-start | bytes 2359296 | tf_op jit(solution)/shard_map/reduce_scatter | solution.py:488
  361.4 1.3 collective-permute-start.1
  362.7 0.6 copy-start.8
  422.7 0.8 copy-start.9
  422.7 0.8 copy-start.10
  422.7 0.8 copy-start.11
  422.7 0.8 copy-start.13
  422.7 0.8 copy-start.14
  422.7 43.3 %copy-start.12 = (f32[1,1024]{1,0:T(1,128)S(1)}, f32[1,1024]{1,0:T(1,128)}, u32[]{:S(2)}) copy-start(f32[1,1024]{1,0:T(1,128)} %get-tuple-element.52) | copy-start | bytes 12292
  422.8 496.0 %all-reduce.8.cloned.1.call-start = ((), (), s32[]{:S(2)}) async-start(), calls=%async_computation.3 | async-start | bytes 10485760 | tf_op jit(solution)/shard_map/psum | solution.py:492
  918.8 4.9 copy-start.6
  918.8 5.9 copy-start
  924.7 4.5 copy-start.3
  929.1 3.7 copy-start.2
  932.8 3.7 copy-start.1
  936.5 2.1 copy-start.5
  936.5 3.1 copy-start.4
Sparse Core Ops, SparseCore 0:
  360.6 360.9 all-reduce.5
  728.8 189.8 all-reduce.7
Sparse Core Ops, SparseCore 1:
  422.9 10.3 reduce-scatter.1

commit v2 on v1

v2 whole, which is shorter than its diff:
```python
import functools

import jax
import jax.numpy as jnp
from jax import lax
from jax.experimental import pallas as pl
from jax.experimental.pallas import tpu as pltpu
from jax.sharding import PartitionSpec as P

F32 = jnp.float32
BF16 = jnp.bfloat16
VMEM_BYTES = 60 * 1024 * 1024
SAFE_SCORE = 80.0


def mm(left, right):
    return jnp.dot(left, right, preferred_element_type=F32)


def mm_nt(left, right):
    return lax.dot_general(left, right, (((1,), (1,)), ((), ())), preferred_element_type=F32)


def mm_tn(left, right):
    return lax.dot_general(left, right, (((0,), (0,)), ((), ())), preferred_element_type=F32)


def sigmoid(x):
    return 0.5 * jnp.tanh(0.5 * x) + 0.5


def cell_forward(preact, cell_prev):
    n = preact.shape[-1] // 4
    in_gate = sigmoid(preact[:, :n])
    forget = sigmoid(preact[:, n : 2 * n])
    candid = jnp.tanh(preact[:, 2 * n : 3 * n])
    out_gate = sigmoid(preact[:, 3 * n :])
    cell_new = forget * cell_prev + in_gate * candid
    tanh_cell = jnp.tanh(cell_new)
    hidden = out_gate * tanh_cell
    factors = (
        candid * in_gate * (1.0 - in_gate),
        cell_prev * forget * (1.0 - forget),
        in_gate * (1.0 - candid * candid),
        tanh_cell * out_gate * (1.0 - out_gate),
        out_gate * (1.0 - tanh_cell * tanh_cell),
        forget,
    )
    return cell_new, hidden, factors


def cell_backward(factors, grad_hidden, grad_cell):
    n = factors.shape[-1] // 6
    part = lambda k: factors[:, k * n : (k + 1) * n]
    total = grad_cell + grad_hidden * part(4)
    grad_preact = jnp.concatenate(
        [total * part(0), total * part(1), total * part(2), grad_hidden * part(3)], -1
    )
    return grad_preact, total * part(5)


def listen_forward_kernel(
    lengths, pairs, w_in, w_rec, bias, rows_out, factors_out, mine_out, other_out,
    proj, emit, hprev,
):
    role = lax.axis_index("role")
    utts, time_len, width4 = proj.shape
    units = width4 // 4
    bias_row = bias[...].astype(F32)
    for u in range(utts):
        proj[u] = mm(pairs[u], w_in[...]) + bias_row
    first = lax.broadcasted_iota(jnp.int32, (8, 1), 0) == 0
    row_lengths = jnp.where(first, lengths[0], lengths[1])

    def step(s, carry):
        hidden, cell = carry
        t = jnp.where(role == 1, time_len - 1 - s, s)
        at = pl.ds(t, 1)
        pre_in = jnp.where(first, proj[0, at, :], proj[1, at, :])
        low = hidden.astype(BF16)
        cell_new, hidden_new, factors = cell_forward(pre_in + mm(low, w_rec[...]), cell)
        live = t < row_lengths
        hidden_next = jnp.where(live, hidden_new, hidden)
        cell_next = jnp.where(live, cell_new, cell)
        emitted = jnp.where(live, hidden_new, 0.0)
        for u in range(2):
            for k in range(6):
                factors_out[u, at, k * units : (k + 1) * units] = factors[k][u : u + 1]
            hprev[u, at, :] = hidden[u : u + 1]
            emit[u, at, :] = emitted[u : u + 1]
        return hidden_next, cell_next

    zero = jnp.zeros((8, units), F32)
    lax.fori_loop(0, time_len, step, (zero, zero))
    mine_out[...] = emit[role].astype(BF16)
    other_out[...] = emit[1 - role].astype(BF16)
    for u in range(utts):
        own = slice(u * time_len, (u + 1) * time_len)
        rows_out[own, :units] = hprev[u].astype(BF16)
    rows_out[:, units:] = jnp.ones((utts * time_len, rows_out.shape[1] - units), BF16)


def listen_forward(lengths, pairs, w_in, w_rec, bias):
    utts, time_len, _ = pairs.shape
    units = w_rec.shape[0]
    vmem = pl.BlockSpec(memory_space=pltpu.VMEM)
    shape = jax.ShapeDtypeStruct
    return pl.pallas_call(
        listen_forward_kernel,
        out_shape=(
            shape((utts * time_len, units + 64), BF16),
            shape((utts, time_len, 6 * units), F32),
            shape((time_len, units), BF16),
            shape((time_len, units), BF16),
        ),
        in_specs=[pl.BlockSpec(memory_space=pltpu.SMEM)] + [vmem] * 4,
        out_specs=(vmem,) * 4,
        scratch_shapes=[
            pltpu.VMEM((utts, time_len, 4 * units), F32),
            pltpu.VMEM((utts, time_len, units), F32),
            pltpu.VMEM((utts, time_len, units), F32),
        ],
        compiler_params=pltpu.CompilerParams(vmem_limit_bytes=VMEM_BYTES),
    )(lengths, pairs, w_in, w_rec, bias)


def speller_forward_kernel(
    lengths, text_lens,
    mine, other, prev_onehot, target_onehot,
    w_lin, w_lhid, b_low, w_uin, w_uhid, b_up, w_key, w_query, vec, w_out, b_out, table,
    loss, acts, key, keys_proj, key_low_t, fact1, fact2, q_rows, w_rows, feat_rows, dw_rows,
    logit_grad_out,
    key_low, emb_proj, s1_rows, s2_rows,
):
    role = lax.axis_index("role")
    time_len, units = mine.shape
    steps = emb_proj.shape[0]
    cells = w_lhid.shape[0]
    embed = table.shape[1]
    pad_time = key.shape[0]
    length = lengths[role]
    text_len = text_lens[0, 0]

    key[time_len:, :] = jnp.zeros((pad_time - time_len, 2 * units), BF16)
    key[:time_len, :units] = jnp.where(role == 0, mine[...], other[...])
    key[:time_len, units:] = jnp.where(role == 0, other[...], mine[...])
    keys_proj[...] = mm(key[:time_len, :], w_key[...])
    key_low_f32 = mm(key[...], w_lin[embed:, :])
    key_low[...] = key_low_f32.astype(BF16)
    key_low_t[...] = jnp.transpose(key_low_f32).astype(BF16)
    emb = mm(prev_onehot[...], table[...]).astype(BF16)
    emb_proj[...] = mm(emb, w_lin[:embed, :]) + b_low[...].astype(F32)
    bias_up = b_up[...].astype(F32)
    vec_row = vec[...].astype(F32)
    lane = lax.broadcasted_iota(jnp.int32, (1, pad_time), 1)
    frame_ok = lane < length
    ones = jnp.ones((1, 256), BF16)
    tail = jnp.zeros((pad_time - time_len, 256), BF16)

    def forward_step(shift_by_max, i, carry):
        cell1, cell2, hid1, hid2, expw, rinv = carry
        at = pl.ds(i, 1)
        pre1 = emb_proj[at, :] + hid1 + mm(expw, key_low[...]) * rinv
        cell1, s1, factors = cell_forward(pre1, cell1)
        for k in range(6):
            fact1[at, k * cells : (k + 1) * cells] = factors[k]
        s1_rows[at, :] = s1
        s1_low = s1.astype(BF16)
        pre2 = hid2 + bias_up + mm(s1_low, w_uin[...])
        hid1 = mm(s1_low, w_lhid[...])
        cell2, s2, factors = cell_forward(pre2, cell2)
        for k in range(6):
            fact2[at, k * cells : (k + 1) * cells] = factors[k]
        s2_rows[at, :] = s2
        s2_low = s2.astype(BF16)
        query = mm(s2_low, w_query[...])
        hid2 = mm(s2_low, w_uhid[...])
        q_rows[at, :] = query
        part = None
        for j in range(query.shape[1] // 128):
            cut = slice(j * 128, (j + 1) * 128)
            term = jnp.tanh(keys_proj[:, cut] + query[:, cut]) * vec_row[:, cut]
            part = term if part is None else part + term
        high = part.astype(BF16)
        low = (part - high.astype(F32)).astype(BF16)
        split = jnp.concatenate([jnp.concatenate([high, low], 1), tail], 0)
        scores = mm_nt(ones, split)
        if shift_by_max:
            scores = jnp.where(frame_ok, scores, -1000000000.0)
            scores = scores - jnp.max(scores, -1, keepdims=True)
        expf = jnp.where(frame_ok, jnp.exp(scores), 0.0)
        rinv = 1.0 / jnp.sum(expf, -1, keepdims=True)
        w_rows[at, :] = expf * rinv
        return cell1, cell2, hid1, hid2, expf.astype(BF16), rinv

    zero = jnp.zeros((1, cells), F32)
    wide = jnp.zeros((1, 4 * cells), F32)
    start = (zero, zero, wide, wide, jnp.zeros((1, pad_time), BF16), jnp.ones((1, 1), F32))
    bound = jnp.sum(jnp.abs(vec_row))

    @pl.when(bound <= SAFE_SCORE)
    def _():
        lax.fori_loop(0, steps, functools.partial(forward_step, False), start)

    @pl.when(bound > SAFE_SCORE)
    def _():
        lax.fori_loop(0, steps, functools.partial(forward_step, True), start)

    w_low = w_rows[...].astype(BF16)
    ctx = mm(w_low, key[...]).astype(BF16)
    s2_low = s2_rows[...].astype(BF16)
    logits = mm(s2_low, w_out[:cells, :]) + mm(ctx, w_out[cells:, :]) + b_out[...].astype(F32)
    top = jnp.max(logits, -1, keepdims=True)
    log_total = top + jnp.log(jnp.sum(jnp.exp(logits - top), -1, keepdims=True))
    target = target_onehot[...]
    cross = log_total - jnp.sum(logits * target, -1, keepdims=True)
    text = text_len.astype(F32)
    alive = lax.broadcasted_iota(jnp.int32, (steps, 1), 0) < text_len
    loss[...] = jnp.sum(jnp.where(alive, cross, 0.0), 0, keepdims=True) / text
    scale = jnp.where(alive, 1.0 / text, 0.0)
    logit_grad = (scale * (jnp.exp(logits - log_total) - target)).astype(BF16)
    logit_grad_out[...] = logit_grad
    feat_rows[...] = mm_nt(logit_grad, w_out[...])
    dw_rows[...] = mm_nt(feat_rows[:, cells:].astype(BF16), key[...])
    acts[steps:, :] = jnp.zeros((acts.shape[0] - steps, acts.shape[1]), BF16)
    acts[:steps, :embed] = emb
    acts[:steps, embed : embed + 2 * units] = ctx
    acts[:steps, embed + 2 * units : embed + 2 * units + cells] = s1_rows[...].astype(BF16)
    acts[:steps, embed + 2 * units + cells :] = s2_low


def speller_forward(
    lengths, text_lens, mine, other, prev_onehot, target_onehot,
    w_lin, w_lhid, b_low, w_uin, w_uhid, b_up, w_key, w_query, vec, w_out, b_out, table,
):
    time_len, units = mine.shape
    steps, vocab = prev_onehot.shape
    cells = w_lhid.shape[0]
    att = w_key.shape[1]
    embed = table.shape[1]
    pad_time = -(-time_len // 256) * 256
    pad_steps = -(-steps // 16) * 16
    vmem = pl.BlockSpec(memory_space=pltpu.VMEM)
    smem = pl.BlockSpec(memory_space=pltpu.SMEM)
    shape = jax.ShapeDtypeStruct
    outs = (
        shape((1, 1), F32),
        shape((pad_steps, embed + 2 * units + 2 * cells), BF16),
        shape((pad_time, 2 * units), BF16),
        shape((time_len, att), F32),
        shape((4 * cells, pad_time), BF16),
        shape((steps, 6 * cells), F32),
        shape((steps, 6 * cells), F32),
        shape((steps, att), F32),
        shape((steps, pad_time), F32),
        shape((steps, w_out.shape[0]), F32),
        shape((steps, pad_time), F32),
        shape((steps, vocab), BF16),
    )
    return pl.pallas_call(
        speller_forward_kernel,
        out_shape=outs,
        in_specs=[smem] * 2 + [vmem] * 16,
        out_specs=(vmem,) * len(outs),
        scratch_shapes=[
            pltpu.VMEM((pad_time, 4 * cells), BF16),
            pltpu.VMEM((steps, 4 * cells), F32),
            pltpu.VMEM((steps, cells), F32),
            pltpu.VMEM((steps, cells), F32),
        ],
        compiler_params=pltpu.CompilerParams(vmem_limit_bytes=VMEM_BYTES),
    )(
        lengths, text_lens, mine, other, prev_onehot, target_onehot,
        w_lin, w_lhid, b_low, w_uin, w_uhid, b_up, w_key, w_query, vec, w_out, b_out, table,
    )


SMALL = 32


def shift_up(rows):
    count = rows.shape[0]
    rolled = pltpu.roll(rows, count - 1, 0)
    at = lax.broadcasted_iota(jnp.int32, rows.shape, 0)
    return jnp.where(at == count - 1, 0.0, rolled)


def speller_backward_kernel(
    w_lin, w_lhid, w_uin, w_uhid, w_key, w_query, vec, prev_onehot,
    acts, key, keys_proj, key_low_t, fact1, fact2, q_rows, w_rows, feat_rows, dw_rows, logit_grad,
    grad_mine, grad_other, dp1_out, dp2_out, pack,
    dp1_rows, dp2_rows, dq_rows, m_scr, keys_acc, vec_acc, small,
):
    role = lax.axis_index("role")
    time_len, att = keys_proj.shape
    steps, vocab = logit_grad.shape
    pad_time = key.shape[0]
    units = key.shape[1] // 2
    cells = w_lhid.shape[0]
    embed = acts.shape[1] - 2 * units - 2 * cells
    vec_row = vec[...].astype(F32)
    zero = jnp.zeros((1, cells), F32)
    wide = jnp.zeros((1, 4 * cells), BF16)
    keys_acc[...] = jnp.zeros_like(keys_acc)
    vec_acc[...] = jnp.zeros_like(vec_acc)
    m_scr[time_len:, :] = jnp.zeros((pad_time - time_len, m_scr.shape[1]), BF16)

    def backward_step(s, carry):
        dp1, back1, back2, dcell1, dcell2 = carry
        i = steps - 1 - s
        at = pl.ds(i, 1)
        query = q_rows[at, :]
        weights = w_rows[at, :]
        dweights = dw_rows[at, :] + mm(dp1, key_low_t[...])
        dscore = weights * (dweights - jnp.sum(weights * dweights, -1, keepdims=True))
        dcol = jnp.transpose(jnp.broadcast_to(dscore, (8, pad_time)))[:time_len, :1]
        for j in range(query.shape[1] // 128):
            cut = slice(j * 128, (j + 1) * 128)
            energy = jnp.tanh(keys_proj[:, cut] + query[:, cut])
            slope = 1.0 - energy * energy
            m_scr[:time_len, cut] = slope.astype(BF16)
            keys_acc[:, cut] += dcol * slope
            vec_acc[:, cut] += jnp.sum((dcol * energy).reshape(time_len // 8, 8, 128), 0)
        dquery = (mm(dscore.astype(BF16), m_scr[...]) * vec_row).astype(BF16)
        dq_rows[at, :] = dquery.astype(F32)
        ds2 = back2 + feat_rows[at, :cells] + mm_nt(dquery, w_query[...])
        pre2, dcell2 = cell_backward(fact2[at, :], ds2, dcell2)
        dp2_rows[at, :] = pre2
        dp2 = pre2.astype(BF16)
        ds1 = back1 + mm_nt(dp2, w_uin[...])
        back2 = mm_nt(dp2, w_uhid[...])
        pre1, dcell1 = cell_backward(fact1[at, :], ds1, dcell1)
        dp1_rows[at, :] = pre1
        dp1 = pre1.astype(BF16)
        back1 = mm_nt(dp1, w_lhid[...])
        return dp1, back1, back2, dcell1, dcell2

    lax.fori_loop(0, steps, backward_step, (wide, zero, zero, zero, zero))

    dp1 = dp1_rows[...].astype(BF16)
    dp2 = dp2_rows[...].astype(BF16)
    dq = dq_rows[...].astype(BF16)
    extra = jnp.zeros((dp1_out.shape[0] - steps, 4 * cells), BF16)
    dp1_out[steps:, :] = extra
    dp2_out[steps:, :] = extra
    dp1_out[:steps, :] = dp1
    dp2_out[:steps, :] = dp2
    next_dp1 = shift_up(dp1.astype(F32)).astype(BF16)
    ctx_grad = (feat_rows[:, cells:] + mm_nt(next_dp1, w_lin[embed:, :])).astype(BF16)
    keys_grad = (keys_acc[...] * vec_row).astype(BF16)
    w_low = w_rows[...].astype(BF16)
    key_grad = mm_nt(keys_grad, w_key[...]) + mm_tn(w_low, ctx_grad)[:time_len, :]
    key_grad = key_grad.astype(BF16)
    grad_mine[...] = jnp.where(role == 0, key_grad[:, :units], key_grad[:, units:])
    grad_other[...] = jnp.where(role == 0, key_grad[:, units:], key_grad[:, :units])
    ctx = acts[:steps, embed : embed + 2 * units]
    s2 = acts[:steps, embed + 2 * units + cells :]
    wide = pack.shape[1]
    deep = 2 * units * att // wide
    g_key = mm_tn(key[:time_len, :], keys_grad)
    g_query = mm_tn(s2, dq)
    for k in range(wide // att):
        cut = slice(k * att, (k + 1) * att)
        pack[:deep, cut] = g_key[k * deep : (k + 1) * deep].astype(BF16)
        pack[deep : 2 * deep, cut] = g_query[k * deep : (k + 1) * deep].astype(BF16)
    emb_grad = mm_nt(dp1, w_lin[:embed, :])
    hot = prev_onehot[...]
    total = None
    for _ in range(3):
        low = emb_grad.astype(BF16)
        emb_grad = emb_grad - low.astype(F32)
        total = mm_tn(hot, low) if total is None else total + mm_tn(hot, low)
    small[...] = jnp.zeros_like(small)
    small[:vocab, :cells] = mm_tn(logit_grad[...], s2)
    small[:vocab, cells : cells + 2 * units] = mm_tn(logit_grad[...], ctx)
    base = cells + 2 * units
    small[:vocab, base : base + embed] = total
    base += embed
    small[0:1, base : base + att] = jnp.sum(vec_acc[...], 0, keepdims=True)
    small[1:2, base : base + vocab] = jnp.sum(logit_grad[...].astype(F32), 0, keepdims=True)
    low_bias = jnp.sum(dp1.astype(F32), 0, keepdims=True)
    up_bias = jnp.sum(dp2.astype(F32), 0, keepdims=True)
    for k in range(4):
        small[2 + k : 3 + k, base : base + cells] = low_bias[:, k * cells : (k + 1) * cells]
        small[6 + k : 7 + k, base : base + cells] = up_bias[:, k * cells : (k + 1) * cells]
    high = small[...].astype(BF16)
    rows = small.shape[0]
    pack[2 * deep : 2 * deep + rows, :] = high
    pack[2 * deep + rows :, :] = (small[...] - high.astype(F32)).astype(BF16)


def speller_backward(
    w_lin, w_lhid, w_uin, w_uhid, w_key, w_query, vec, prev_onehot,
    acts, key, keys_proj, key_low_t, fact1, fact2, q_rows, w_rows, feat_rows, dw_rows, logit_grad,
):
    time_len, att = keys_proj.shape
    steps, vocab = logit_grad.shape
    pad_time = key.shape[0]
    units = key.shape[1] // 2
    cells = w_lhid.shape[0]
    pad_steps = acts.shape[0]
    vmem = pl.BlockSpec(memory_space=pltpu.VMEM)
    shape = jax.ShapeDtypeStruct
    outs = (
        shape((time_len, units), BF16),
        shape((time_len, units), BF16),
        shape((pad_steps, 4 * cells), BF16),
        shape((pad_steps, 4 * cells), BF16),
        shape(((2 * units + cells) * att // (4 * cells) + 2 * SMALL, 4 * cells), BF16),
    )
    return pl.pallas_call(
        speller_backward_kernel,
        out_shape=outs,
        in_specs=[vmem] * 19,
        out_specs=(vmem,) * len(outs),
        scratch_shapes=[
            pltpu.VMEM((steps, 4 * cells), F32),
            pltpu.VMEM((steps, 4 * cells), F32),
            pltpu.VMEM((steps, att), F32),
            pltpu.VMEM((pad_time, att), BF16),
            pltpu.VMEM((time_len, att), F32),
            pltpu.VMEM((8, att), F32),
            pltpu.VMEM((SMALL, 4 * cells), F32),
        ],
        compiler_params=pltpu.CompilerParams(vmem_limit_bytes=VMEM_BYTES),
    )(
        w_lin, w_lhid, w_uin, w_uhid, w_key, w_query, vec, prev_onehot,
        acts, key, keys_proj, key_low_t, fact1, fact2, q_rows, w_rows, feat_rows, dw_rows, logit_grad,
    )


def unpack(pack, units, cells, att, vocab, embed):
    wide = pack.shape[1]
    deep = 2 * units * att // wide
    unfold = lambda part: part.reshape(deep, wide // att, att).swapaxes(0, 1).reshape(-1, att)
    g_key = unfold(pack[:deep].astype(F32))
    g_query = unfold(pack[deep : 2 * deep].astype(F32))
    small = pack[2 * deep : 2 * deep + SMALL].astype(F32) + pack[2 * deep + SMALL :].astype(F32)
    base = cells + 2 * units
    g_out = small[:vocab, :base].T
    g_table = small[:vocab, base : base + embed]
    base += embed
    low_bias = small[2:6, base : base + cells].reshape(-1)
    up_bias = small[6:10, base : base + cells].reshape(-1)
    g_vec = small[0, base : base + att]
    g_obias = small[1, base : base + vocab]
    return low_bias, up_bias, g_key, g_query, g_vec, g_out, g_obias, g_table


def backward_steps(role, lengths, factors, grad_out, w_rec, grad_pre, first_step, count, carry):
    time_len = factors.shape[1]
    first = lax.broadcasted_iota(jnp.int32, (8, 1), 0) == 0
    row_lengths = jnp.where(first, lengths[0], lengths[1])

    def step(s, carry):
        grad_hidden, grad_cell = carry
        t = jnp.where(role == 1, s, time_len - 1 - s)
        at = pl.ds(t, 1)
        live = t < row_lengths
        fact = jnp.where(first, factors[0, at, :], factors[1, at, :])
        arrived = jnp.where(first, grad_out[0, at, :], grad_out[1, at, :])
        fact = jnp.where(live, fact, 0.0)
        total = grad_hidden + jnp.where(live, arrived, 0.0)
        pre, cell_back = cell_backward(fact, total, grad_cell)
        for u in range(2):
            grad_pre[u, at, :] = pre[u : u + 1]
        back = mm_nt(pre.astype(BF16), w_rec[...])
        return jnp.where(live, back, total), jnp.where(live, cell_back, grad_cell)

    return lax.fori_loop(first_step, first_step + count, step, carry)


def listen_backward_kernel(
    lengths, factors, grad_mine, grad_other, w_rec, pre_out, grad_pre, grad_out
):
    role = lax.axis_index("role")
    grad_out[role] = grad_mine[...].astype(F32)
    grad_out[1 - role] = grad_other[...].astype(F32)
    zero = jnp.zeros((8, w_rec.shape[0]), F32)
    backward_steps(
        role, lengths, factors, grad_out, w_rec, grad_pre, 0, factors.shape[1], (zero, zero)
    )
    pre_out[...] = grad_pre[...].astype(BF16)


def listen_backward(lengths, factors, grad_mine, grad_other, w_rec):
    utts, time_len, _ = factors.shape
    units = w_rec.shape[0]
    vmem = pl.BlockSpec(memory_space=pltpu.VMEM)
    return pl.pallas_call(
        listen_backward_kernel,
        out_shape=jax.ShapeDtypeStruct((utts, time_len, 4 * units), BF16),
        in_specs=[pl.BlockSpec(memory_space=pltpu.SMEM)] + [vmem] * 4,
        out_specs=vmem,
        scratch_shapes=[
            pltpu.VMEM((utts, time_len, 4 * units), F32),
            pltpu.VMEM((utts, time_len, units), F32),
        ],
        compiler_params=pltpu.CompilerParams(vmem_limit_bytes=VMEM_BYTES),
    )(lengths, factors, grad_mine, grad_other, w_rec)


SEGMENT = 32
STREAMS = ((0, 3), (3, 5), (5, 6))


def remote(src, dst, send, recv, device):
    return pltpu.make_async_remote_copy(
        src_ref=src, dst_ref=dst, send_sem=send, recv_sem=recv,
        device_id=device, device_id_type=pl.DeviceIdType.MESH,
    )


def start(copies):
    for copy in copies:
        copy.start()


def wait(copies):
    for copy in copies:
        copy.wait()


class Gather:
    def __init__(self, dims, me, view, chunks, sems):
        self.dims, self.view, self.chunks = dims, view, chunks
        self.role, self.z, self.y, self.x = me
        self.send, self.recv = sems

    def device(self, z, y, x):
        _, ny, nx = self.dims
        return (self.role, (z * ny + y) * nx + x)

    def copies(self, k, which, spans, others, base):
        out = []
        for device in others:
            for span in spans:
                ref = self.view(which, k, *span)
                out.append(
                    remote(ref, ref, self.send.at[k, base], self.recv.at[k, base], device)
                )
                base += 1
        return out

    def along_x(self):
        nx = self.dims[2]
        return [self.device(self.z, self.y, (self.x + j) % nx) for j in range(1, nx)]

    def along_y(self):
        ny = self.dims[1]
        return [self.device(self.z, (self.y + j) % ny, self.x) for j in range(1, ny)]

    def first(self, k):
        nz, ny, nx = self.dims
        slot = (self.y * nx + self.x) * nz + self.z
        others = [self.device((self.z + j) % nz, self.y, self.x) for j in range(1, nz)]
        return self.copies(k, None, [(slot, 1)], others, 0)

    def second(self, k):
        nz, ny, nx = self.dims
        column = ((self.y * nx + self.x) * nz, nz)
        base = nz - 1
        to_x = self.copies(k, 0, [column], self.along_x(), base)
        return to_x + self.copies(k, 1, [column], self.along_y(), base + nx - 1)

    def third(self, k):
        nz, ny, nx = self.dims
        base = nz - 1 + nx - 1 + ny - 1
        to_y = self.copies(k, 0, [(self.y * nx * nz, nx * nz)], self.along_y(), base)
        spans = [((b * nx + self.x) * nz, nz) for b in range(ny)]
        return to_y + self.copies(k, 1, spans, self.along_x(), base + ny - 1)

    @staticmethod
    def semaphores(dims, chunks):
        nz, ny, nx = dims
        count = nz - 1 + 2 * (nx - 1) + 2 * (ny - 1) + (nx - 1) * (ny - 1)
        return pltpu.SemaphoreType.DMA((len(chunks), count))


SP_CHUNKS = ((0, 352), (352, 352), (704, 320), (1024, 320))
LI_CHUNKS = ((0, 352), (352, 320))


def exchange_kernel(
    dims,
    lengths, factors, grad_mine, grad_other, w_in, w_rec, dp1, dp2, pack, acts_all, pairs_all, rows_all,
    frames_out, li_out, sp_out,
    grad_pre, grad_out, acts_buf, pairs_buf, rows_buf, dp_pair, got, got_t, prod, column,
    li_send, li_got, li_rows, li_acc, li_all, fr_send, fr_got, weave,
    pk_pair, pk_x, pk_xsum, pk_y, pk_ysum, pk_z,
    local_sem, chip_send, chip_recv, aa_send, aa_recv, li_aa_send, li_aa_recv,
    sp_send, sp_recv, li_ag_send, li_ag_recv, pk_send, pk_recv,
):
    nz, ny, nx = dims
    chips = nz * ny * nx
    role = lax.axis_index("role")
    dp = lax.axis_index("dp")
    z, y, x = dp // (ny * nx), (dp // nx) % ny, dp % nx
    utts, time_len, width = grad_pre.shape
    units = w_rec.shape[0]
    cells = dp1.shape[1] // 4
    half_time = time_len // 2
    pads = dp1.shape[0]
    twin = (1 - role, dp)

    def slot_of(chip):
        return (((chip // nx) % ny) * nx + chip % nx) * nz + chip // (ny * nx)

    slot = slot_of(dp)
    lanes = pl.ds(pl.multiple_of(slot * 128, 128), 128)

    barrier = pltpu.get_barrier_semaphore()
    mesh = pl.DeviceIdType.MESH

    def greet(k, _):
        pl.semaphore_signal(barrier, inc=1, device_id=(role, (dp + k) % chips), device_id_type=mesh)
        return 0

    pl.semaphore_signal(barrier, inc=1, device_id=twin, device_id_type=mesh)
    lax.fori_loop(1, chips, greet, 0)
    load_acts = pltpu.make_async_copy(
        acts_all.at[:, pl.ds(pl.multiple_of(role * cells, 128), acts_buf.shape[1])],
        acts_buf, local_sem.at[0],
    )
    load_acts.start()
    load_rows = pltpu.make_async_copy(rows_all, rows_buf, local_sem.at[1])
    load_rows.start()
    load_pairs = pltpu.make_async_copy(pairs_all, pairs_buf, local_sem.at[4])
    load_pairs.start()
    dp_pair[role] = jnp.where(role == 0, dp1[...], dp2[...])
    dp_pair[2] = jnp.where(role == 0, dp2[...], dp1[...])
    grad_out[role] = grad_mine[...].astype(F32)
    grad_out[1 - role] = grad_other[...].astype(F32)
    pl.semaphore_wait(barrier, chips)

    to_twin = remote(dp_pair.at[2], dp_pair.at[role], chip_send.at[0], chip_recv.at[0], twin)
    to_twin.start()
    pack_twin = remote(pack, pk_pair, pk_send.at[0], pk_recv.at[0], twin)

    @pl.when(role == 0)
    def _():
        pack_twin.start()

    to_twin.wait()

    def block(k):
        chip = (dp + k) % chips
        cut = pl.ds(pl.multiple_of(slot_of(chip) * 128, 128), 128)
        return remote(
            dp_pair.at[pl.ds(0, 2), :, cut], got.at[dp],
            aa_send.at[k - 1], aa_recv.at[k - 1], (role, chip),
        )

    lax.fori_loop(1, chips, lambda k, _: (block(k).start(), 0)[1], 0)
    own_block = pltpu.make_async_copy(
        dp_pair.at[pl.ds(0, 2), :, lanes], got.at[dp], local_sem.at[2]
    )
    own_block.start()

    plain = pack.shape[0] - 2 * SMALL

    def rounded(total):
        value = total[plain : plain + SMALL] + total[plain + SMALL :]
        high = value.astype(BF16)
        low = (value - high.astype(F32)).astype(BF16)
        return jnp.concatenate([total[:plain].astype(BF16), high, low], 0)

    chip_at = lambda a, b, c: (role, (a * ny + b) * nx + c)
    x_other, y_other = (x + 1) % nx, (y + 1) % ny
    column_wide = nz * 128

    def pack_x(b):
        first = pl.multiple_of((b * nx + x_other) * column_wide, 128)
        return remote(
            pk_pair.at[:, pl.ds(first, column_wide)], pk_x.at[b],
            pk_send.at[1 + b], pk_recv.at[1 + b], chip_at(z, y, x_other),
        )

    pack_y = remote(
        pk_xsum.at[y_other], pk_y, pk_send.at[1 + ny], pk_recv.at[1 + ny], chip_at(z, y_other, x)
    )

    def pack_z(j):
        to = (z + j) % nz
        return remote(
            pk_ysum.at[:, pl.ds(pl.multiple_of(to * 128, 128), 128)], pk_z.at[z],
            pk_send.at[1 + ny + j], pk_recv.at[1 + ny + j], chip_at(to, y, x),
        )

    @pl.when(role == 0)
    def _():
        pack_twin.wait_send()

    @pl.when(role == 1)
    def _():
        pack_twin.wait_recv()

        def add(b, _):
            cut = pl.ds(pl.multiple_of(b * 128, 128), 128)
            total = pk_pair[:, cut].astype(F32) + pack[:, cut].astype(F32)
            pk_pair[:, cut] = rounded(total)
            return 0

        lax.fori_loop(0, pack.shape[1] // 128, add, 0)
        for b in range(ny):
            pack_x(b).start()

    def pack_after_x():
        for b in range(ny):
            pack_x(b).wait()
            first = pl.multiple_of((b * nx + x) * column_wide, 128)

            def add(c, _):
                here = pl.ds(pl.multiple_of(first + c * 128, 128), 128)
                cut = pl.ds(pl.multiple_of(c * 128, 128), 128)
                total = pk_pair[:, here].astype(F32) + pk_x[b, :, cut].astype(F32)
                pk_xsum[b, :, cut] = rounded(total)
                return 0

            lax.fori_loop(0, nz, add, 0)
        pack_y.start()

    def pack_after_y():
        pack_y.wait()

        def add(c, _):
            cut = pl.ds(pl.multiple_of(c * 128, 128), 128)
            total = pk_xsum[y, :, cut].astype(F32) + pk_y[:, cut].astype(F32)
            pk_ysum[:, cut] = rounded(total)
            return 0

        lax.fori_loop(0, nz, add, 0)
        for j in range(1, nz):
            pack_z(j).start()

    def pack_after_z():
        for j in range(1, nz):
            pack_z(j).wait()
        pk_z[z] = pk_ysum[:, pl.ds(pl.multiple_of(z * 128, 128), 128)]
        total = pk_z[0].astype(F32)
        for j in range(1, nz):
            total = total + pk_z[j].astype(F32)
        column[column.shape[0] - total.shape[0] :, :] = rounded(total)

    def view_sp(which, k, first, count):
        rows = SP_CHUNKS[k]
        if which is not None:
            rows = (rows[0] + which * rows[1] // 2, rows[1] // 2)
        cut = pl.ds(pl.multiple_of(first * 128, 128), count * 128)
        return sp_out.at[role, pl.ds(*rows), cut]

    def view_li(which, k, first, count):
        rows = LI_CHUNKS[k]
        if which is not None:
            rows = (rows[0] + which * rows[1] // 2, rows[1] // 2)
        return li_all.at[pl.ds(first, count), pl.ds(*rows)]

    me = (role, z, y, x)
    sp = Gather(dims, me, view_sp, SP_CHUNKS, (sp_send, sp_recv))
    li = Gather(dims, me, view_li, LI_CHUNKS, (li_ag_send, li_ag_recv))

    def sp_last(k):
        ref = sp_out.at[role, pl.ds(*SP_CHUNKS[k])]
        return [remote(ref, ref, chip_send.at[2 + k], chip_recv.at[2 + k], twin)]

    def rows_of(j):
        return jnp.where(role == 1, SEGMENT * j, time_len - SEGMENT * (j + 1))

    def pack_columns(first_segment, last_segment):
        lane = lax.broadcasted_iota(jnp.int32, (SEGMENT, 128), 1)
        for j in range(first_segment, last_segment):
            rows = pl.ds(pl.multiple_of(rows_of(j), SEGMENT), SEGMENT)
            for b in range(width // 128):
                one = grad_pre[0, rows, b * 128 : (b + 1) * 128]
                two = grad_pre[1, rows, b * 128 : (b + 1) * 128]
                even = jnp.where(lane < 64, one, pltpu.roll(two, 64, 1))
                odd = jnp.where(lane < 64, pltpu.roll(one, 64, 1), two)
                li_send[2 * b, rows, :] = even.astype(BF16)
                li_send[2 * b + 1, rows, :] = odd.astype(BF16)

    def stream(n):
        first_segment, last_segment = STREAMS[n]
        count = SEGMENT * (last_segment - first_segment)
        begin = jnp.where(role == 1, SEGMENT * first_segment, time_len - SEGMENT * last_segment)
        rows = pl.ds(pl.multiple_of(begin, SEGMENT), count)

        def one(k):
            chip = (dp + k) % chips
            return remote(
                li_send.at[slot_of(chip), rows], li_got.at[dp, rows],
                li_aa_send.at[n, k - 1], li_aa_recv.at[n, k - 1], (role, chip),
            )

        return one

    def start_stream(n):
        pack_columns(*STREAMS[n])
        one = stream(n)
        lax.fori_loop(1, chips, lambda k, _: (one(k).start(), 0)[1], 0)

    def wait_stream(n):
        one = stream(n)
        lax.fori_loop(1, chips, lambda k, _: (one(k).wait(), 0)[1], 0)

    zero = jnp.zeros((8, units), F32)
    carry = (zero, zero)

    def run(j, carry):
        return backward_steps(
            role, lengths, factors, grad_out, w_rec, grad_pre, SEGMENT * j, SEGMENT, carry
        )

    carry = run(0, carry)
    pl.when(role == 1)(pack_after_x)
    carry = run(1, carry)
    pl.when(role == 1)(pack_after_y)

    lax.fori_loop(1, chips, lambda k, _: (block(k).wait(), 0)[1], 0)
    own_block.wait()
    load_acts.wait()
    both = got[...].reshape(chips * 2 * pads, 128).astype(F32)
    rolled = pltpu.roll(both, chips * 2 * pads - 1, 0)
    got_t[0] = jnp.transpose(both).astype(BF16)
    got_t[1] = jnp.transpose(rolled).astype(BF16)
    groups = acts_buf.shape[1] // 256
    span = groups * 256
    for g in range(groups):
        cut = slice(g * 256, (g + 1) * 256)
        if g == 0:
            left = got_t[0]
        elif g < groups - cells // 256:
            left = got_t[1 - role]
        else:
            left = got_t[1]
        to = (g + groups - 1) % groups * 256
        prod[:, to : to + 256] = mm(left, acts_buf[:, cut])
    column[:span, :] = jnp.transpose(prod[...]).astype(BF16)
    column[span:, :] = jnp.zeros((column.shape[0] - span, 128), BF16)

    def place(first, count):
        copy = pltpu.make_async_copy(
            column.at[pl.ds(first, count)], sp_out.at[role, pl.ds(first, count), lanes],
            local_sem.at[3],
        )
        copy.start()
        copy.wait()

    tail_first, tail_count = SP_CHUNKS[-1]
    place(0, tail_first)
    for k in range(len(SP_CHUNKS) - 1):
        start(sp.first(k))

    carry = run(2, carry)
    pl.when(role == 1)(pack_after_z)
    place(tail_first, tail_count)
    start(sp.first(len(SP_CHUNKS) - 1))
    start_stream(0)
    far = jnp.where(role == 0, half_time, 0)
    near = half_time - far
    for u in range(utts):
        rows = pl.ds(pl.multiple_of(far, half_time), half_time)
        fr_send[u] = mm_nt(grad_pre[u, rows, :].astype(BF16), w_in[...]).astype(BF16)
    frames_copy = remote(fr_send, fr_got, chip_send.at[1], chip_recv.at[1], twin)
    frames_copy.start()
    wait(sp.first(0))
    start(sp.second(0))
    carry = run(3, carry)
    wait(sp.first(1))
    start(sp.second(1))
    wait(sp.second(0))
    start(sp.third(0))
    carry = run(4, carry)
    start_stream(1)
    wait(sp.first(2))
    start(sp.second(2))
    wait(sp.second(1))
    start(sp.third(1))
    carry = run(5, carry)
    start_stream(2)
    wait(sp.first(3))
    start(sp.second(3))
    wait(sp.second(2))
    start(sp.third(2))

    frames_copy.wait()
    feat = frames_out.shape[2]
    for u in range(utts):
        rows = pl.ds(pl.multiple_of(near, half_time), half_time)
        total = mm_nt(grad_pre[u, rows, :].astype(BF16), w_in[...]) + fr_got[u].astype(F32)
        for j in range(feat // 128):
            for half in range(2):
                cut = slice(half * feat + j * 128, half * feat + (j + 1) * 128)
                weave[pl.ds(half, half_time, stride=2), :] = total[:, cut]
            frames_out[u, :, j * 128 : (j + 1) * 128] = weave[...]

    li_got[dp] = li_send[slot]
    load_rows.wait()
    load_pairs.wait()
    for n in range(len(STREAMS)):
        wait_stream(n)

    def spread(c, _):
        value = li_got[c].astype(F32)
        base = pl.multiple_of(c * 2 * time_len, 16)
        li_rows[pl.ds(base, time_len), :] = value.astype(BF16)
        base = pl.multiple_of(c * 2 * time_len + time_len, 16)
        li_rows[pl.ds(base, time_len), :] = pltpu.roll(value, 64, 1).astype(BF16)
        return 0

    lax.fori_loop(0, chips, spread, 0)
    li_acc[...] = jnp.zeros_like(li_acc)
    deep = 4 * time_len
    features = pairs_buf.shape[1]

    def accumulate(c, _):
        rows = pl.ds(pl.multiple_of(c * deep, 256), deep)
        left = jnp.transpose(li_rows[rows, :])
        li_acc[:, :features] += mm(left, pairs_buf[rows, :])
        li_acc[:, features:] += mm(left, rows_buf[rows, :])
        return 0

    lax.fori_loop(0, chips * 2 * time_len // deep, accumulate, 0)
    flipped = jnp.transpose(li_acc[...])
    tall = flipped.shape[0] // 2
    lane = lax.broadcasted_iota(jnp.int32, (tall, 128), 1)
    packed = jnp.where(lane < 64, flipped[:tall], pltpu.roll(flipped[tall:], 64, 1))
    li_all[slot] = packed.astype(BF16)

    for k in range(len(LI_CHUNKS)):
        start(li.first(k))
    wait(sp.second(3))
    start(sp.third(3))
    wait(li.first(0))
    start(li.second(0))
    wait(sp.third(0))
    start(sp_last(0))
    wait(sp.third(1))
    start(sp_last(1))
    wait(li.first(1))
    start(li.second(1))
    wait(li.second(0))
    start(li.third(0))
    wait(sp.third(2))
    start(sp_last(2))
    wait(li.second(1))
    start(li.third(1))
    wait(sp.third(3))
    start(sp_last(3))
    wait(li.third(0))
    wait(li.third(1))

    def assemble(b, _):
        cut = pl.ds(pl.multiple_of(b * 128, 128), 128)
        even = li_all[2 * b].astype(F32)
        odd = li_all[2 * b + 1].astype(F32)
        li_out[:tall, cut] = jnp.where(lane < 64, even, pltpu.roll(odd, 64, 1)).astype(BF16)
        li_out[tall:, cut] = jnp.where(lane < 64, pltpu.roll(even, 64, 1), odd).astype(BF16)
        return 0

    lax.fori_loop(0, width // 128, assemble, 0)
    for k in range(len(SP_CHUNKS)):
        wait(sp_last(k))


def exchange(
    dims, lengths, factors, grad_mine, grad_other, w_in, w_rec, dp1, dp2, pack, acts_all, pairs_all, rows_all
):
    utts, time_len, _ = factors.shape
    units = w_rec.shape[0]
    width = 4 * units
    pads, wide = dp1.shape
    cells = wide // 4
    chips = dims[0] * dims[1] * dims[2]
    span = acts_all.shape[1] - cells
    deep = sum(rows for _, rows in SP_CHUNKS)
    nz, ny, _ = dims
    packed = pack.shape[0]
    total = pairs_all.shape[1] + rows_all.shape[1]
    feat = w_in.shape[0] // 2
    half_time = time_len // 2
    vmem = pl.BlockSpec(memory_space=pltpu.VMEM)
    anywhere = pl.BlockSpec(memory_space=pl.ANY)
    shape = jax.ShapeDtypeStruct
    dma = pltpu.SemaphoreType.DMA
    sp_sems = Gather.semaphores(dims, SP_CHUNKS)
    li_sems = Gather.semaphores(dims, LI_CHUNKS)
    return pl.pallas_call(
        functools.partial(exchange_kernel, dims),
        out_shape=(
            shape((utts, time_len, feat), F32),
            shape((total, width), BF16),
            shape((2, deep, wide), BF16),
        ),
        in_specs=[pl.BlockSpec(memory_space=pltpu.SMEM)] + [vmem] * 8 + [anywhere] * 3,
        out_specs=(vmem, vmem, anywhere),
        scratch_shapes=[
            pltpu.VMEM((utts, time_len, width), F32),
            pltpu.VMEM((utts, time_len, units), F32),
            pltpu.VMEM((acts_all.shape[0], span), BF16),
            pltpu.VMEM(pairs_all.shape, BF16),
            pltpu.VMEM(rows_all.shape, BF16),
            pltpu.VMEM((3, pads, wide), BF16),
            pltpu.VMEM((chips, 2, pads, 128), BF16),
            pltpu.VMEM((2, 128, chips * 2 * pads), BF16),
            pltpu.VMEM((128, span), F32),
            pltpu.VMEM((deep, 128), BF16),
            pltpu.VMEM((chips, time_len, 128), BF16),
            pltpu.VMEM((chips, time_len, 128), BF16),
            pltpu.VMEM((chips * 2 * time_len, 128), BF16),
            pltpu.VMEM((128, total), F32),
            pltpu.VMEM((chips, total // 2, 128), BF16),
            pltpu.VMEM((utts, half_time, 2 * feat), BF16),
            pltpu.VMEM((utts, half_time, 2 * feat), BF16),
            pltpu.VMEM((time_len, 128), F32),
            pltpu.VMEM((packed, wide), BF16),
            pltpu.VMEM((ny, packed, nz * 128), BF16),
            pltpu.VMEM((ny, packed, nz * 128), BF16),
            pltpu.VMEM((packed, nz * 128), BF16),
            pltpu.VMEM((packed, nz * 128), BF16),
            pltpu.VMEM((nz, packed, 128), BF16),
            dma((5,)),
            dma((2 + len(SP_CHUNKS),)),
            dma((2 + len(SP_CHUNKS),)),
            dma((chips - 1,)),
            dma((chips - 1,)),
            dma((len(STREAMS), chips - 1)),
            dma((len(STREAMS), chips - 1)),
            sp_sems,
            sp_sems,
            li_sems,
            li_sems,
            dma((1 + ny + nz,)),
            dma((1 + ny + nz,)),
        ],
        compiler_params=pltpu.CompilerParams(
            vmem_limit_bytes=VMEM_BYTES, collective_id=0, has_side_effects=True
        ),
        cost_estimate=pl.CostEstimate(
            flops=100_000_000_000, bytes_accessed=100_000_000, transcendentals=0
        ),
    )(
        lengths, factors, grad_mine, grad_other, w_in, w_rec, dp1, dp2, pack,
        acts_all, pairs_all, rows_all,
    )


def shards(
    frames,
    step_lengths,
    characters,
    char_lengths,
    listen_input,
    listen_hidden,
    listen_bias,
    lower_input,
    lower_hidden,
    lower_bias,
    upper_input,
    upper_hidden,
    upper_bias,
    key_proj,
    query_proj,
    score_vector,
    output_proj,
    output_bias,
    char_table,
):
    chips = lax.axis_size("dp")
    utts, frame_len, feat = frames.shape
    time_len = frame_len // 2
    swap = [(0, 1), (1, 0)]
    w_in, w_rec = listen_input[0], listen_hidden[0]
    units = w_rec.shape[0]
    cells = lower_hidden.shape[0]
    vocab, embed = char_table.shape
    pairs = frames.reshape(utts, time_len, 2 * feat)
    rows, factors, mine, other = listen_forward(step_lengths, pairs, w_in, w_rec, listen_bias)
    other = lax.ppermute(other, "role", swap)
    chars = characters[0, 0]
    previous = jnp.concatenate([jnp.zeros((1,), jnp.int32), chars[:-1]])
    ids = jnp.arange(vocab)[None, :]
    prev_onehot = (previous[:, None] == ids).astype(BF16)
    target_onehot = (chars[:, None] == ids).astype(F32)
    vec = score_vector[None]
    loss, acts, key, *kept = speller_forward(
        step_lengths, char_lengths, mine, other, prev_onehot, target_onehot,
        lower_input, lower_hidden, lower_bias[None], upper_input, upper_hidden, upper_bias[None],
        key_proj, query_proj, vec, output_proj, output_bias[None], char_table,
    )
    grad_mine, grad_other, dp1, dp2, pack = speller_backward(
        lower_input, lower_hidden, upper_input, upper_hidden, key_proj, query_proj, vec,
        prev_onehot, acts, key, *kept,
    )
    grad_other = lax.ppermute(grad_other, "role", swap)
    fits = (
        chips % 4 == 0
        and 4 * cells == 128 * chips
        and 4 * units == 64 * chips
        and embed == 256
        and cells == 2 * units
        and time_len == SEGMENT * STREAMS[-1][1]
        and cells + 2 * units == SP_CHUNKS[-1][0]
        and pack.shape[0] == SP_CHUNKS[-1][1]
        and 2 * feat + units + 64 == 2 * sum(rows for _, rows in LI_CHUNKS)
    )
    if fits:
        own_pairs = lax.dynamic_index_in_dim(pairs, lax.axis_index("role"), 0, keepdims=False)
        pairs_all = lax.all_gather(own_pairs, ("dp", "role"), tiled=True)
        rows_all = lax.all_gather(rows, "dp", tiled=True)
        acts_all = lax.all_gather(acts, ("dp", "role"), tiled=True)
        frame_grad, li, sp = exchange(
            (chips // 4, 2, 2), step_lengths, factors, grad_mine, grad_other, w_in, w_rec,
            dp1, dp2, pack, acts_all, pairs_all, rows_all,
        )
        width = 2 * feat
        sum_in, sum_rec = li[:width].astype(F32), li[width : width + units].astype(F32)
        sum_bias = li[width + units : width + units + 1].astype(F32)
        low, high = 2 * units, 2 * units + cells
        lower = (
            jnp.concatenate([sp[0, high : high + embed], sp[0, :low]], 0).astype(F32),
            sp[0, low:high].astype(F32),
        )
        upper = (sp[1, :cells].astype(F32), sp[1, cells:high].astype(F32))
        pack = sp[1, high:]
    else:
        pack = lax.psum(pack.astype(F32), ("role", "dp"))
        pre = listen_backward(step_lengths, factors, grad_mine, grad_other, w_rec)
        flat = pre.reshape(utts * time_len, 4 * units)
        sums = mm(jnp.concatenate([pairs.reshape(flat.shape[0], 2 * feat), rows], 1).T, flat)
        sums = lax.psum(sums, "dp")
        width = 2 * feat
        sum_in, sum_rec = sums[:width], sums[width : width + units]
        sum_bias = sums[width + units : width + units + 1]
        grad_pairs = mm(flat, w_in.T).reshape(utts, frame_len, feat)
        frame_grad = lax.psum_scatter(grad_pairs, "role", scatter_dimension=1, tiled=True)
        cuts = [embed, embed + 2 * units, embed + 2 * units + cells]
        emb, ctx, s1, s2 = jnp.split(acts, cuts, axis=1)
        local = (
            jnp.concatenate([mm(emb.T, dp1), mm(ctx[:-1].T, dp1[1:])], 0),
            mm(s1[:-1].T, dp1[1:]),
            mm(s1.T, dp2),
            mm(s2[:-1].T, dp2[1:]),
        )
        local = lax.psum(local, ("role", "dp"))
        lower, upper = local[:2], local[2:]
    low_bias, up_bias, g_key, g_query, g_vec, g_out, g_obias, g_table = unpack(
        pack, units, cells, key_proj.shape[1], vocab, embed
    )
    return (
        loss, frame_grad, sum_in[None], sum_rec[None], sum_bias,
        *lower, low_bias, *upper, up_bias,
        g_key, g_query, g_vec, g_out, g_obias, g_table,
    )


def solution(mesh):
    whole = P()
    return jax.shard_map(
        shards,
        mesh=mesh,
        in_specs=(
            P("dp", None, None),
            P("dp"),
            P("dp", "role", None),
            P("dp", "role"),
            P("role", None, None),
            P("role", None, None),
            P("role", None),
        )
        + (whole,) * 12,
        out_specs=(
            P("dp", "role"),
            P("dp", "role", None),
            P("role", None, None),
            P("role", None, None),
            P("role", None),
        )
        + (whole,) * 12,
        check_vma=False,
    )
```

time: 952 us -> 539 us (0.57)
  waiting for transfers between devices: 424 us -> 1.57 us
  Pallas kernels: 400 us -> 476 us
  blocking collectives: 70.9 us -> 0 us
  other arithmetic: 1.43 us -> 22.8 us
  local copies, waits for them, and re-layouts: 34.5 us -> 23.4 us
    psum x2 -> x0, waiting for transfers between devices: 422 us -> none  [the longest x1 227 us: shards(): summed = lax.psum(tuple(grads), ('role', 'dp'))]
    pallas_call x3 -> x4, Pallas kernels: 400 us -> 476 us  [the longest x1 188 us: speller_backward(): pl.pallas_call(speller_backward_kernel, out_shape=outs, in_specs=[vmem] *...]
    psum x2 -> x0, blocking collectives: 70.9 us -> none  [the longest x1 42.5 us: shards(): summed = lax.psum(tuple(grads), ('role', 'dp'))]
    unnamed x42 -> x25, local copies, waits for them, and re-layouts: 27.4 us -> 4.24 us
    convert_element_type x0 -> x3, other arithmetic: none -> 13.5 us  [the longest x1 8.65 us: shards(): upper = (sp[1, :cells].astype(F32), sp[1, cells:high].astype(F32))]
    reshape x1 -> x5, local copies, waits for them, and re-layouts: 2.57 us -> 13 us  [the longest x4 10.9 us: unpack(): part.reshape(deep, wide // att, att).swapaxes(0, 1).reshape(-1, att)]
  transfers between devices with their start and end apart: 5 -> 5, of which waited for: 3 -> 1; matrix products, arithmetic and copies ran while one was open for 1% -> 1% of each run, Pallas kernels for 6% -> 55%
where the time goes in v2:
time: 539 us
  Pallas kernels  476 us (88%)
  local copies, waits for them, and re-layouts  23.4 us (4%)
  other arithmetic  22.8 us (4%)
  between operations  14.5 us (3%)
    pallas_call x1, Pallas kernels, speller_backward(): pl.pallas_call(speller_backward_kernel, out_shape=outs, in_specs=[vmem] *...  188 us
    pallas_call x1, Pallas kernels, exchange(): pl.pallas_call(functools.partial(exchange_kernel, dims), out_shape=(shape...  134 us
    pallas_call x1, Pallas kernels, speller_forward(): pl.pallas_call(speller_forward_kernel, out_shape=outs, in_specs=[smem] *...  110 us
    pallas_call x1, Pallas kernels, listen_forward(): pl.pallas_call(listen_forward_kernel, out_shape=(shape((utts * time_len,...  44 us
    reshape x4, local copies, waits for them, and re-layouts, unpack(): part.reshape(deep, wide // att, att).swapaxes(0, 1).reshape(-1, att)  10.9 us
  transfers between devices with their start and end apart: 5, of which 1 were waited for; matrix products, arithmetic and copies ran while one was open for 1% of the time, Pallas kernels for 55%

profile of v2, /device:TPU:9, one launch (start us, length us, event | category | flops | bytes accessed | tf_op | source)
XLA Modules:
  0.0 538.9 jit_solution(8169992038309984196)
XLA Ops:
  7.3 2.1 reshape.79.pairs
  9.4 44.0 %shard_map.314 = (bf16[384,320]{1,0:T(8,128)(2,1)}, f32[2,192,1536]{2,1,0:T(8,128)}, bf16[192,256]{1,0:T(8,128)(2,1)}, bf16[192,256]{1,0:T(8,128)(2,1)}) custom-call(s32[2]{0:T(128)} %lengths.5, bf16[2,192,1024]{2,1,0:T(8,128)(2,1)} %reshape.79.pairs, bf16[1024,1024]{1,0:T(8,128)(2,1)} %bitcast.45, bf16[256,1024]{1,0:T(8,128)(2,1)} %bitcast.49, ...), custom_call_target="tpu_custom_call" | custom-call | tf_op jit(solution)/shard_map/pallas_call | solution.py:108
  53.5 0.7 collective-permute-start
  54.3 0.7 fusion
  57.5 0.9 copy.36.w_out
  59.0 109.9 %shard_map.315 = (f32[1,1]{1,0:T(1,128)}, bf16[80,1792]{1,0:T(8,128)(2,1)}, bf16[256,512]{1,0:T(8,128)(2,1)}, f32[192,512]{1,0:T(8,128)}, bf16[2048,256]{1,0:T(8...) custom-call(s32[2]{0:T(128)} %lengths.5, ...), custom_call_target="tpu_custom_call" | custom-call | tf_op jit(solution)/shard_map/pallas_call | solution.py:260
  169.0 0.8 constant_dynamic-slice_fusion
  169.8 188.2 %shard_map.316 = (bf16[192,256]{1,0:T(8,128)(2,1)}, bf16[192,256]{1,0:T(8,128)(2,1)}, bf16[80,2048]{1,0:T(8,128)(2,1)}, bf16[80,2048]{1,0:T(8,128)(2,1)}, bf16[320,2048]{1,0:T(8,128)(2,1)}) custom-call(bf16[768,2048]{1,0:T(8,128)(2,1)} %w_lin.3, bf16[512,2048]{1,0:T(8,128)(2,1)} %w_lhid.3, bf16[512,2048]{1,0:T(8,128)(2,1)} %w_uin.3, ...), custom_call_target="tpu_custom_call" | custom-call | tf_op jit(solution)/shard_map/pallas_call | solution.py:411
  358.0 1.5 collective-permute-done.1.grad_other
  360.2 133.6 %shard_map.317 = (f32[2,192,512]{2,1,0:T(8,128)}, bf16[1344,1024]{1,0:T(8,128)(2,1)}, bf16[2,1344,2048]{2,1,0:T(8,128)(2,1)}) custom-call(s32[2]{0:T(128)} %lengths.5, f32[2,192,1536]{2,1,0:T(8,128)} %get-tuple-element.44.factors, bf16[192,256]{1,0:T(8,128)(2,1)} %get-tuple-element.56.grad_mine, bf16[192,256]{1,0:T(8,128)(2,1)} %copy-done.9, ...), custom_call_target="tpu_custom_call" | custom-call | flops 99999997952 | bytes 100000000 | tf_op jit(solution)/shard_map/pallas_call | solution.py:987
  493.7 1.1 add_bitcast_fusion
  496.6 0.7 slice_bitcast_fusion.2
  497.3 1.3 slice_convert_fusion.2
  498.6 2.1 bitcast_convert_fusion.4
  500.7 1.3 slice_bitcast_fusion.1
  502.0 2.5 bitcast_convert_fusion.3
  504.5 2.8 slice_convert_fusion
  507.2 8.7 %bitcast_convert_fusion = (f32[512,2048]{1,0:T(8,128)}, f32[512,2048]{1,0:T(8,128)}, f32[512,2048]{1,0:T(8,128)}, bf16[512,2048]{1,0:T(8,128)(2,1)S(1)}) fusion(bf16[2,1344,2048]{2,1,0:T(8,128)(2,1)} %get-tuple-element.64), kind=kLoop, calls=%fused_computation.1 | loop fusion | flops 3145728 | bytes 23068672 | tf_op jit(solution)/shard_map/convert_element_type | solution.py:1123
  517.1 2.9 reshape.100
  520.0 2.5 copy.38
  522.5 2.9 reshape.98
  525.4 2.5 copy.37
  528.0 3.5 maximum_convert_fusion
  531.5 0.9 copy.43
  (42 shorter events, 6.3 us)
Async XLA Ops:
  7.2 47.0 %copy-start.8 = (s32[1,1,72]{2,1,0:T(1,128)S(1)}, s32[1,1,72]{2,1,0:T(1,128)}, u32[]{:S(2)}) copy-start(s32[1,1,72]{2,1,0:T(1,128)} %param.21) | copy-start | bytes 868
  7.2 48.4 %copy-start.7 = (bf16[512]{0:T(512)(128)(2,1)S(1)}, bf16[512]{0:T(512)(128)(2,1)}, u32[]{:S(2)}) copy-start(bf16[512]{0:T(512)(128)(2,1)} %param.34) | copy-start | bytes 3076
  7.2 49.0 %copy-start.5 = (bf16[2048]{0:T(1024)(128)(2,1)S(1)}, bf16[2048]{0:T(1024)(128)(2,1)}, u32[]{:S(2)}) copy-start(bf16[2048]{0:T(1024)(128)(2,1)} %param.28) | copy-start | bytes 12292
  7.2 49.6 %copy-start.6 = (bf16[2048]{0:T(1024)(128)(2,1)S(1)}, bf16[2048]{0:T(1024)(128)(2,1)}, u32[]{:S(2)}) copy-start(bf16[2048]{0:T(1024)(128)(2,1)} %param.31) | copy-start | bytes 12292
  7.2 50.2 %copy-start.4 = (bf16[1024,30]{0,1:T(8,128)(2,1)S(1)}, bf16[1024,30]{0,1:T(8,128)(2,1)}, u32[]{:S(2)}) copy-start(bf16[1024,30]{0,1:T(8,128)(2,1)} %param.35) | copy-start | bytes 184324
  7.2 352.3 %all-gather.7.cloned.1.call-start = ((), (), s32[]{:S(2)}) async-start(), calls=%async_computation.1 | async-start | bytes 5013504 | tf_op jit(solution)/shard_map/all_gather | solution.py:1109
  53.4 306.1 %all-gather.5.cloned.1.call-start = ((), (), s32[]{:S(2)}) async-start(), calls=%async_computation | async-start | bytes 9461760 | tf_op jit(solution)/shard_map/all_gather | solution.py:1110
  53.5 4.9 collective-permute-start
  58.3 0.6 copy-start.3
  59.0 110.0 %copy-start = (bf16[2,192,1024]{2,1,0:T(8,128)(2,1)S(1)}, bf16[2,192,1024]{2,1,0:T(8,128)(2,1)}, u32[]{:S(2)}) copy-start(bf16[2,192,1024]{2,1,0:T(8,128)(2,1)} %reshape.79.pairs) | copy-start | bytes 2359300
  168.9 190.6 %all-gather.9.cloned.1.call-start = ((), (), s32[]{:S(2)}) async-start(), calls=%async_computation.2 | async-start | bytes 12976128 | tf_op jit(solution)/shard_map/all_gather | solution.py:1108
  358.0 1.5 collective-permute-start.1
  359.5 0.6 copy-start.9
  493.7 8.3 %copy-start.1 = (bf16[1344,1024]{1,0:T(8,128)(2,1)S(1)}, bf16[1344,1024]{1,0:T(8,128)(2,1)}, u32[]{:S(2)}) copy-start(bf16[1344,1024]{1,0:T(8,128)(2,1)} %get-tuple-element.63) | copy-start | bytes 8257540
  528.0 3.5 copy-start.2
Sparse Core Ops, SparseCore 0:
  53.5 80.2 all-gather.6
  169.1 81.7 all-gather.4
  254.3 94.1 all-gather.8

commit v3 on v2

--- a/solution.py
+++ b/solution.py
@@ -10,7 +10,6 @@
 F32 = jnp.float32
 BF16 = jnp.bfloat16
 VMEM_BYTES = 60 * 1024 * 1024
-SAFE_SCORE = 80.0
 
 
 def mm(left, right):
@@ -59,11 +58,37 @@
     return grad_preact, total * part(5)
 
 
+def remote(src, dst, send, recv, device):
+    return pltpu.make_async_remote_copy(
+        src_ref=src, dst_ref=dst, send_sem=send, recv_sem=recv,
+        device_id=device, device_id_type=pl.DeviceIdType.MESH,
+    )
+
+
+def start(copies):
+    for copy in copies:
+        copy.start()
+
+
+def wait(copies):
+    for copy in copies:
+        copy.wait()
+
+
 def listen_forward_kernel(
-    lengths, pairs, w_in, w_rec, bias, rows_out, factors_out, mine_out, other_out,
-    proj, emit, hprev,
+    dims, lengths, pairs, w_in, w_rec, bias, rows_out, factors_out, mine_out, other_out, *rest
 ):
     role = lax.axis_index("role")
+    twin = (1 - role, lax.axis_index("dp"))
+    if dims is not None:
+        proj, emit, hprev, to_other, cross = rest
+        barrier = pltpu.get_barrier_semaphore()
+        pl.semaphore_signal(
+            barrier, inc=1, device_id=twin, device_id_type=pl.DeviceIdType.MESH
+        )
+        pl.semaphore_wait(barrier, 1)
+    else:
+        proj, emit, hprev = rest
     utts, time_len, width4 = proj.shape
     units = width4 // 4
     bias_row = bias[...].astype(F32)
@@ -93,74 +118,253 @@
     zero = jnp.zeros((8, units), F32)
     lax.fori_loop(0, time_len, step, (zero, zero))
     mine_out[...] = emit[role].astype(BF16)
-    other_out[...] = emit[1 - role].astype(BF16)
+    if dims is None:
+        other_out[...] = emit[1 - role].astype(BF16)
+    else:
+        to_other[...] = emit[1 - role].astype(BF16)
+        crossing = remote(to_other, other_out, cross.at[0], cross.at[1], twin)
+        crossing.start()
     for u in range(utts):
         own = slice(u * time_len, (u + 1) * time_len)
-        rows_out[own, :units] = hprev[u].astype(BF16)
-    rows_out[:, units:] = jnp.ones((utts * time_len, rows_out.shape[1] - units), BF16)
-
-
-def listen_forward(lengths, pairs, w_in, w_rec, bias):
-    utts, time_len, _ = pairs.shape
+        rows_out[own, :] = hprev[u].astype(BF16)
+    if dims is not None:
+        crossing.wait()
+
+
+def listen_forward(dims, lengths, pairs, w_in, w_rec, bias):
+    utts, time_len, width = pairs.shape
     units = w_rec.shape[0]
     vmem = pl.BlockSpec(memory_space=pltpu.VMEM)
     shape = jax.ShapeDtypeStruct
+    outs = [
+        shape((utts * time_len, units), BF16),
+        shape((utts, time_len, 6 * units), F32),
+        shape((time_len, units), BF16),
+        shape((time_len, units), BF16),
+    ]
+    out_specs = [vmem] * 4
+    scratch = [
+        pltpu.VMEM((utts, time_len, 4 * units), F32),
+        pltpu.VMEM((utts, time_len, units), F32),
+        pltpu.VMEM((utts, time_len, units), F32),
+    ]
+    params = dict(vmem_limit_bytes=VMEM_BYTES)
+    if dims is not None:
+        scratch += [pltpu.VMEM((time_len, units), BF16), pltpu.SemaphoreType.DMA((2,))]
+        params.update(collective_id=1, has_side_effects=True)
     return pl.pallas_call(
-        listen_forward_kernel,
-        out_shape=(
-            shape((utts * time_len, units + 64), BF16),
-            shape((utts, time_len, 6 * units), F32),
-            shape((time_len, units), BF16),
-            shape((time_len, units), BF16),
-        ),
+        functools.partial(listen_forward_kernel, dims),
+        out_shape=outs,
         in_specs=[pl.BlockSpec(memory_space=pltpu.SMEM)] + [vmem] * 4,
-        out_specs=(vmem,) * 4,
-        scratch_shapes=[
-            pltpu.VMEM((utts, time_len, 4 * units), F32),
-            pltpu.VMEM((utts, time_len, units), F32),
-            pltpu.VMEM((utts, time_len, units), F32),
-        ],
-        compiler_params=pltpu.CompilerParams(vmem_limit_bytes=VMEM_BYTES),
+        out_specs=out_specs,
+        scratch_shapes=scratch,
+        compiler_params=pltpu.CompilerParams(**params),
     )(lengths, pairs, w_in, w_rec, bias)
 
 
+class Gather:
+    def __init__(self, dims, me, view, chunks, sems):
+        self.dims, self.view, self.chunks = dims, view, chunks
+        self.role, self.z, self.y, self.x = me
+        self.send, self.recv = sems
+
+    def device(self, z, y, x):
+        _, ny, nx = self.dims
+        return (self.role, (z * ny + y) * nx + x)
+
+    def copies(self, k, which, spans, others, base):
+        out = []
+        for device in others:
+            for span in spans:
+                ref = self.view(which, k, *span)
+                out.append(
+                    remote(ref, ref, self.send.at[k, base], self.recv.at[k, base], device)
+                )
+                base += 1
+        return out
+
+    def along_x(self):
+        nx = self.dims[2]
+        return [self.device(self.z, self.y, (self.x + j) % nx) for j in range(1, nx)]
+
+    def along_y(self):
+        ny = self.dims[1]
+        return [self.device(self.z, (self.y + j) % ny, self.x) for j in range(1, ny)]
+
+    def first(self, k):
+        nz, ny, nx = self.dims
+        slot = (self.y * nx + self.x) * nz + self.z
+        others = [self.device((self.z + j) % nz, self.y, self.x) for j in range(1, nz)]
+        return self.copies(k, None, [(slot, 1)], others, 0)
+
+    def second(self, k):
+        nz, ny, nx = self.dims
+        column = ((self.y * nx + self.x) * nz, nz)
+        base = nz - 1
+        to_x = self.copies(k, 0, [column], self.along_x(), base)
+        return to_x + self.copies(k, 1, [column], self.along_y(), base + nx - 1)
+
+    def third(self, k):
+        nz, ny, nx = self.dims
+        base = nz - 1 + nx - 1 + ny - 1
+        to_y = self.copies(k, 0, [(self.y * nx * nz, nx * nz)], self.along_y(), base)
+        spans = [((b * nx + self.x) * nz, nz) for b in range(ny)]
+        return to_y + self.copies(k, 1, spans, self.along_x(), base + ny - 1)
+
+    @staticmethod
+    def semaphores(dims, chunks):
+        nz, ny, nx = dims
+        count = nz - 1 + 2 * (nx - 1) + 2 * (ny - 1) + (nx - 1) * (ny - 1)
+        return pltpu.SemaphoreType.DMA((len(chunks), count))
+
+
+ROW_CHUNKS = tuple((96 * k, 96) for k in range(4))
+FRAME_CHUNKS = tuple((32 * k, 32) for k in range(6))
+FRAME_EVENTS = {
+    2: ([(0, 0)], [(1, 0)]),
+    6: ([(1, 0), (0, 1)], [(2, 0), (1, 1)]),
+    10: ([(0, 2)], [(1, 2)]),
+    12: ([(2, 0)], []),
+    14: ([(1, 1), (0, 3)], [(2, 1), (1, 3)]),
+    16: ([(1, 2)], [(2, 2)]),
+    18: ([(0, 4)], [(1, 4)]),
+    20: ([(2, 1)], []),
+    22: ([(1, 3)], [(2, 3)]),
+    24: ([(0, 5)], [(1, 5)]),
+    26: ([(2, 2)], []),
+    28: ([(1, 4), (0, 6)], [(2, 4), (1, 6)]),
+    32: ([(2, 3)], []),
+    34: ([(1, 5), (0, 7)], [(2, 5), (1, 7)]),
+    38: ([(0, 8)], [(1, 8)]),
+    40: ([(2, 4)], [(3, 4)]),
+    42: ([(1, 6), (0, 9)], [(2, 6), (1, 9)]),
+    46: ([(2, 5)], [(3, 5)]),
+    48: ([(1, 7)], [(2, 7)]),
+    52: ([(1, 8)], [(2, 8)]),
+    56: ([(2, 6)], [(3, 6)]),
+    58: ([(1, 9)], [(2, 9)]),
+    64: ([(2, 7)], [(3, 7)]),
+    68: ([(2, 8)], [(3, 8)]),
+    72: ([(2, 9)], [(3, 9)]),
+}
+
+
+class Gathers:
+    def __init__(self, dims, role, dp, states, frames, sems):
+        nz, ny, nx = dims
+        me = (role, dp // (ny * nx), (dp // nx) % ny, dp % nx)
+        self.twin = (1 - role, dp)
+        self.role, self.frames = role, frames
+        row_send, row_recv, frame_send, frame_recv, self.last_send, self.last_recv = sems
+
+        def cut(chunk, which):
+            first, count = chunk
+            if which is not None:
+                first, count = first + which * count // 2, count // 2
+            return pl.ds(first, count)
+
+        def view_states(which, k, first, count):
+            return states.at[pl.ds(first, count), cut(ROW_CHUNKS[k], which)]
+
+        def view_frames(which, k, first, count):
+            return frames.at[role, pl.ds(first, count), cut(FRAME_CHUNKS[k], which)]
+
+        self.one = Gather(dims, me, view_states, ROW_CHUNKS, (row_send, row_recv))
+        self.two = Gather(dims, me, view_frames, FRAME_CHUNKS, (frame_send, frame_recv))
+        self.slot = (me[2] * nx + me[3]) * nz + me[1]
+        one = self.one
+        to_z = [one.device((one.z + j) % nz, one.y, one.x) for j in range(1, nz)]
+        self.partners = to_z + one.along_x() + one.along_y() + [self.twin]
+
+    def phase(self, n, c):
+        if n == 3:
+            k = c - len(ROW_CHUNKS)
+            ref = self.frames.at[self.role, :, pl.ds(*FRAME_CHUNKS[k])]
+            return [remote(ref, ref, self.last_send.at[k], self.last_recv.at[k], self.twin)]
+        gather, k = (self.one, c) if c < len(ROW_CHUNKS) else (self.two, c - len(ROW_CHUNKS))
+        return (gather.first, gather.second, gather.third)[n](k)
+
+    def begin(self):
+        for c in range(len(ROW_CHUNKS) + len(FRAME_CHUNKS)):
+            start(self.phase(0, c))
+
+    def event(self, ended, begun):
+        for n, c in ended:
+            wait(self.phase(n, c))
+        for n, c in begun:
+            start(self.phase(n, c))
+
+    def look(self, step):
+        def some():
+            for at, (ended, begun) in FRAME_EVENTS.items():
+                pl.when(step == at)(functools.partial(self.event, ended, begun))
+
+        pl.when(step % 2 == 0)(some)
+
+    def finish(self, steps):
+        for at, (ended, begun) in FRAME_EVENTS.items():
+            if at >= steps:
+                self.event(ended, begun)
+        for k in range(len(FRAME_CHUNKS)):
+            wait(self.phase(3, len(ROW_CHUNKS) + k))
+
+
 def speller_forward_kernel(
-    lengths, text_lens,
+    dims, lengths, text_lens, pairs, states,
     mine, other, prev_onehot, target_onehot,
     w_lin, w_lhid, b_low, w_uin, w_uhid, b_up, w_key, w_query, vec, w_out, b_out, table,
-    loss, acts, key, keys_proj, key_low_t, fact1, fact2, q_rows, w_rows, feat_rows, dw_rows,
-    logit_grad_out,
-    key_low, emb_proj, s1_rows, s2_rows,
+    loss, acts, key, keys_proj, key_low, fact1, fact2, q_rows, w_cols, feat_rows, dw_cols,
+    logit_grad_out, *rest
 ):
     role = lax.axis_index("role")
+    gather = None
+    if dims is not None:
+        pairs_all, states_all, *rest = rest
+        rest, (stage, own_sem), sems = rest[:-8], rest[-8:-6], rest[-6:]
+        gather = Gathers(dims, role, lax.axis_index("dp"), states_all, pairs_all, sems)
+        barrier = pltpu.get_barrier_semaphore()
+        for device in gather.partners:
+            pl.semaphore_signal(
+                barrier, inc=1, device_id=device, device_id_type=pl.DeviceIdType.MESH
+            )
+        load = pltpu.make_async_copy(pairs.at[role], stage, own_sem.at[0])
+        load.start()
+        place = [
+            pltpu.make_async_copy(stage, pairs_all.at[role, gather.slot], own_sem.at[1]),
+            pltpu.make_async_copy(states, states_all.at[gather.slot], own_sem.at[2]),
+        ]
+        place[1].start()
+        load.wait()
+        place[0].start()
+        wait(place)
+        pl.semaphore_wait(barrier, len(gather.partners))
+        gather.begin()
+    emb_proj, s1_rows, s2_rows = rest
     time_len, units = mine.shape
     steps = emb_proj.shape[0]
     cells = w_lhid.shape[0]
     embed = table.shape[1]
-    pad_time = key.shape[0]
     length = lengths[role]
     text_len = text_lens[0, 0]
 
-    key[time_len:, :] = jnp.zeros((pad_time - time_len, 2 * units), BF16)
-    key[:time_len, :units] = jnp.where(role == 0, mine[...], other[...])
-    key[:time_len, units:] = jnp.where(role == 0, other[...], mine[...])
-    keys_proj[...] = mm(key[:time_len, :], w_key[...])
-    key_low_f32 = mm(key[...], w_lin[embed:, :])
-    key_low[...] = key_low_f32.astype(BF16)
-    key_low_t[...] = jnp.transpose(key_low_f32).astype(BF16)
+    key[:, :units] = jnp.where(role == 0, mine[...], other[...])
+    key[:, units:] = jnp.where(role == 0, other[...], mine[...])
+    keys_proj[...] = mm(key[...], w_key[...])
+    key_low[...] = mm(key[...], w_lin[embed:, :])
     emb = mm(prev_onehot[...], table[...]).astype(BF16)
     emb_proj[...] = mm(emb, w_lin[:embed, :]) + b_low[...].astype(F32)
     bias_up = b_up[...].astype(F32)
     vec_row = vec[...].astype(F32)
-    lane = lax.broadcasted_iota(jnp.int32, (1, pad_time), 1)
-    frame_ok = lane < length
-    ones = jnp.ones((1, 256), BF16)
-    tail = jnp.zeros((pad_time - time_len, 256), BF16)
-
-    def forward_step(shift_by_max, i, carry):
-        cell1, cell2, hid1, hid2, expw, rinv = carry
+    frame_ok = lax.broadcasted_iota(jnp.int32, (time_len, 1), 0) < length
+    lane = lax.broadcasted_iota(jnp.int32, w_cols.shape, 1)
+    w_cols[...] = jnp.zeros_like(w_cols)
+
+    def forward_step(i, carry):
+        cell1, cell2, hid1, hid2, ctx_low = carry
+        if gather is not None:
+            gather.look(i)
         at = pl.ds(i, 1)
-        pre1 = emb_proj[at, :] + hid1 + mm(expw, key_low[...]) * rinv
+        pre1 = emb_proj[at, :] + hid1 + ctx_low
         cell1, s1, factors = cell_forward(pre1, cell1)
         for k in range(6):
             fact1[at, k * cells : (k + 1) * cells] = factors[k]
@@ -181,35 +385,29 @@
             cut = slice(j * 128, (j + 1) * 128)
             term = jnp.tanh(keys_proj[:, cut] + query[:, cut]) * vec_row[:, cut]
             part = term if part is None else part + term
-        high = part.astype(BF16)
-        low = (part - high.astype(F32)).astype(BF16)
-        split = jnp.concatenate([jnp.concatenate([high, low], 1), tail], 0)
-        scores = mm_nt(ones, split)
-        if shift_by_max:
-            scores = jnp.where(frame_ok, scores, -1000000000.0)
-            scores = scores - jnp.max(scores, -1, keepdims=True)
+        scores = jnp.sum(part, -1, keepdims=True)
+        scores = jnp.where(frame_ok, scores, -1000000000.0)
+        scores = scores - jnp.max(scores, 0, keepdims=True)
         expf = jnp.where(frame_ok, jnp.exp(scores), 0.0)
-        rinv = 1.0 / jnp.sum(expf, -1, keepdims=True)
-        w_rows[at, :] = expf * rinv
-        return cell1, cell2, hid1, hid2, expf.astype(BF16), rinv
+        rinv = 1.0 / jnp.sum(expf, 0, keepdims=True)
+        w_cols[...] = jnp.where(lane == i, expf * rinv, w_cols[...])
+        ctx_low = jnp.concatenate(
+            [
+                jnp.sum(expf * key_low[:, j * 128 : (j + 1) * 128], 0, keepdims=True)
+                for j in range(key_low.shape[1] // 128)
+            ],
+            1,
+        )
+        return cell1, cell2, hid1, hid2, ctx_low * rinv
 
     zero = jnp.zeros((1, cells), F32)
     wide = jnp.zeros((1, 4 * cells), F32)
-    start = (zero, zero, wide, wide, jnp.zeros((1, pad_time), BF16), jnp.ones((1, 1), F32))
-    bound = jnp.sum(jnp.abs(vec_row))
-
-    @pl.when(bound <= SAFE_SCORE)
-    def _():
-        lax.fori_loop(0, steps, functools.partial(forward_step, False), start)
-
-    @pl.when(bound > SAFE_SCORE)
-    def _():
-        lax.fori_loop(0, steps, functools.partial(forward_step, True), start)
-
-    w_low = w_rows[...].astype(BF16)
+    lax.fori_loop(0, steps, forward_step, (zero, zero, wide, wide, wide))
+
+    w_low = jnp.transpose(w_cols[...])[:steps].astype(BF16)
     ctx = mm(w_low, key[...]).astype(BF16)
     s2_low = s2_rows[...].astype(BF16)
-    logits = mm(s2_low, w_out[:cells, :]) + mm(ctx, w_out[cells:, :]) + b_out[...].astype(F32)
+    logits = mm_nt(s2_low, w_out[:, :cells]) + mm_nt(ctx, w_out[:, cells:]) + b_out[...].astype(F32)
     top = jnp.max(logits, -1, keepdims=True)
     log_total = top + jnp.log(jnp.sum(jnp.exp(logits - top), -1, keepdims=True))
     target = target_onehot[...]
@@ -220,17 +418,20 @@
     scale = jnp.where(alive, 1.0 / text, 0.0)
     logit_grad = (scale * (jnp.exp(logits - log_total) - target)).astype(BF16)
     logit_grad_out[...] = logit_grad
-    feat_rows[...] = mm_nt(logit_grad, w_out[...])
-    dw_rows[...] = mm_nt(feat_rows[:, cells:].astype(BF16), key[...])
+    feat_rows[...] = mm(logit_grad, w_out[...])
+    dw_cols[...] = jnp.zeros_like(dw_cols)
+    dw_cols[:, :steps] = mm_nt(key[...], feat_rows[:, cells:].astype(BF16))
     acts[steps:, :] = jnp.zeros((acts.shape[0] - steps, acts.shape[1]), BF16)
     acts[:steps, :embed] = emb
     acts[:steps, embed : embed + 2 * units] = ctx
     acts[:steps, embed + 2 * units : embed + 2 * units + cells] = s1_rows[...].astype(BF16)
     acts[:steps, embed + 2 * units + cells :] = s2_low
+    if gather is not None:
+        gather.finish(steps)
 
 
 def speller_forward(
-    lengths, text_lens, mine, other, prev_onehot, target_onehot,
+    dims, lengths, text_lens, pairs, states, mine, other, prev_onehot, target_onehot,
     w_lin, w_lhid, b_low, w_uin, w_uhid, b_up, w_key, w_query, vec, w_out, b_out, table,
 ):
     time_len, units = mine.shape
@@ -238,39 +439,50 @@
     cells = w_lhid.shape[0]
     att = w_key.shape[1]
     embed = table.shape[1]
-    pad_time = -(-time_len // 256) * 256
     pad_steps = -(-steps // 16) * 16
     vmem = pl.BlockSpec(memory_space=pltpu.VMEM)
     smem = pl.BlockSpec(memory_space=pltpu.SMEM)
     shape = jax.ShapeDtypeStruct
-    outs = (
+    outs = [
         shape((1, 1), F32),
         shape((pad_steps, embed + 2 * units + 2 * cells), BF16),
-        shape((pad_time, 2 * units), BF16),
+        shape((time_len, 2 * units), BF16),
         shape((time_len, att), F32),
-        shape((4 * cells, pad_time), BF16),
+        shape((time_len, 4 * cells), F32),
         shape((steps, 6 * cells), F32),
         shape((steps, 6 * cells), F32),
         shape((steps, att), F32),
-        shape((steps, pad_time), F32),
-        shape((steps, w_out.shape[0]), F32),
-        shape((steps, pad_time), F32),
+        shape((time_len, -(-steps // 128) * 128), F32),
+        shape((steps, w_out.shape[1]), F32),
+        shape((time_len, -(-steps // 128) * 128), F32),
         shape((steps, vocab), BF16),
-    )
+    ]
+    out_specs = [vmem] * len(outs)
+    scratch = [
+        pltpu.VMEM((steps, 4 * cells), F32),
+        pltpu.VMEM((steps, cells), F32),
+        pltpu.VMEM((steps, cells), F32),
+    ]
+    params = dict(vmem_limit_bytes=VMEM_BYTES)
+    if dims is not None:
+        chips = dims[0] * dims[1] * dims[2]
+        dma = pltpu.SemaphoreType.DMA
+        outs += [shape((2, chips, *pairs.shape[1:]), BF16), shape((chips, *states.shape), BF16)]
+        out_specs += [pl.BlockSpec(memory_space=pl.ANY)] * 2
+        scratch += [pltpu.VMEM(pairs.shape[1:], BF16), dma((3,))]
+        scratch += [Gather.semaphores(dims, ROW_CHUNKS)] * 2
+        scratch += [Gather.semaphores(dims, FRAME_CHUNKS)] * 2
+        scratch += [dma((len(FRAME_CHUNKS),))] * 2
+        params.update(collective_id=2, has_side_effects=True)
     return pl.pallas_call(
-        speller_forward_kernel,
+        functools.partial(speller_forward_kernel, dims),
         out_shape=outs,
-        in_specs=[smem] * 2 + [vmem] * 16,
-        out_specs=(vmem,) * len(outs),
-        scratch_shapes=[
-            pltpu.VMEM((pad_time, 4 * cells), BF16),
-            pltpu.VMEM((steps, 4 * cells), F32),
-            pltpu.VMEM((steps, cells), F32),
-            pltpu.VMEM((steps, cells), F32),
-        ],
-        compiler_params=pltpu.CompilerParams(vmem_limit_bytes=VMEM_BYTES),
+        in_specs=[smem] * 2 + [pl.BlockSpec(memory_space=pl.ANY)] + [vmem] * 17,
+        out_specs=out_specs,
+        scratch_shapes=scratch,
+        compiler_params=pltpu.CompilerParams(**params),
     )(
-        lengths, text_lens, mine, other, prev_onehot, target_onehot,
+        lengths, text_lens, pairs, states, mine, other, prev_onehot, target_onehot,
         w_lin, w_lhid, b_low, w_uin, w_uhid, b_up, w_key, w_query, vec, w_out, b_out, table,
     )
 
@@ -287,14 +499,13 @@
 
 def speller_backward_kernel(
     w_lin, w_lhid, w_uin, w_uhid, w_key, w_query, vec, prev_onehot,
-    acts, key, keys_proj, key_low_t, fact1, fact2, q_rows, w_rows, feat_rows, dw_rows, logit_grad,
+    acts, key, keys_proj, key_low, fact1, fact2, q_rows, w_cols, feat_rows, dw_cols, logit_grad,
     grad_mine, grad_other, dp1_out, dp2_out, pack,
-    dp1_rows, dp2_rows, dq_rows, m_scr, keys_acc, vec_acc, small,
+    dp1_rows, dp2_rows, dq_rows, keys_acc, vec_acc, small, t_lhid, t_uin, t_uhid, t_query,
 ):
     role = lax.axis_index("role")
     time_len, att = keys_proj.shape
     steps, vocab = logit_grad.shape
-    pad_time = key.shape[0]
     units = key.shape[1] // 2
     cells = w_lhid.shape[0]
     embed = acts.shape[1] - 2 * units - 2 * cells
@@ -303,39 +514,49 @@
     wide = jnp.zeros((1, 4 * cells), BF16)
     keys_acc[...] = jnp.zeros_like(keys_acc)
     vec_acc[...] = jnp.zeros_like(vec_acc)
-    m_scr[time_len:, :] = jnp.zeros((pad_time - time_len, m_scr.shape[1]), BF16)
+    t_lhid[...] = w_lhid[...].T
+    t_uin[...] = w_uin[...].T
+    t_uhid[...] = w_uhid[...].T
+    t_query[...] = w_query[...].T
+    lane = lax.broadcasted_iota(jnp.int32, w_cols.shape, 1)
 
     def backward_step(s, carry):
-        dp1, back1, back2, dcell1, dcell2 = carry
+        dp1, dp2, dcell1, dcell2 = carry
         i = steps - 1 - s
         at = pl.ds(i, 1)
         query = q_rows[at, :]
-        weights = w_rows[at, :]
-        dweights = dw_rows[at, :] + mm(dp1, key_low_t[...])
-        dscore = weights * (dweights - jnp.sum(weights * dweights, -1, keepdims=True))
-        dcol = jnp.transpose(jnp.broadcast_to(dscore, (8, pad_time)))[:time_len, :1]
+        dp1_row = dp1.astype(F32)
+        here = lane == i
+        part = jnp.where(here, dw_cols[...], 0.0)
+        for j in range(key_low.shape[1] // 128):
+            cut = slice(j * 128, (j + 1) * 128)
+            part = part + dp1_row[:, cut] * key_low[:, cut]
+        dweights = jnp.sum(part, -1, keepdims=True)
+        weights = jnp.sum(jnp.where(here, w_cols[...], 0.0), -1, keepdims=True)
+        back2 = mm(dp2, t_uhid[...])
+        back1 = mm(dp1, t_lhid[...])
+        shared = weights * dweights
+        dscore = shared - weights * jnp.sum(shared, 0, keepdims=True)
+        sums = []
         for j in range(query.shape[1] // 128):
             cut = slice(j * 128, (j + 1) * 128)
             energy = jnp.tanh(keys_proj[:, cut] + query[:, cut])
-            slope = 1.0 - energy * energy
-            m_scr[:time_len, cut] = slope.astype(BF16)
-            keys_acc[:, cut] += dcol * slope
-            vec_acc[:, cut] += jnp.sum((dcol * energy).reshape(time_len // 8, 8, 128), 0)
-        dquery = (mm(dscore.astype(BF16), m_scr[...]) * vec_row).astype(BF16)
+            moved = dscore * (1.0 - energy * energy)
+            keys_acc[:, cut] += moved
+            sums.append(jnp.sum(moved, 0, keepdims=True))
+            vec_acc[:, cut] += jnp.sum((dscore * energy).reshape(time_len // 8, 8, 128), 0)
+        dquery = (jnp.concatenate(sums, 1) * vec_row).astype(BF16)
         dq_rows[at, :] = dquery.astype(F32)
-        ds2 = back2 + feat_rows[at, :cells] + mm_nt(dquery, w_query[...])
+        ds2 = back2 + feat_rows[at, :cells] + mm(dquery, t_query[...])
         pre2, dcell2 = cell_backward(fact2[at, :], ds2, dcell2)
         dp2_rows[at, :] = pre2
         dp2 = pre2.astype(BF16)
-        ds1 = back1 + mm_nt(dp2, w_uin[...])
-        back2 = mm_nt(dp2, w_uhid[...])
+        ds1 = back1 + mm(dp2, t_uin[...])
         pre1, dcell1 = cell_backward(fact1[at, :], ds1, dcell1)
         dp1_rows[at, :] = pre1
-        dp1 = pre1.astype(BF16)
-        back1 = mm_nt(dp1, w_lhid[...])
-        return dp1, back1, back2, dcell1, dcell2
-
-    lax.fori_loop(0, steps, backward_step, (wide, zero, zero, zero, zero))
+        return pre1.astype(BF16), dp2, dcell1, dcell2
+
+    lax.fori_loop(0, steps, backward_step, (wide, wide, zero, zero))
 
     dp1 = dp1_rows[...].astype(BF16)
     dp2 = dp2_rows[...].astype(BF16)
@@ -348,8 +569,8 @@
     next_dp1 = shift_up(dp1.astype(F32)).astype(BF16)
     ctx_grad = (feat_rows[:, cells:] + mm_nt(next_dp1, w_lin[embed:, :])).astype(BF16)
     keys_grad = (keys_acc[...] * vec_row).astype(BF16)
-    w_low = w_rows[...].astype(BF16)
-    key_grad = mm_nt(keys_grad, w_key[...]) + mm_tn(w_low, ctx_grad)[:time_len, :]
+    w_low = w_cols[...].astype(BF16)[:, :steps]
+    key_grad = mm_nt(keys_grad, w_key[...]) + mm(w_low, ctx_grad)
     key_grad = key_grad.astype(BF16)
     grad_mine[...] = jnp.where(role == 0, key_grad[:, :units], key_grad[:, units:])
     grad_other[...] = jnp.where(role == 0, key_grad[:, units:], key_grad[:, :units])
@@ -357,12 +578,14 @@
     s2 = acts[:steps, embed + 2 * units + cells :]
     wide = pack.shape[1]
     deep = 2 * units * att // wide
-    g_key = mm_tn(key[:time_len, :], keys_grad)
+    g_key = mm_tn(key[...], keys_grad)
     g_query = mm_tn(s2, dq)
     for k in range(wide // att):
         cut = slice(k * att, (k + 1) * att)
-        pack[:deep, cut] = g_key[k * deep : (k + 1) * deep].astype(BF16)
-        pack[deep : 2 * deep, cut] = g_query[k * deep : (k + 1) * deep].astype(BF16)
+        first = 2 * SMALL
+        pack[first : first + deep, cut] = g_key[k * deep : (k + 1) * deep].astype(BF16)
+        first += deep
+        pack[first : first + deep, cut] = g_query[k * deep : (k + 1) * deep].astype(BF16)
     emb_grad = mm_nt(dp1, w_lin[:embed, :])
     hot = prev_onehot[...]
     total = None
@@ -384,58 +607,61 @@
         small[2 + k : 3 + k, base : base + cells] = low_bias[:, k * cells : (k + 1) * cells]
         small[6 + k : 7 + k, base : base + cells] = up_bias[:, k * cells : (k + 1) * cells]
     high = small[...].astype(BF16)
-    rows = small.shape[0]
-    pack[2 * deep : 2 * deep + rows, :] = high
-    pack[2 * deep + rows :, :] = (small[...] - high.astype(F32)).astype(BF16)
+    pack[:SMALL, :] = high
+    pack[SMALL : 2 * SMALL, :] = (small[...] - high.astype(F32)).astype(BF16)
 
 
 def speller_backward(
     w_lin, w_lhid, w_uin, w_uhid, w_key, w_query, vec, prev_onehot,
-    acts, key, keys_proj, key_low_t, fact1, fact2, q_rows, w_rows, feat_rows, dw_rows, logit_grad,
+    acts, key, keys_proj, key_low, fact1, fact2, q_rows, w_cols, feat_rows, dw_cols, logit_grad,
 ):
     time_len, att = keys_proj.shape
     steps, vocab = logit_grad.shape
-    pad_time = key.shape[0]
     units = key.shape[1] // 2
     cells = w_lhid.shape[0]
     pad_steps = acts.shape[0]
     vmem = pl.BlockSpec(memory_space=pltpu.VMEM)
     shape = jax.ShapeDtypeStruct
-    outs = (
+    outs = [
         shape((time_len, units), BF16),
         shape((time_len, units), BF16),
         shape((pad_steps, 4 * cells), BF16),
         shape((pad_steps, 4 * cells), BF16),
         shape(((2 * units + cells) * att // (4 * cells) + 2 * SMALL, 4 * cells), BF16),
-    )
+    ]
+    out_specs = [vmem] * 5
+    scratch = [
+        pltpu.VMEM((steps, 4 * cells), F32),
+        pltpu.VMEM((steps, 4 * cells), F32),
+        pltpu.VMEM((steps, att), F32),
+        pltpu.VMEM((time_len, att), F32),
+        pltpu.VMEM((8, att), F32),
+        pltpu.VMEM((SMALL, 4 * cells), F32),
+        pltpu.VMEM((4 * cells, cells), BF16),
+        pltpu.VMEM((4 * cells, cells), BF16),
+        pltpu.VMEM((4 * cells, cells), BF16),
+        pltpu.VMEM((att, cells), BF16),
+    ]
     return pl.pallas_call(
         speller_backward_kernel,
         out_shape=outs,
         in_specs=[vmem] * 19,
-        out_specs=(vmem,) * len(outs),
-        scratch_shapes=[
-            pltpu.VMEM((steps, 4 * cells), F32),
-            pltpu.VMEM((steps, 4 * cells), F32),
-            pltpu.VMEM((steps, att), F32),
-            pltpu.VMEM((pad_time, att), BF16),
-            pltpu.VMEM((time_len, att), F32),
-            pltpu.VMEM((8, att), F32),
-            pltpu.VMEM((SMALL, 4 * cells), F32),
-        ],
+        out_specs=out_specs,
+        scratch_shapes=scratch,
         compiler_params=pltpu.CompilerParams(vmem_limit_bytes=VMEM_BYTES),
     )(
         w_lin, w_lhid, w_uin, w_uhid, w_key, w_query, vec, prev_onehot,
-        acts, key, keys_proj, key_low_t, fact1, fact2, q_rows, w_rows, feat_rows, dw_rows, logit_grad,
-    )
-
-
-def unpack(pack, units, cells, att, vocab, embed):
-    wide = pack.shape[1]
-    deep = 2 * units * att // wide
-    unfold = lambda part: part.reshape(deep, wide // att, att).swapaxes(0, 1).reshape(-1, att)
-    g_key = unfold(pack[:deep].astype(F32))
-    g_query = unfold(pack[deep : 2 * deep].astype(F32))
-    small = pack[2 * deep : 2 * deep + SMALL].astype(F32) + pack[2 * deep + SMALL :].astype(F32)
+        acts, key, keys_proj, key_low, fact1, fact2, q_rows, w_cols, feat_rows, dw_cols, logit_grad,
+    )
+
+
+def unfold(folded, width):
+    deep = folded.shape[0]
+    return folded.reshape(deep, -1, width).swapaxes(0, 1).reshape(-1, width)
+
+
+def unpack(small, units, cells, att, vocab, embed):
+    small = small[:SMALL].astype(F32) + small[SMALL:].astype(F32)
     base = cells + 2 * units
     g_out = small[:vocab, :base].T
     g_table = small[:vocab, base : base + embed]
@@ -444,7 +670,7 @@
     up_bias = small[6:10, base : base + cells].reshape(-1)
     g_vec = small[0, base : base + att]
     g_obias = small[1, base : base + vocab]
-    return low_bias, up_bias, g_key, g_query, g_vec, g_out, g_obias, g_table
+    return low_bias, up_bias, g_vec, g_out, g_obias, g_table
 
 
 def backward_steps(role, lengths, factors, grad_out, w_rec, grad_pre, first_step, count, carry):
@@ -504,92 +730,19 @@
 STREAMS = ((0, 3), (3, 5), (5, 6))
 
 
-def remote(src, dst, send, recv, device):
-    return pltpu.make_async_remote_copy(
-        src_ref=src, dst_ref=dst, send_sem=send, recv_sem=recv,
-        device_id=device, device_id_type=pl.DeviceIdType.MESH,
-    )
-
-
-def start(copies):
-    for copy in copies:
-        copy.start()
-
-
-def wait(copies):
-    for copy in copies:
-        copy.wait()
-
-
-class Gather:
-    def __init__(self, dims, me, view, chunks, sems):
-        self.dims, self.view, self.chunks = dims, view, chunks
-        self.role, self.z, self.y, self.x = me
-        self.send, self.recv = sems
-
-    def device(self, z, y, x):
-        _, ny, nx = self.dims
-        return (self.role, (z * ny + y) * nx + x)
-
-    def copies(self, k, which, spans, others, base):
-        out = []
-        for device in others:
-            for span in spans:
-                ref = self.view(which, k, *span)
-                out.append(
-                    remote(ref, ref, self.send.at[k, base], self.recv.at[k, base], device)
-                )
-                base += 1
-        return out
-
-    def along_x(self):
-        nx = self.dims[2]
-        return [self.device(self.z, self.y, (self.x + j) % nx) for j in range(1, nx)]
-
-    def along_y(self):
-        ny = self.dims[1]
-        return [self.device(self.z, (self.y + j) % ny, self.x) for j in range(1, ny)]
-
-    def first(self, k):
-        nz, ny, nx = self.dims
-        slot = (self.y * nx + self.x) * nz + self.z
-        others = [self.device((self.z + j) % nz, self.y, self.x) for j in range(1, nz)]
-        return self.copies(k, None, [(slot, 1)], others, 0)
-
-    def second(self, k):
-        nz, ny, nx = self.dims
-        column = ((self.y * nx + self.x) * nz, nz)
-        base = nz - 1
-        to_x = self.copies(k, 0, [column], self.along_x(), base)
-        return to_x + self.copies(k, 1, [column], self.along_y(), base + nx - 1)
-
-    def third(self, k):
-        nz, ny, nx = self.dims
-        base = nz - 1 + nx - 1 + ny - 1
-        to_y = self.copies(k, 0, [(self.y * nx * nz, nx * nz)], self.along_y(), base)
-        spans = [((b * nx + self.x) * nz, nz) for b in range(ny)]
-        return to_y + self.copies(k, 1, spans, self.along_x(), base + ny - 1)
-
-    @staticmethod
-    def semaphores(dims, chunks):
-        nz, ny, nx = dims
-        count = nz - 1 + 2 * (nx - 1) + 2 * (ny - 1) + (nx - 1) * (ny - 1)
-        return pltpu.SemaphoreType.DMA((len(chunks), count))
-
-
-SP_CHUNKS = ((0, 352), (352, 352), (704, 320), (1024, 320))
+SP_CHUNKS = ((320, 352), (672, 352), (1024, 320), (0, 320))
 LI_CHUNKS = ((0, 352), (352, 320))
 
 
 def exchange_kernel(
     dims,
     lengths, factors, grad_mine, grad_other, w_in, w_rec, dp1, dp2, pack, acts_all, pairs_all, rows_all,
-    frames_out, li_out, sp_out,
+    frames_out, li_out, sp_out, kq_out,
     grad_pre, grad_out, acts_buf, pairs_buf, rows_buf, dp_pair, got, got_t, prod, column,
     li_send, li_got, li_rows, li_acc, li_all, fr_send, fr_got, weave,
     pk_pair, pk_x, pk_xsum, pk_y, pk_ysum, pk_z,
     local_sem, chip_send, chip_recv, aa_send, aa_recv, li_aa_send, li_aa_recv,
-    sp_send, sp_recv, li_ag_send, li_ag_recv, pk_send, pk_recv,
+    sp_send, sp_recv, li_ag_send, li_ag_recv, pk_send, pk_recv, far_grad,
 ):
     nz, ny, nx = dims
     chips = nz * ny * nx
@@ -623,15 +776,26 @@
         acts_buf, local_sem.at[0],
     )
     load_acts.start()
-    load_rows = pltpu.make_async_copy(rows_all, rows_buf, local_sem.at[1])
-    load_rows.start()
+    load_rows = [
+        pltpu.make_async_copy(
+            rows_all.at[c, pl.ds(u * time_len, time_len)],
+            rows_buf.at[pl.ds((u * chips + c) * time_len, time_len), pl.ds(0, units)],
+            local_sem.at[5 + c * utts + u],
+        )
+        for c in range(chips)
+        for u in range(utts)
+    ]
+    rows_buf[:, units:] = jnp.ones((rows_buf.shape[0], rows_buf.shape[1] - units), BF16)
+    start(load_rows)
     load_pairs = pltpu.make_async_copy(pairs_all, pairs_buf, local_sem.at[4])
     load_pairs.start()
     dp_pair[role] = jnp.where(role == 0, dp1[...], dp2[...])
     dp_pair[2] = jnp.where(role == 0, dp2[...], dp1[...])
     grad_out[role] = grad_mine[...].astype(F32)
-    grad_out[1 - role] = grad_other[...].astype(F32)
     pl.semaphore_wait(barrier, chips)
+    last = chip_send.shape[0] - 1
+    crossing = remote(grad_other, far_grad, chip_send.at[last], chip_recv.at[last], twin)
+    crossing.start()
 
     to_twin = remote(dp_pair.at[2], dp_pair.at[role], chip_send.at[0], chip_recv.at[0], twin)
     to_twin.start()
@@ -657,13 +821,11 @@
     )
     own_block.start()
 
-    plain = pack.shape[0] - 2 * SMALL
-
     def rounded(total):
-        value = total[plain : plain + SMALL] + total[plain + SMALL :]
+        value = total[:SMALL] + total[SMALL : 2 * SMALL]
         high = value.astype(BF16)
         low = (value - high.astype(F32)).astype(BF16)
-        return jnp.concatenate([total[:plain].astype(BF16), high, low], 0)
+        return jnp.concatenate([high, low, total[2 * SMALL :].astype(BF16)], 0)
 
     chip_at = lambda a, b, c: (role, (a * ny + b) * nx + c)
     x_other, y_other = (x + 1) % nx, (y + 1) % ny
@@ -740,7 +902,7 @@
         total = pk_z[0].astype(F32)
         for j in range(1, nz):
             total = total + pk_z[j].astype(F32)
-        column[column.shape[0] - total.shape[0] :, :] = rounded(total)
+        column[: total.shape[0], :] = rounded(total)
 
     def view_sp(which, k, first, count):
         rows = SP_CHUNKS[k]
@@ -802,6 +964,8 @@
         one = stream(n)
         lax.fori_loop(1, chips, lambda k, _: (one(k).wait(), 0)[1], 0)
 
+    crossing.wait()
+    grad_out[1 - role] = far_grad[...].astype(F32)
     zero = jnp.zeros((8, units), F32)
     carry = (zero, zero)
 
@@ -823,7 +987,6 @@
     got_t[0] = jnp.transpose(both).astype(BF16)
     got_t[1] = jnp.transpose(rolled).astype(BF16)
     groups = acts_buf.shape[1] // 256
-    span = groups * 256
     for g in range(groups):
         cut = slice(g * 256, (g + 1) * 256)
         if g == 0:
@@ -832,10 +995,9 @@
             left = got_t[1 - role]
         else:
             left = got_t[1]
-        to = (g + groups - 1) % groups * 256
-        prod[:, to : to + 256] = mm(left, acts_buf[:, cut])
-    column[:span, :] = jnp.transpose(prod[...]).astype(BF16)
-    column[span:, :] = jnp.zeros((column.shape[0] - span, 128), BF16)
+        prod[:, cut] = mm(left, acts_buf[:, cut])
+    column[2 * SMALL :, :] = jnp.transpose(prod[...]).astype(BF16)
+    column[: 2 * SMALL, :] = jnp.zeros((2 * SMALL, 128), BF16)
 
     def place(first, count):
         copy = pltpu.make_async_copy(
@@ -845,14 +1007,14 @@
         copy.start()
         copy.wait()
 
-    tail_first, tail_count = SP_CHUNKS[-1]
-    place(0, tail_first)
+    head = SP_CHUNKS[-1][1]
+    place(head, column.shape[0] - head)
     for k in range(len(SP_CHUNKS) - 1):
         start(sp.first(k))
 
     carry = run(2, carry)
     pl.when(role == 1)(pack_after_z)
-    place(tail_first, tail_count)
+    place(0, head)
     start(sp.first(len(SP_CHUNKS) - 1))
     start_stream(0)
     far = jnp.where(role == 0, half_time, 0)
@@ -894,17 +1056,16 @@
             frames_out[u, :, j * 128 : (j + 1) * 128] = weave[...]
 
     li_got[dp] = li_send[slot]
-    load_rows.wait()
+    wait(load_rows)
     load_pairs.wait()
     for n in range(len(STREAMS)):
         wait_stream(n)
 
     def spread(c, _):
         value = li_got[c].astype(F32)
-        base = pl.multiple_of(c * 2 * time_len, 16)
-        li_rows[pl.ds(base, time_len), :] = value.astype(BF16)
-        base = pl.multiple_of(c * 2 * time_len + time_len, 16)
-        li_rows[pl.ds(base, time_len), :] = pltpu.roll(value, 64, 1).astype(BF16)
+        for u, part in enumerate((value, pltpu.roll(value, 64, 1))):
+            base = pl.multiple_of((u * chips + slot_of(c)) * time_len, 16)
+            li_rows[pl.ds(base, time_len), :] = part.astype(BF16)
         return 0
 
     lax.fori_loop(0, chips, spread, 0)
@@ -960,6 +1121,20 @@
     lax.fori_loop(0, width // 128, assemble, 0)
     for k in range(len(SP_CHUNKS)):
         wait(sp_last(k))
+    att = kq_out.shape[2]
+    folds = sp_out.shape[2] // att
+    deep = att // folds
+    unfold = [
+        pltpu.make_async_copy(
+            sp_out.at[1, pl.ds(2 * SMALL + which * deep, deep), pl.ds(k * att, att)],
+            kq_out.at[which, pl.ds(k * deep, deep)],
+            local_sem.at[5 + which * folds + k],
+        )
+        for which in range(2)
+        for k in range(folds)
+    ]
+    start(unfold)
+    wait(unfold)
 
 
 def exchange(
@@ -975,7 +1150,7 @@
     deep = sum(rows for _, rows in SP_CHUNKS)
     nz, ny, _ = dims
     packed = pack.shape[0]
-    total = pairs_all.shape[1] + rows_all.shape[1]
+    total = pairs_all.shape[1] + units + 64
     feat = w_in.shape[0] // 2
     half_time = time_len // 2
     vmem = pl.BlockSpec(memory_space=pltpu.VMEM)
@@ -990,15 +1165,16 @@
             shape((utts, time_len, feat), F32),
             shape((total, width), BF16),
             shape((2, deep, wide), BF16),
+            shape((2, cells, cells), BF16),
         ),
         in_specs=[pl.BlockSpec(memory_space=pltpu.SMEM)] + [vmem] * 8 + [anywhere] * 3,
-        out_specs=(vmem, vmem, anywhere),
+        out_specs=(vmem, vmem, anywhere, vmem),
         scratch_shapes=[
             pltpu.VMEM((utts, time_len, width), F32),
             pltpu.VMEM((utts, time_len, units), F32),
             pltpu.VMEM((acts_all.shape[0], span), BF16),
             pltpu.VMEM(pairs_all.shape, BF16),
-            pltpu.VMEM(rows_all.shape, BF16),
+            pltpu.VMEM((chips * utts * time_len, units + 64), BF16),
             pltpu.VMEM((3, pads, wide), BF16),
             pltpu.VMEM((chips, 2, pads, 128), BF16),
             pltpu.VMEM((2, 128, chips * 2 * pads), BF16),
@@ -1018,9 +1194,9 @@
             pltpu.VMEM((packed, nz * 128), BF16),
             pltpu.VMEM((packed, nz * 128), BF16),
             pltpu.VMEM((nz, packed, 128), BF16),
-            dma((5,)),
-            dma((2 + len(SP_CHUNKS),)),
-            dma((2 + len(SP_CHUNKS),)),
+            dma((5 + chips * utts,)),
+            dma((3 + len(SP_CHUNKS),)),
+            dma((3 + len(SP_CHUNKS),)),
             dma((chips - 1,)),
             dma((chips - 1,)),
             dma((len(STREAMS), chips - 1)),
@@ -1031,12 +1207,10 @@
             li_sems,
             dma((1 + ny + nz,)),
             dma((1 + ny + nz,)),
+            pltpu.VMEM(grad_other.shape, BF16),
         ],
         compiler_params=pltpu.CompilerParams(
             vmem_limit_bytes=VMEM_BYTES, collective_id=0, has_side_effects=True
-        ),
-        cost_estimate=pl.CostEstimate(
-            flops=100_000_000_000, bytes_accessed=100_000_000, transcendentals=0
         ),
     )(
         lengths, factors, grad_mine, grad_other, w_in, w_rec, dp1, dp2, pack,
@@ -1074,8 +1248,25 @@
     cells = lower_hidden.shape[0]
     vocab, embed = char_table.shape
     pairs = frames.reshape(utts, time_len, 2 * feat)
-    rows, factors, mine, other = listen_forward(step_lengths, pairs, w_in, w_rec, listen_bias)
-    other = lax.ppermute(other, "role", swap)
+    fits = (
+        chips % 4 == 0
+        and 4 * cells == 128 * chips
+        and 4 * units == 64 * chips
+        and embed == 256
+        and cells == 2 * units
+        and time_len == SEGMENT * STREAMS[-1][1]
+        and embed + 2 * units + cells + 2 * SMALL == sum(rows for _, rows in SP_CHUNKS)
+        and embed + 2 * SMALL == SP_CHUNKS[-1][1]
+        and time_len == sum(count for _, count in FRAME_CHUNKS)
+        and utts * time_len == sum(count for _, count in ROW_CHUNKS)
+        and 2 * feat + units + 64 == 2 * sum(rows for _, rows in LI_CHUNKS)
+    )
+    dims = (chips // 4, 2, 2) if fits else None
+    rows, factors, mine, other = listen_forward(
+        dims, step_lengths, pairs, w_in, w_rec, listen_bias
+    )
+    if not fits:
+        other = lax.ppermute(other, "role", swap)
     chars = characters[0, 0]
     previous = jnp.concatenate([jnp.zeros((1,), jnp.int32), chars[:-1]])
     ids = jnp.arange(vocab)[None, :]
@@ -1083,54 +1274,46 @@
     target_onehot = (chars[:, None] == ids).astype(F32)
     vec = score_vector[None]
     loss, acts, key, *kept = speller_forward(
-        step_lengths, char_lengths, mine, other, prev_onehot, target_onehot,
+        dims, step_lengths, char_lengths, pairs, rows, mine, other, prev_onehot, target_onehot,
         lower_input, lower_hidden, lower_bias[None], upper_input, upper_hidden, upper_bias[None],
-        key_proj, query_proj, vec, output_proj, output_bias[None], char_table,
-    )
+        key_proj, query_proj, vec, output_proj.T, output_bias[None], char_table,
+    )
+    if fits:
+        *kept, pairs_all, rows_all = kept
     grad_mine, grad_other, dp1, dp2, pack = speller_backward(
         lower_input, lower_hidden, upper_input, upper_hidden, key_proj, query_proj, vec,
         prev_onehot, acts, key, *kept,
     )
-    grad_other = lax.ppermute(grad_other, "role", swap)
-    fits = (
-        chips % 4 == 0
-        and 4 * cells == 128 * chips
-        and 4 * units == 64 * chips
-        and embed == 256
-        and cells == 2 * units
-        and time_len == SEGMENT * STREAMS[-1][1]
-        and cells + 2 * units == SP_CHUNKS[-1][0]
-        and pack.shape[0] == SP_CHUNKS[-1][1]
-        and 2 * feat + units + 64 == 2 * sum(rows for _, rows in LI_CHUNKS)
-    )
     if fits:
-        own_pairs = lax.dynamic_index_in_dim(pairs, lax.axis_index("role"), 0, keepdims=False)
-        pairs_all = lax.all_gather(own_pairs, ("dp", "role"), tiled=True)
-        rows_all = lax.all_gather(rows, "dp", tiled=True)
+        pairs_all = pairs_all.reshape(chips * utts * time_len, 2 * feat)
         acts_all = lax.all_gather(acts, ("dp", "role"), tiled=True)
-        frame_grad, li, sp = exchange(
-            (chips // 4, 2, 2), step_lengths, factors, grad_mine, grad_other, w_in, w_rec,
+        frame_grad, li, sp, kq = exchange(
+            dims, step_lengths, factors, grad_mine, grad_other, w_in, w_rec,
             dp1, dp2, pack, acts_all, pairs_all, rows_all,
         )
         width = 2 * feat
         sum_in, sum_rec = li[:width].astype(F32), li[width : width + units].astype(F32)
         sum_bias = li[width + units : width + units + 1].astype(F32)
-        low, high = 2 * units, 2 * units + cells
-        lower = (
-            jnp.concatenate([sp[0, high : high + embed], sp[0, :low]], 0).astype(F32),
-            sp[0, low:high].astype(F32),
+        first = 2 * SMALL
+        low, high = first + embed, first + embed + 2 * units
+        lower = (sp[0, first:high].astype(F32), sp[0, high:].astype(F32))
+        upper = (sp[1, low : low + cells].astype(F32), sp[1, low + cells :].astype(F32))
+        small = sp[1, :first]
+        g_key, g_query = kq[0].astype(F32), kq[1].astype(F32)
+    else:
+        grad_other = lax.ppermute(grad_other, "role", swap)
+        pack = lax.psum(pack.astype(F32), ("role", "dp"))
+        small = pack[: 2 * SMALL]
+        g_key, g_query = (
+            unfold(part, cells) for part in jnp.split(pack[2 * SMALL :], 2, axis=0)
         )
-        upper = (sp[1, :cells].astype(F32), sp[1, cells:high].astype(F32))
-        pack = sp[1, high:]
-    else:
-        pack = lax.psum(pack.astype(F32), ("role", "dp"))
         pre = listen_backward(step_lengths, factors, grad_mine, grad_other, w_rec)
         flat = pre.reshape(utts * time_len, 4 * units)
         sums = mm(jnp.concatenate([pairs.reshape(flat.shape[0], 2 * feat), rows], 1).T, flat)
         sums = lax.psum(sums, "dp")
         width = 2 * feat
         sum_in, sum_rec = sums[:width], sums[width : width + units]
-        sum_bias = sums[width + units : width + units + 1]
+        sum_bias = lax.psum(jnp.sum(flat.astype(F32), 0, keepdims=True), "dp")
         grad_pairs = mm(flat, w_in.T).reshape(utts, frame_len, feat)
         frame_grad = lax.psum_scatter(grad_pairs, "role", scatter_dimension=1, tiled=True)
         cuts = [embed, embed + 2 * units, embed + 2 * units + cells]
@@ -1143,8 +1326,8 @@
         )
         local = lax.psum(local, ("role", "dp"))
         lower, upper = local[:2], local[2:]
-    low_bias, up_bias, g_key, g_query, g_vec, g_out, g_obias, g_table = unpack(
-        pack, units, cells, key_proj.shape[1], vocab, embed
+    low_bias, up_bias, g_vec, g_out, g_obias, g_table = unpack(
+        small, units, cells, key_proj.shape[1], vocab, embed
     )
     return (
         loss, frame_grad, sum_in[None], sum_rec[None], sum_bias,

time: 539 us -> 454 us (0.84)
  Pallas kernels: 476 us -> 402 us
  local copies, waits for them, and re-layouts: 23.4 us -> 11.1 us
    pallas_call x1, Pallas kernels: 188 us -> 97.7 us  [speller_backward(): pl.pallas_call(speller_backward_kernel, out_shape=outs, in_specs=[vmem] *...]
    pallas_call x2, Pallas kernels: 154 us -> 174 us  [the longest x1 128 us: speller_forward(): pl.pallas_call(functools.partial(speller_forward_kernel, dims), out_shape...]
    reshape x4 -> x0, local copies, waits for them, and re-layouts: 10.9 us -> none  [unpack(): part.reshape(deep, wide // att, att).swapaxes(0, 1).reshape(-1, att)]
    convert_element_type x2 -> x3, other arithmetic: 12.2 us -> 13 us  [the longest x1 6.19 us: shards(): lower = (sp[0, first:high].astype(F32), sp[0, high:].astype(F32))]
  transfers between devices with their start and end apart: 5 -> 1, of which waited for: 1 -> 0; matrix products, arithmetic and copies ran while one was open for 1% -> 0% of each run, Pallas kernels for 55% -> 22%
where the time goes in v3:
time: 454 us; the launch traced here: 453 us
  Pallas kernels  402 us (89%)
  other arithmetic  23.2 us (5%)
  between operations  16.5 us (4%)
  local copies, waits for them, and re-layouts  11.1 us (2%)
    pallas_call x1, Pallas kernels, exchange(): pl.pallas_call(functools.partial(exchange_kernel, dims), out_shape=(shape...  131 us
    pallas_call x1, Pallas kernels, speller_forward(): pl.pallas_call(functools.partial(speller_forward_kernel, dims), out_shape...  128 us
    pallas_call x1, Pallas kernels, speller_backward(): pl.pallas_call(speller_backward_kernel, out_shape=outs, in_specs=[vmem] *...  97.7 us
    pallas_call x1, Pallas kernels, listen_forward(): pl.pallas_call(functools.partial(listen_forward_kernel, dims), out_shape=...  45.6 us
  transfers between devices with their start and end apart: 1, of which 0 were waited for; matrix products, arithmetic and copies ran while one was open for 0% of the time, Pallas kernels for 22%

profile of v3, /device:TPU:9, one launch (start us, length us, event | category | flops | bytes accessed | tf_op | source)
XLA Modules:
  0.0 453.2 jit_solution(11980436075206591061)
XLA Ops:
  7.9 0.7 slice_bitcast_fusion.4
  8.5 1.3 broadcast_in_dim.28.vec
  9.8 1.3 broadcast_in_dim.26.b_low
  11.1 1.3 broadcast_in_dim.27.b_up
  12.4 2.1 reshape.66.pairs
  14.6 1.4 fusion
  15.9 45.6 %shard_map.314 = (bf16[384,256]{1,0:T(8,128)(2,1)}, f32[2,192,1536]{2,1,0:T(8,128)}, bf16[192,256]{1,0:T(8,128)(2,1)}, bf16[192,256]{1,0:T(8,128)(2,1)}) custom-call(s32[2]{0:T(128)} %lengths.5, bf16[2,192,1024]{2,1,0:T(8,128)(2,1)} %reshape.66.pairs, bf16[1024,1024]{1,0:T(8,128)(2,1)} %bitcast.46, bf16[256,1024]{1,0:T(8,128)(2,1)} %bitcast.48, ...), custom_call_target="tpu_custom_call" | custom-call | tf_op jit(solution)/shard_map/pallas_call | solution.py:155
  61.6 127.9 %shard_map.315 = (f32[1,1]{1,0:T(1,128)}, bf16[80,1792]{1,0:T(8,128)(2,1)}, bf16[192,512]{1,0:T(8,128)(2,1)}, f32[192,512]{1,0:T(8,128)}, f32[192,2048]{1,0:T(8,...) custom-call(s32[2]{0:T(128)} %lengths.5, ...), custom_call_target="tpu_custom_call" | custom-call | tf_op jit(solution)/shard_map/pallas_call | solution.py:477
  189.5 97.7 %shard_map.316 = (bf16[192,256]{1,0:T(8,128)(2,1)}, bf16[192,256]{1,0:T(8,128)(2,1)}, bf16[80,2048]{1,0:T(8,128)(2,1)}, bf16[80,2048]{1,0:T(8,128)(2,1)}, bf16[320,2048]{1,0:T(8,128)(2,1)}) custom-call(bf16[768,2048]{1,0:T(8,128)(2,1)} %w_lin.3, bf16[512,2048]{1,0:T(8,128)(2,1)} %w_lhid.3, bf16[512,2048]{1,0:T(8,128)(2,1)} %w_uin.3, ...), custom_call_target="tpu_custom_call" | custom-call | tf_op jit(solution)/shard_map/pallas_call | solution.py:645
  287.2 131.1 %shard_map.317 = (f32[2,192,512]{2,1,0:T(8,128)}, bf16[1344,1024]{1,0:T(8,128)(2,1)}, bf16[2,1344,2048]{2,1,0:T(8,128)(2,1)}, bf16[2,512,512]{2,1,0:T(8,128)(2,1)}) custom-call(s32[2]{0:T(128)} %lengths.5, f32[2,192,1536]{2,1,0:T(8,128)} %get-tuple-element.48.factors, bf16[192,256]{1,0:T(8,128)(2,1)} %get-tuple-element.60.grad_mine, ...), custom_call_target="tpu_custom_call" | custom-call | tf_op jit(solution)/shard_map/pallas_call | solution.py:1162
  418.4 1.0 add_bitcast_fusion
  419.4 0.5 slice_bitcast_fusion.3
  419.9 0.6 slice.83
  420.5 0.6 slice.86
  421.1 0.7 slice_bitcast_fusion
  421.7 1.3 slice_convert_fusion
  423.0 2.1 bitcast_convert_fusion.7
  425.2 4.3 bitcast_convert_fusion.4
  429.5 6.2 %bitcast_convert_fusion = f32[768,2048]{1,0:T(8,128)} fusion(bf16[2,1344,2048]{2,1,0:T(8,128)(2,1)} %get-tuple-element.69), kind=kLoop, calls=%fused_computation | loop fusion | flops 1572864 | bytes 9437184 | tf_op jit(solution)/shard_map/convert_element_type | solution.py:1299
  435.7 5.2 %bitcast_convert_fusion.1 = (f32[512,2048]{1,0:T(8,128)}, f32[512,2048]{1,0:T(8,128)}, f32[512,2048]{1,0:T(8,128)}) fusion(bf16[2,1344,2048]{2,1,0:T(8,128)(2,1)S(1)} %copy-done), kind=kLoop, calls=%fused_computation.1 | loop fusion | flops 3145728 | bytes 18874368 | tf_op jit(solution)/shard_map/convert_element_type | solution.py:1300
  440.9 0.6 copy.37
  441.5 0.6 copy.36
  442.1 1.6 bitcast_convert_fusion.5
  444.3 0.9 copy.42
  (11 shorter events, 0.1 us)
Async XLA Ops:
  7.2 280.0 %all-gather.2.cloned.1.call-start = ((), (), s32[]{:S(2)}) async-start(), calls=%async_computation | async-start | bytes 9461760 | tf_op jit(solution)/shard_map/all_gather | solution.py:1289
  425.2 10.5 %copy-start = (bf16[2,1344,2048]{2,1,0:T(8,128)(2,1)S(1)}, bf16[2,1344,2048]{2,1,0:T(8,128)(2,1)}, u32[]{:S(2)}) copy-start(bf16[2,1344,2048]{2,1,0:T(8,128)(2,1)} %get-tuple-element.69) | copy-start | bytes 33030148
  435.7 6.4 %copy-start.1 = (bf16[2,512,512]{2,1,0:T(8,128)(2,1)S(1)}, bf16[2,512,512]{2,1,0:T(8,128)(2,1)}, u32[]{:S(2)}) copy-start(bf16[2,512,512]{2,1,0:T(8,128)(2,1)} %get-tuple-element.70) | copy-start | bytes 3145732
  440.9 3.4 copy-start.2
Sparse Core Ops, SparseCore 0:
  189.6 80.1 all-gather.1

commit v4 on v3

--- a/solution.py
+++ b/solution.py
@@ -75,25 +75,203 @@
         copy.wait()
 
 
+class Gather:
+    def __init__(self, dims, me, view, chunks, sems):
+        self.dims, self.view, self.chunks = dims, view, chunks
+        self.role, self.z, self.y, self.x = me
+        self.send, self.recv = sems
+
+    def device(self, z, y, x):
+        _, ny, nx = self.dims
+        return (self.role, (z * ny + y) * nx + x)
+
+    def copies(self, k, which, spans, others, base):
+        out = []
+        for device in others:
+            for span in spans:
+                ref = self.view(which, k, *span)
+                out.append(
+                    remote(ref, ref, self.send.at[k, base], self.recv.at[k, base], device)
+                )
+                base += 1
+        return out
+
+    def along_x(self):
+        nx = self.dims[2]
+        return [self.device(self.z, self.y, (self.x + j) % nx) for j in range(1, nx)]
+
+    def along_y(self):
+        ny = self.dims[1]
+        return [self.device(self.z, (self.y + j) % ny, self.x) for j in range(1, ny)]
+
+    def first(self, k):
+        nz, ny, nx = self.dims
+        slot = (self.y * nx + self.x) * nz + self.z
+        others = [self.device((self.z + j) % nz, self.y, self.x) for j in range(1, nz)]
+        return self.copies(k, None, [(slot, 1)], others, 0)
+
+    def second(self, k):
+        nz, ny, nx = self.dims
+        column = ((self.y * nx + self.x) * nz, nz)
+        base = nz - 1
+        to_x = self.copies(k, 0, [column], self.along_x(), base)
+        return to_x + self.copies(k, 1, [column], self.along_y(), base + nx - 1)
+
+    def third(self, k):
+        nz, ny, nx = self.dims
+        base = nz - 1 + nx - 1 + ny - 1
+        to_y = self.copies(k, 0, [(self.y * nx * nz, nx * nz)], self.along_y(), base)
+        spans = [((b * nx + self.x) * nz, nz) for b in range(ny)]
+        return to_y + self.copies(k, 1, spans, self.along_x(), base + ny - 1)
+
+    @staticmethod
+    def semaphores(dims, chunks):
+        nz, ny, nx = dims
+        count = nz - 1 + 2 * (nx - 1) + 2 * (ny - 1) + (nx - 1) * (ny - 1)
+        return pltpu.SemaphoreType.DMA((len(chunks), count))
+
+
+PART = 64
+LISTEN_GROUPS = 6
+LISTEN_CHUNKS = ((0, 0, 32), (0, 32, 32))
+LISTEN_EVENTS = (
+    ((), ((0, 0), (0, 1))),
+    (((0, 0),), ((1, 0),)),
+    (((1, 0), (0, 1)), ((2, 0), (1, 1))),
+    (((2, 0),), ((3, 0),)),
+    (((1, 1),), ((2, 1),)),
+    (((2, 1),), ((3, 1),)),
+    ((), ()),
+)
+SPELL_GROUPS = 18
+SPELL_CHUNKS = ((0, 0, PART), (1, 0, PART))
+SPELL_EVENTS = (
+    ((), ((0, 0), (0, 1))),
+    ((), ()),
+    (((0, 0),), ((1, 0), (0, 2))),
+    (((0, 1),), ((1, 1), (0, 3))),
+    (((1, 0),), ((2, 0),)),
+    (((1, 1), (0, 2)), ((2, 1), (1, 2), (0, 4))),
+    (((2, 0),), ()),
+    (((0, 3), (2, 1)), ((1, 3),)),
+    (((1, 2),), ((2, 2),)),
+    (((1, 3),), ((2, 3),)),
+    (((0, 4),), ((1, 4),)),
+    (((2, 2),), ()),
+    ((), ()),
+    (((2, 3),), ((3, 3),)),
+    (((1, 4),), ((2, 4),)),
+    ((), ()),
+    ((), ()),
+    (((2, 4),), ((3, 4),)),
+    ((), ()),
+)
+
+
+class Gathers:
+    def __init__(self, dims, role, dp, events, frames, chunks, states, sems):
+        nz, ny, nx = dims
+        me = (role, dp // (ny * nx), (dp // nx) % ny, dp % nx)
+        self.twin = (1 - role, dp)
+        self.role, self.frames, self.chunks, self.events = role, frames, chunks, events
+        send, recv, self.last_send, self.last_recv = sems[:4]
+        self.slot = (me[2] * nx + me[3]) * nz + me[1]
+
+        def half(first, count, which):
+            if which is not None:
+                first, count = first + which * count // 2, count // 2
+            return pl.ds(first, count)
+
+        def view_frames(which, k, first, count):
+            part, *rows = chunks[k]
+            return frames.at[part, role, pl.ds(first, count), half(*rows, which)]
+
+        self.two = Gather(dims, me, view_frames, chunks, (send, recv))
+        self.lead = 0
+        if states is not None:
+            self.lead = states.shape[0]
+
+            def view_states(which, k, first, count):
+                rows = half(0, states.shape[3], which)
+                return states.at[k, :, pl.ds(first, count), rows]
+
+            self.one = Gather(dims, me, view_states, range(self.lead), sems[4:])
+        g = self.two
+        to_z = [g.device((g.z + j) % nz, g.y, g.x) for j in range(1, nz)]
+        self.partners = to_z + g.along_x() + g.along_y() + [self.twin]
+
+    def greet(self):
+        barrier = pltpu.get_barrier_semaphore()
+        for device in self.partners:
+            pl.semaphore_signal(
+                barrier, inc=1, device_id=device, device_id_type=pl.DeviceIdType.MESH
+            )
+
+    def phase(self, n, c):
+        if n == 3:
+            k = c - self.lead
+            part, *rows = self.chunks[k]
+            ref = self.frames.at[part, self.role, :, pl.ds(*rows)]
+            return [remote(ref, ref, self.last_send.at[k], self.last_recv.at[k], self.twin)]
+        gather, k = (self.one, c) if c < self.lead else (self.two, c - self.lead)
+        return (gather.first, gather.second, gather.third)[n](k)
+
+    def begin(self):
+        pl.semaphore_wait(pltpu.get_barrier_semaphore(), len(self.partners))
+
+    def look(self, group):
+        ended, begun = self.events[group]
+        for n, c in ended:
+            wait(self.phase(n, c))
+        for n, c in begun:
+            start(self.phase(n, c))
+
+    def finish(self):
+        for k in range(len(self.chunks)):
+            wait(self.phase(3, self.lead + k))
+
+    @staticmethod
+    def scratch(dims, chunks, states):
+        dma = pltpu.SemaphoreType.DMA
+        sems = [Gather.semaphores(dims, chunks)] * 2 + [dma((len(chunks),))] * 2
+        if states:
+            sems += [Gather.semaphores(dims, range(states))] * 2
+        return sems
+
+
 def listen_forward_kernel(
-    dims, lengths, pairs, w_in, w_rec, bias, rows_out, factors_out, mine_out, other_out, *rest
+    dims, lengths, frames, w_in, w_rec, bias,
+    pairs, rows_out, factors_out, mine_out, other_out, *rest
 ):
     role = lax.axis_index("role")
-    twin = (1 - role, lax.axis_index("dp"))
     if dims is not None:
-        proj, emit, hprev, to_other, cross = rest
-        barrier = pltpu.get_barrier_semaphore()
-        pl.semaphore_signal(
-            barrier, inc=1, device_id=twin, device_id_type=pl.DeviceIdType.MESH
-        )
-        pl.semaphore_wait(barrier, 1)
+        pairs_all, proj, emit, hprev, to_other, cross, *sems = rest
+        gather = Gathers(
+            dims, role, lax.axis_index("dp"), LISTEN_EVENTS, pairs_all, LISTEN_CHUNKS, None, sems
+        )
+        gather.greet()
     else:
         proj, emit, hprev = rest
     utts, time_len, width4 = proj.shape
     units = width4 // 4
+    feat = frames.shape[-1]
+    rows = lax.broadcasted_iota(jnp.int32, (time_len, 2 * time_len), 0)
+    cols = lax.broadcasted_iota(jnp.int32, (time_len, 2 * time_len), 1)
+    for half in range(2):
+        pick = jnp.where(cols == 2 * rows + half, 1.0, 0.0).astype(BF16)
+        for u in range(utts):
+            pairs[u, :, half * feat : (half + 1) * feat] = mm(pick, frames[u]).astype(BF16)
+    if dims is not None:
+        place = pltpu.make_async_copy(
+            pairs.at[role, pl.ds(0, PART)], pairs_all.at[0, role, gather.slot], cross.at[2]
+        )
+        place.start()
     bias_row = bias[...].astype(F32)
     for u in range(utts):
         proj[u] = mm(pairs[u], w_in[...]) + bias_row
+    if dims is not None:
+        place.wait()
+        gather.begin()
     first = lax.broadcasted_iota(jnp.int32, (8, 1), 0) == 0
     row_lengths = jnp.where(first, lengths[0], lengths[1])
 
@@ -116,33 +294,43 @@
         return hidden_next, cell_next
 
     zero = jnp.zeros((8, units), F32)
-    lax.fori_loop(0, time_len, step, (zero, zero))
+    carry = (zero, zero)
+    if dims is None:
+        lax.fori_loop(0, time_len, step, carry)
+    else:
+        count = time_len // LISTEN_GROUPS
+        for group in range(LISTEN_GROUPS):
+            gather.look(group)
+            carry = lax.fori_loop(group * count, (group + 1) * count, step, carry)
     mine_out[...] = emit[role].astype(BF16)
     if dims is None:
         other_out[...] = emit[1 - role].astype(BF16)
     else:
         to_other[...] = emit[1 - role].astype(BF16)
-        crossing = remote(to_other, other_out, cross.at[0], cross.at[1], twin)
+        crossing = remote(to_other, other_out, cross.at[0], cross.at[1], gather.twin)
         crossing.start()
+        gather.look(LISTEN_GROUPS)
     for u in range(utts):
         own = slice(u * time_len, (u + 1) * time_len)
         rows_out[own, :] = hprev[u].astype(BF16)
     if dims is not None:
         crossing.wait()
-
-
-def listen_forward(dims, lengths, pairs, w_in, w_rec, bias):
-    utts, time_len, width = pairs.shape
+        gather.finish()
+
+
+def listen_forward(dims, lengths, frames, w_in, w_rec, bias):
+    utts, time_len, width = frames.shape[0], frames.shape[1] // 2, 2 * frames.shape[2]
     units = w_rec.shape[0]
     vmem = pl.BlockSpec(memory_space=pltpu.VMEM)
     shape = jax.ShapeDtypeStruct
     outs = [
+        shape((utts, time_len, width), BF16),
         shape((utts * time_len, units), BF16),
         shape((utts, time_len, 6 * units), F32),
         shape((time_len, units), BF16),
         shape((time_len, units), BF16),
     ]
-    out_specs = [vmem] * 4
+    out_specs = [vmem] * 5
     scratch = [
         pltpu.VMEM((utts, time_len, 4 * units), F32),
         pltpu.VMEM((utts, time_len, units), F32),
@@ -150,7 +338,11 @@
     ]
     params = dict(vmem_limit_bytes=VMEM_BYTES)
     if dims is not None:
-        scratch += [pltpu.VMEM((time_len, units), BF16), pltpu.SemaphoreType.DMA((2,))]
+        chips = dims[0] * dims[1] * dims[2]
+        outs.append(shape((1, 2, chips, PART, width), BF16))
+        out_specs.append(pl.BlockSpec(memory_space=pl.ANY))
+        scratch += [pltpu.VMEM((time_len, units), BF16), pltpu.SemaphoreType.DMA((3,))]
+        scratch += Gathers.scratch(dims, LISTEN_CHUNKS, 0)
         params.update(collective_id=1, has_side_effects=True)
     return pl.pallas_call(
         functools.partial(listen_forward_kernel, dims),
@@ -159,187 +351,49 @@
         out_specs=out_specs,
         scratch_shapes=scratch,
         compiler_params=pltpu.CompilerParams(**params),
-    )(lengths, pairs, w_in, w_rec, bias)
-
-
-class Gather:
-    def __init__(self, dims, me, view, chunks, sems):
-        self.dims, self.view, self.chunks = dims, view, chunks
-        self.role, self.z, self.y, self.x = me
-        self.send, self.recv = sems
-
-    def device(self, z, y, x):
-        _, ny, nx = self.dims
-        return (self.role, (z * ny + y) * nx + x)
-
-    def copies(self, k, which, spans, others, base):
-        out = []
-        for device in others:
-            for span in spans:
-                ref = self.view(which, k, *span)
-                out.append(
-                    remote(ref, ref, self.send.at[k, base], self.recv.at[k, base], device)
-                )
-                base += 1
-        return out
-
-    def along_x(self):
-        nx = self.dims[2]
-        return [self.device(self.z, self.y, (self.x + j) % nx) for j in range(1, nx)]
-
-    def along_y(self):
-        ny = self.dims[1]
-        return [self.device(self.z, (self.y + j) % ny, self.x) for j in range(1, ny)]
-
-    def first(self, k):
-        nz, ny, nx = self.dims
-        slot = (self.y * nx + self.x) * nz + self.z
-        others = [self.device((self.z + j) % nz, self.y, self.x) for j in range(1, nz)]
-        return self.copies(k, None, [(slot, 1)], others, 0)
-
-    def second(self, k):
-        nz, ny, nx = self.dims
-        column = ((self.y * nx + self.x) * nz, nz)
-        base = nz - 1
-        to_x = self.copies(k, 0, [column], self.along_x(), base)
-        return to_x + self.copies(k, 1, [column], self.along_y(), base + nx - 1)
-
-    def third(self, k):
-        nz, ny, nx = self.dims
-        base = nz - 1 + nx - 1 + ny - 1
-        to_y = self.copies(k, 0, [(self.y * nx * nz, nx * nz)], self.along_y(), base)
-        spans = [((b * nx + self.x) * nz, nz) for b in range(ny)]
-        return to_y + self.copies(k, 1, spans, self.along_x(), base + ny - 1)
-
-    @staticmethod
-    def semaphores(dims, chunks):
-        nz, ny, nx = dims
-        count = nz - 1 + 2 * (nx - 1) + 2 * (ny - 1) + (nx - 1) * (ny - 1)
-        return pltpu.SemaphoreType.DMA((len(chunks), count))
-
-
-ROW_CHUNKS = tuple((96 * k, 96) for k in range(4))
-FRAME_CHUNKS = tuple((32 * k, 32) for k in range(6))
-FRAME_EVENTS = {
-    2: ([(0, 0)], [(1, 0)]),
-    6: ([(1, 0), (0, 1)], [(2, 0), (1, 1)]),
-    10: ([(0, 2)], [(1, 2)]),
-    12: ([(2, 0)], []),
-    14: ([(1, 1), (0, 3)], [(2, 1), (1, 3)]),
-    16: ([(1, 2)], [(2, 2)]),
-    18: ([(0, 4)], [(1, 4)]),
-    20: ([(2, 1)], []),
-    22: ([(1, 3)], [(2, 3)]),
-    24: ([(0, 5)], [(1, 5)]),
-    26: ([(2, 2)], []),
-    28: ([(1, 4), (0, 6)], [(2, 4), (1, 6)]),
-    32: ([(2, 3)], []),
-    34: ([(1, 5), (0, 7)], [(2, 5), (1, 7)]),
-    38: ([(0, 8)], [(1, 8)]),
-    40: ([(2, 4)], [(3, 4)]),
-    42: ([(1, 6), (0, 9)], [(2, 6), (1, 9)]),
-    46: ([(2, 5)], [(3, 5)]),
-    48: ([(1, 7)], [(2, 7)]),
-    52: ([(1, 8)], [(2, 8)]),
-    56: ([(2, 6)], [(3, 6)]),
-    58: ([(1, 9)], [(2, 9)]),
-    64: ([(2, 7)], [(3, 7)]),
-    68: ([(2, 8)], [(3, 8)]),
-    72: ([(2, 9)], [(3, 9)]),
-}
-
-
-class Gathers:
-    def __init__(self, dims, role, dp, states, frames, sems):
-        nz, ny, nx = dims
-        me = (role, dp // (ny * nx), (dp // nx) % ny, dp % nx)
-        self.twin = (1 - role, dp)
-        self.role, self.frames = role, frames
-        row_send, row_recv, frame_send, frame_recv, self.last_send, self.last_recv = sems
-
-        def cut(chunk, which):
-            first, count = chunk
-            if which is not None:
-                first, count = first + which * count // 2, count // 2
-            return pl.ds(first, count)
-
-        def view_states(which, k, first, count):
-            return states.at[pl.ds(first, count), cut(ROW_CHUNKS[k], which)]
-
-        def view_frames(which, k, first, count):
-            return frames.at[role, pl.ds(first, count), cut(FRAME_CHUNKS[k], which)]
-
-        self.one = Gather(dims, me, view_states, ROW_CHUNKS, (row_send, row_recv))
-        self.two = Gather(dims, me, view_frames, FRAME_CHUNKS, (frame_send, frame_recv))
-        self.slot = (me[2] * nx + me[3]) * nz + me[1]
-        one = self.one
-        to_z = [one.device((one.z + j) % nz, one.y, one.x) for j in range(1, nz)]
-        self.partners = to_z + one.along_x() + one.along_y() + [self.twin]
-
-    def phase(self, n, c):
-        if n == 3:
-            k = c - len(ROW_CHUNKS)
-            ref = self.frames.at[self.role, :, pl.ds(*FRAME_CHUNKS[k])]
-            return [remote(ref, ref, self.last_send.at[k], self.last_recv.at[k], self.twin)]
-        gather, k = (self.one, c) if c < len(ROW_CHUNKS) else (self.two, c - len(ROW_CHUNKS))
-        return (gather.first, gather.second, gather.third)[n](k)
-
-    def begin(self):
-        for c in range(len(ROW_CHUNKS) + len(FRAME_CHUNKS)):
-            start(self.phase(0, c))
-
-    def event(self, ended, begun):
-        for n, c in ended:
-            wait(self.phase(n, c))
-        for n, c in begun:
-            start(self.phase(n, c))
-
-    def look(self, step):
-        def some():
-            for at, (ended, begun) in FRAME_EVENTS.items():
-                pl.when(step == at)(functools.partial(self.event, ended, begun))
-
-        pl.when(step % 2 == 0)(some)
-
-    def finish(self, steps):
-        for at, (ended, begun) in FRAME_EVENTS.items():
-            if at >= steps:
-                self.event(ended, begun)
-        for k in range(len(FRAME_CHUNKS)):
-            wait(self.phase(3, len(ROW_CHUNKS) + k))
+    )(lengths, frames, w_in, w_rec, bias)
 
 
 def speller_forward_kernel(
-    dims, lengths, text_lens, pairs, states,
-    mine, other, prev_onehot, target_onehot,
+    dims, lengths, text_lens, chars, pairs, states,
+    mine, other,
     w_lin, w_lhid, b_low, w_uin, w_uhid, b_up, w_key, w_query, vec, w_out, b_out, table,
-    loss, acts, key, keys_proj, key_low, fact1, fact2, q_rows, w_cols, feat_rows, dw_cols,
+    loss, prev_onehot, acts, key, keys_proj, key_low, fact1, fact2, q_rows, w_cols, feat_rows, dw_cols,
     logit_grad_out, *rest
 ):
     role = lax.axis_index("role")
     gather = None
     if dims is not None:
-        pairs_all, states_all, *rest = rest
-        rest, (stage, own_sem), sems = rest[:-8], rest[-8:-6], rest[-6:]
-        gather = Gathers(dims, role, lax.axis_index("dp"), states_all, pairs_all, sems)
-        barrier = pltpu.get_barrier_semaphore()
-        for device in gather.partners:
-            pl.semaphore_signal(
-                barrier, inc=1, device_id=device, device_id_type=pl.DeviceIdType.MESH
+        pairs_all, states_all, emb_proj, s1_rows, s2_rows, hot, stage, own_sem, *sems = rest
+        gather = Gathers(
+            dims, role, lax.axis_index("dp"), SPELL_EVENTS, pairs_all, SPELL_CHUNKS, states_all, sems
+        )
+        gather.greet()
+        load = pltpu.make_async_copy(
+            pairs.at[role, pl.ds(PART, stage.shape[0])], stage, own_sem.at[0]
+        )
+        load.start()
+        parts, utts = states_all.shape[:2]
+        place = [
+            pltpu.make_async_copy(
+                states.at[pl.ds((u * parts + part) * PART, PART)],
+                states_all.at[part, u, gather.slot],
+                own_sem.at[1 + u * parts + part],
             )
-        load = pltpu.make_async_copy(pairs.at[role], stage, own_sem.at[0])
-        load.start()
-        place = [
-            pltpu.make_async_copy(stage, pairs_all.at[role, gather.slot], own_sem.at[1]),
-            pltpu.make_async_copy(states, states_all.at[gather.slot], own_sem.at[2]),
+            for u in range(utts)
+            for part in range(parts)
         ]
-        place[1].start()
-        load.wait()
-        place[0].start()
-        wait(place)
-        pl.semaphore_wait(barrier, len(gather.partners))
-        gather.begin()
-    emb_proj, s1_rows, s2_rows = rest
+        start(place)
+        staged = [
+            pltpu.make_async_copy(
+                stage.at[pl.ds(part * PART, PART)],
+                pairs_all.at[part, role, gather.slot],
+                own_sem.at[1 + len(place) + part],
+            )
+            for part in range(pairs_all.shape[0])
+        ]
+    else:
+        emb_proj, s1_rows, s2_rows, hot = rest
     time_len, units = mine.shape
     steps = emb_proj.shape[0]
     cells = w_lhid.shape[0]
@@ -350,19 +404,34 @@
     key[:, :units] = jnp.where(role == 0, mine[...], other[...])
     key[:, units:] = jnp.where(role == 0, other[...], mine[...])
     keys_proj[...] = mm(key[...], w_key[...])
+    if gather is not None:
+        load.wait()
+        start(staged)
     key_low[...] = mm(key[...], w_lin[embed:, :])
+    ids = lax.broadcasted_iota(jnp.int32, (1, hot.shape[2]), 1)
+
+    def mark(i, previous):
+        here = chars[0, 0, i]
+        hot[0, pl.ds(i, 1), :] = jnp.where(ids == previous, 1.0, 0.0)
+        hot[1, pl.ds(i, 1), :] = jnp.where(ids == here, 1.0, 0.0)
+        return here
+
+    lax.fori_loop(0, steps, mark, 0)
+    prev_onehot[...] = hot[0].astype(BF16)
     emb = mm(prev_onehot[...], table[...]).astype(BF16)
-    emb_proj[...] = mm(emb, w_lin[:embed, :]) + b_low[...].astype(F32)
-    bias_up = b_up[...].astype(F32)
-    vec_row = vec[...].astype(F32)
+    emb_proj[...] = mm(emb, w_lin[:embed, :]) + b_low[...].astype(F32)[None]
+    bias_up = b_up[...].astype(F32)[None]
+    vec_row = vec[...].astype(F32)[None]
     frame_ok = lax.broadcasted_iota(jnp.int32, (time_len, 1), 0) < length
     lane = lax.broadcasted_iota(jnp.int32, w_cols.shape, 1)
     w_cols[...] = jnp.zeros_like(w_cols)
+    if gather is not None:
+        wait(place)
+        wait(staged)
+        gather.begin()
 
     def forward_step(i, carry):
         cell1, cell2, hid1, hid2, ctx_low = carry
-        if gather is not None:
-            gather.look(i)
         at = pl.ds(i, 1)
         pre1 = emb_proj[at, :] + hid1 + ctx_low
         cell1, s1, factors = cell_forward(pre1, cell1)
@@ -402,15 +471,23 @@
 
     zero = jnp.zeros((1, cells), F32)
     wide = jnp.zeros((1, 4 * cells), F32)
-    lax.fori_loop(0, steps, forward_step, (zero, zero, wide, wide, wide))
+    carry = (zero, zero, wide, wide, wide)
+    if gather is None:
+        lax.fori_loop(0, steps, forward_step, carry)
+    else:
+        count = steps // SPELL_GROUPS
+        for group in range(SPELL_GROUPS):
+            gather.look(group)
+            carry = lax.fori_loop(group * count, (group + 1) * count, forward_step, carry)
+        gather.look(SPELL_GROUPS)
 
     w_low = jnp.transpose(w_cols[...])[:steps].astype(BF16)
     ctx = mm(w_low, key[...]).astype(BF16)
     s2_low = s2_rows[...].astype(BF16)
-    logits = mm_nt(s2_low, w_out[:, :cells]) + mm_nt(ctx, w_out[:, cells:]) + b_out[...].astype(F32)
+    logits = mm_nt(s2_low, w_out[:, :cells]) + mm_nt(ctx, w_out[:, cells:]) + b_out[...].astype(F32)[None]
     top = jnp.max(logits, -1, keepdims=True)
     log_total = top + jnp.log(jnp.sum(jnp.exp(logits - top), -1, keepdims=True))
-    target = target_onehot[...]
+    target = hot[1]
     cross = log_total - jnp.sum(logits * target, -1, keepdims=True)
     text = text_len.astype(F32)
     alive = lax.broadcasted_iota(jnp.int32, (steps, 1), 0) < text_len
@@ -427,15 +504,15 @@
     acts[:steps, embed + 2 * units : embed + 2 * units + cells] = s1_rows[...].astype(BF16)
     acts[:steps, embed + 2 * units + cells :] = s2_low
     if gather is not None:
-        gather.finish(steps)
+        gather.finish()
 
 
 def speller_forward(
-    dims, lengths, text_lens, pairs, states, mine, other, prev_onehot, target_onehot,
+    dims, lengths, text_lens, chars, pairs, states, mine, other,
     w_lin, w_lhid, b_low, w_uin, w_uhid, b_up, w_key, w_query, vec, w_out, b_out, table,
 ):
     time_len, units = mine.shape
-    steps, vocab = prev_onehot.shape
+    steps, vocab = chars.shape[2], table.shape[0]
     cells = w_lhid.shape[0]
     att = w_key.shape[1]
     embed = table.shape[1]
@@ -445,6 +522,7 @@
     shape = jax.ShapeDtypeStruct
     outs = [
         shape((1, 1), F32),
+        shape((steps, vocab), BF16),
         shape((pad_steps, embed + 2 * units + 2 * cells), BF16),
         shape((time_len, 2 * units), BF16),
         shape((time_len, att), F32),
@@ -462,27 +540,30 @@
         pltpu.VMEM((steps, 4 * cells), F32),
         pltpu.VMEM((steps, cells), F32),
         pltpu.VMEM((steps, cells), F32),
+        pltpu.VMEM((2, steps, vocab), F32),
     ]
     params = dict(vmem_limit_bytes=VMEM_BYTES)
     if dims is not None:
         chips = dims[0] * dims[1] * dims[2]
         dma = pltpu.SemaphoreType.DMA
-        outs += [shape((2, chips, *pairs.shape[1:]), BF16), shape((chips, *states.shape), BF16)]
+        utts, _, width = pairs.shape
+        parts = time_len // PART
+        high = parts - 1
+        outs.append(shape((high, utts, chips, PART, width), BF16))
+        outs.append(shape((parts, utts, chips, PART, units), BF16))
         out_specs += [pl.BlockSpec(memory_space=pl.ANY)] * 2
-        scratch += [pltpu.VMEM(pairs.shape[1:], BF16), dma((3,))]
-        scratch += [Gather.semaphores(dims, ROW_CHUNKS)] * 2
-        scratch += [Gather.semaphores(dims, FRAME_CHUNKS)] * 2
-        scratch += [dma((len(FRAME_CHUNKS),))] * 2
+        scratch += [pltpu.VMEM((high * PART, width), BF16), dma((1 + high + utts * parts,))]
+        scratch += Gathers.scratch(dims, SPELL_CHUNKS, parts)
         params.update(collective_id=2, has_side_effects=True)
     return pl.pallas_call(
         functools.partial(speller_forward_kernel, dims),
         out_shape=outs,
-        in_specs=[smem] * 2 + [pl.BlockSpec(memory_space=pl.ANY)] + [vmem] * 17,
+        in_specs=[smem] * 3 + [pl.BlockSpec(memory_space=pl.ANY)] + [vmem] * 15,
         out_specs=out_specs,
         scratch_shapes=scratch,
         compiler_params=pltpu.CompilerParams(**params),
     )(
-        lengths, text_lens, pairs, states, mine, other, prev_onehot, target_onehot,
+        lengths, text_lens, chars, pairs, states, mine, other,
         w_lin, w_lhid, b_low, w_uin, w_uhid, b_up, w_key, w_query, vec, w_out, b_out, table,
     )
 
@@ -509,7 +590,7 @@
     units = key.shape[1] // 2
     cells = w_lhid.shape[0]
     embed = acts.shape[1] - 2 * units - 2 * cells
-    vec_row = vec[...].astype(F32)
+    vec_row = vec[...].astype(F32)[None]
     zero = jnp.zeros((1, cells), F32)
     wide = jnp.zeros((1, 4 * cells), BF16)
     keys_acc[...] = jnp.zeros_like(keys_acc)
@@ -736,8 +817,8 @@
 
 def exchange_kernel(
     dims,
-    lengths, factors, grad_mine, grad_other, w_in, w_rec, dp1, dp2, pack, acts_all, pairs_all, rows_all,
-    frames_out, li_out, sp_out, kq_out,
+    lengths, factors, grad_mine, grad_other, w_in, w_rec, dp1, dp2, pack, acts_all, pairs_low, pairs_high, rows_all,
+    frames_out, li_out, sp_out,
     grad_pre, grad_out, acts_buf, pairs_buf, rows_buf, dp_pair, got, got_t, prod, column,
     li_send, li_got, li_rows, li_acc, li_all, fr_send, fr_got, weave,
     pk_pair, pk_x, pk_xsum, pk_y, pk_ysum, pk_z,
@@ -776,19 +857,15 @@
         acts_buf, local_sem.at[0],
     )
     load_acts.start()
-    load_rows = [
-        pltpu.make_async_copy(
-            rows_all.at[c, pl.ds(u * time_len, time_len)],
-            rows_buf.at[pl.ds((u * chips + c) * time_len, time_len), pl.ds(0, units)],
-            local_sem.at[5 + c * utts + u],
-        )
-        for c in range(chips)
-        for u in range(utts)
-    ]
+    load_rows = [pltpu.make_async_copy(rows_all, rows_buf.at[:, pl.ds(0, units)], local_sem.at[1])]
     rows_buf[:, units:] = jnp.ones((rows_buf.shape[0], rows_buf.shape[1] - units), BF16)
     start(load_rows)
-    load_pairs = pltpu.make_async_copy(pairs_all, pairs_buf, local_sem.at[4])
-    load_pairs.start()
+    split = pairs_low.shape[0]
+    load_pairs = [
+        pltpu.make_async_copy(pairs_low, pairs_buf.at[pl.ds(0, split)], local_sem.at[4]),
+        pltpu.make_async_copy(pairs_high, pairs_buf.at[pl.ds(split, pairs_high.shape[0])], local_sem.at[5]),
+    ]
+    start(load_pairs)
     dp_pair[role] = jnp.where(role == 0, dp1[...], dp2[...])
     dp_pair[2] = jnp.where(role == 0, dp2[...], dp1[...])
     grad_out[role] = grad_mine[...].astype(F32)
@@ -1057,15 +1134,16 @@
 
     li_got[dp] = li_send[slot]
     wait(load_rows)
-    load_pairs.wait()
+    wait(load_pairs)
     for n in range(len(STREAMS)):
         wait_stream(n)
 
     def spread(c, _):
         value = li_got[c].astype(F32)
         for u, part in enumerate((value, pltpu.roll(value, 64, 1))):
-            base = pl.multiple_of((u * chips + slot_of(c)) * time_len, 16)
-            li_rows[pl.ds(base, time_len), :] = part.astype(BF16)
+            for p in range(time_len // PART):
+                base = pl.multiple_of(((p * utts + u) * chips + slot_of(c)) * PART, PART)
+                li_rows[pl.ds(base, PART), :] = part[p * PART : (p + 1) * PART].astype(BF16)
         return 0
 
     lax.fori_loop(0, chips, spread, 0)
@@ -1121,24 +1199,11 @@
     lax.fori_loop(0, width // 128, assemble, 0)
     for k in range(len(SP_CHUNKS)):
         wait(sp_last(k))
-    att = kq_out.shape[2]
-    folds = sp_out.shape[2] // att
-    deep = att // folds
-    unfold = [
-        pltpu.make_async_copy(
-            sp_out.at[1, pl.ds(2 * SMALL + which * deep, deep), pl.ds(k * att, att)],
-            kq_out.at[which, pl.ds(k * deep, deep)],
-            local_sem.at[5 + which * folds + k],
-        )
-        for which in range(2)
-        for k in range(folds)
-    ]
-    start(unfold)
-    wait(unfold)
 
 
 def exchange(
-    dims, lengths, factors, grad_mine, grad_other, w_in, w_rec, dp1, dp2, pack, acts_all, pairs_all, rows_all
+    dims, lengths, factors, grad_mine, grad_other, w_in, w_rec, dp1, dp2, pack, acts_all,
+    pairs_low, pairs_high, rows_all,
 ):
     utts, time_len, _ = factors.shape
     units = w_rec.shape[0]
@@ -1150,7 +1215,8 @@
     deep = sum(rows for _, rows in SP_CHUNKS)
     nz, ny, _ = dims
     packed = pack.shape[0]
-    total = pairs_all.shape[1] + units + 64
+    features = pairs_low.shape[1]
+    total = features + units + 64
     feat = w_in.shape[0] // 2
     half_time = time_len // 2
     vmem = pl.BlockSpec(memory_space=pltpu.VMEM)
@@ -1165,15 +1231,14 @@
             shape((utts, time_len, feat), F32),
             shape((total, width), BF16),
             shape((2, deep, wide), BF16),
-            shape((2, cells, cells), BF16),
         ),
-        in_specs=[pl.BlockSpec(memory_space=pltpu.SMEM)] + [vmem] * 8 + [anywhere] * 3,
-        out_specs=(vmem, vmem, anywhere, vmem),
+        in_specs=[pl.BlockSpec(memory_space=pltpu.SMEM)] + [vmem] * 8 + [anywhere] * 4,
+        out_specs=(vmem, vmem, anywhere),
         scratch_shapes=[
             pltpu.VMEM((utts, time_len, width), F32),
             pltpu.VMEM((utts, time_len, units), F32),
             pltpu.VMEM((acts_all.shape[0], span), BF16),
-            pltpu.VMEM(pairs_all.shape, BF16),
+            pltpu.VMEM((chips * utts * time_len, features), BF16),
             pltpu.VMEM((chips * utts * time_len, units + 64), BF16),
             pltpu.VMEM((3, pads, wide), BF16),
             pltpu.VMEM((chips, 2, pads, 128), BF16),
@@ -1194,7 +1259,7 @@
             pltpu.VMEM((packed, nz * 128), BF16),
             pltpu.VMEM((packed, nz * 128), BF16),
             pltpu.VMEM((nz, packed, 128), BF16),
-            dma((5 + chips * utts,)),
+            dma((5 + 2 * 4,)),
             dma((3 + len(SP_CHUNKS),)),
             dma((3 + len(SP_CHUNKS),)),
             dma((chips - 1,)),
@@ -1214,8 +1279,102 @@
         ),
     )(
         lengths, factors, grad_mine, grad_other, w_in, w_rec, dp1, dp2, pack,
-        acts_all, pairs_all, rows_all,
+        acts_all, pairs_low, pairs_high, rows_all,
     )
+
+
+PIECE = 128
+SLOTS = 3
+
+
+def widen_kernel(jobs, sizes, sp, li, *refs):
+    *outs, narrow, wide, few, last, in_sem, out_sem, few_sem = refs
+    g_out, g_table, low_bias, up_bias, g_vec, g_obias, sum_bias = outs[-7:]
+
+    def source(n):
+        which, row, col, out, _, rows = jobs[n]
+        ref = li if which == 2 else sp.at[which]
+        width = outs[out].shape[-1]
+        return pltpu.make_async_copy(
+            ref.at[pl.ds(row, rows), pl.ds(col, width)],
+            narrow.at[n % SLOTS, pl.ds(0, rows), pl.ds(0, width)],
+            in_sem.at[n % SLOTS],
+        )
+
+    def target(n):
+        _, _, _, out, row, rows = jobs[n]
+        width = outs[out].shape[-1]
+        return pltpu.make_async_copy(
+            wide.at[n % SLOTS, pl.ds(0, rows), pl.ds(0, width)],
+            outs[out].at[pl.ds(row, rows)],
+            out_sem.at[n % SLOTS],
+        )
+
+    load_few = [
+        pltpu.make_async_copy(sp.at[1, pl.ds(0, 2 * SMALL)], few, few_sem.at[0]),
+        pltpu.make_async_copy(li.at[pl.ds(sizes[-1], 16)], last, few_sem.at[1]),
+    ]
+    for n in range(min(SLOTS, len(jobs))):
+        source(n).start()
+    start(load_few)
+    for n in range(len(jobs)):
+        source(n).wait()
+        if n >= SLOTS:
+            target(n - SLOTS).wait()
+        rows, width = jobs[n][5], outs[jobs[n][3]].shape[-1]
+        wide[n % SLOTS, :rows, :width] = narrow[n % SLOTS, :rows, :width].astype(F32)
+        target(n).start()
+        if n + SLOTS < len(jobs):
+            source(n + SLOTS).start()
+    wait(load_few)
+    small = few[:SMALL].astype(F32) + few[SMALL:].astype(F32)
+    cells, base, embed, att, vocab, _ = sizes
+    g_out[...] = small[:vocab, :base]
+    g_table[...] = small[:vocab, base : base + embed]
+    base += embed
+    for k in range(4):
+        cut = slice(k * cells, (k + 1) * cells)
+        low_bias[cut] = small[2 + k, base : base + cells]
+        up_bias[cut] = small[6 + k, base : base + cells]
+    g_vec[...] = small[0, base : base + att]
+    g_obias[...] = small[1, base : base + vocab]
+    sum_bias[...] = last[0:1, :].astype(F32)
+    for n in range(max(0, len(jobs) - SLOTS), len(jobs)):
+        target(n).wait()
+
+
+def widen(sp, li, parts, sizes):
+    jobs = []
+    for out, (_, pieces) in enumerate(parts):
+        done = 0
+        for which, row, col, rows in pieces:
+            for at in range(0, rows, PIECE):
+                count = min(PIECE, rows - at)
+                jobs.append((which, row + at, col, out, done, count))
+                done += count
+    cells, base, embed, att, vocab, _ = sizes
+    wide = sp.shape[2]
+    anywhere = pl.BlockSpec(memory_space=pl.ANY)
+    vmem = pl.BlockSpec(memory_space=pltpu.VMEM)
+    dma = pltpu.SemaphoreType.DMA
+    few = ((vocab, base), (vocab, embed), (4 * cells,), (4 * cells,), (att,), (vocab,), (1, li.shape[1]))
+    return pl.pallas_call(
+        functools.partial(widen_kernel, jobs, sizes),
+        out_shape=[jax.ShapeDtypeStruct(shape, F32) for shape, _ in parts]
+        + [jax.ShapeDtypeStruct(shape, F32) for shape in few],
+        in_specs=[anywhere] * 2,
+        out_specs=[anywhere] * len(parts) + [vmem] * len(few),
+        scratch_shapes=[
+            pltpu.VMEM((SLOTS, PIECE, wide), BF16),
+            pltpu.VMEM((SLOTS, PIECE, wide), F32),
+            pltpu.VMEM((2 * SMALL, wide), BF16),
+            pltpu.VMEM((16, li.shape[1]), BF16),
+            dma((SLOTS,)),
+            dma((SLOTS,)),
+            dma((2,)),
+        ],
+        compiler_params=pltpu.CompilerParams(vmem_limit_bytes=VMEM_BYTES),
+    )(sp, li)
 
 
 def shards(
@@ -1247,7 +1406,6 @@
     units = w_rec.shape[0]
     cells = lower_hidden.shape[0]
     vocab, embed = char_table.shape
-    pairs = frames.reshape(utts, time_len, 2 * feat)
     fits = (
         chips % 4 == 0
         and 4 * cells == 128 * chips
@@ -1257,55 +1415,68 @@
         and time_len == SEGMENT * STREAMS[-1][1]
         and embed + 2 * units + cells + 2 * SMALL == sum(rows for _, rows in SP_CHUNKS)
         and embed + 2 * SMALL == SP_CHUNKS[-1][1]
-        and time_len == sum(count for _, count in FRAME_CHUNKS)
-        and utts * time_len == sum(count for _, count in ROW_CHUNKS)
+        and time_len == 3 * PART
+        and characters.shape[2] % SPELL_GROUPS == 0
         and 2 * feat + units + 64 == 2 * sum(rows for _, rows in LI_CHUNKS)
     )
     dims = (chips // 4, 2, 2) if fits else None
-    rows, factors, mine, other = listen_forward(
-        dims, step_lengths, pairs, w_in, w_rec, listen_bias
+    pairs, rows, factors, mine, other, *low_pairs = listen_forward(
+        dims, step_lengths, frames, w_in, w_rec, listen_bias
     )
     if not fits:
         other = lax.ppermute(other, "role", swap)
-    chars = characters[0, 0]
-    previous = jnp.concatenate([jnp.zeros((1,), jnp.int32), chars[:-1]])
-    ids = jnp.arange(vocab)[None, :]
-    prev_onehot = (previous[:, None] == ids).astype(BF16)
-    target_onehot = (chars[:, None] == ids).astype(F32)
-    vec = score_vector[None]
-    loss, acts, key, *kept = speller_forward(
-        dims, step_lengths, char_lengths, pairs, rows, mine, other, prev_onehot, target_onehot,
-        lower_input, lower_hidden, lower_bias[None], upper_input, upper_hidden, upper_bias[None],
-        key_proj, query_proj, vec, output_proj.T, output_bias[None], char_table,
+    vec = score_vector
+    loss, prev_onehot, acts, key, *kept = speller_forward(
+        dims, step_lengths, char_lengths, characters, pairs, rows, mine, other,
+        lower_input, lower_hidden, lower_bias, upper_input, upper_hidden, upper_bias,
+        key_proj, query_proj, vec, output_proj.T, output_bias, char_table,
     )
     if fits:
-        *kept, pairs_all, rows_all = kept
+        *kept, high_pairs, rows_all = kept
     grad_mine, grad_other, dp1, dp2, pack = speller_backward(
         lower_input, lower_hidden, upper_input, upper_hidden, key_proj, query_proj, vec,
         prev_onehot, acts, key, *kept,
     )
     if fits:
-        pairs_all = pairs_all.reshape(chips * utts * time_len, 2 * feat)
+        flat = lambda gathered: gathered.reshape(-1, gathered.shape[-1])
         acts_all = lax.all_gather(acts, ("dp", "role"), tiled=True)
-        frame_grad, li, sp, kq = exchange(
+        frame_grad, li, sp = exchange(
             dims, step_lengths, factors, grad_mine, grad_other, w_in, w_rec,
-            dp1, dp2, pack, acts_all, pairs_all, rows_all,
+            dp1, dp2, pack, acts_all, flat(low_pairs[0]), flat(high_pairs), flat(rows_all),
         )
         width = 2 * feat
-        sum_in, sum_rec = li[:width].astype(F32), li[width : width + units].astype(F32)
-        sum_bias = li[width + units : width + units + 1].astype(F32)
+        att = key_proj.shape[1]
         first = 2 * SMALL
         low, high = first + embed, first + embed + 2 * units
-        lower = (sp[0, first:high].astype(F32), sp[0, high:].astype(F32))
-        upper = (sp[1, low : low + cells].astype(F32), sp[1, low + cells :].astype(F32))
-        small = sp[1, :first]
-        g_key, g_query = kq[0].astype(F32), kq[1].astype(F32)
+        wide = 4 * cells
+        deep = 2 * units * att // wide
+        folded = lambda row: tuple((1, row, col, deep) for col in range(0, wide, att))
+        *layers, sum_in, sum_rec, g_key, g_query, g_out, g_table, low_bias, up_bias, g_vec, g_obias, sum_bias = widen(
+            sp,
+            li,
+            (
+                ((high - first, wide), ((0, first, 0, high - first),)),
+                ((cells, wide), ((0, high, 0, cells),)),
+                ((cells, wide), ((1, low, 0, cells),)),
+                ((cells, wide), ((1, low + cells, 0, cells),)),
+                ((width, 4 * units), ((2, 0, 0, width),)),
+                ((units, 4 * units), ((2, width, 0, units),)),
+                ((2 * units, att), folded(first)),
+                ((cells, att), folded(first + deep)),
+            ),
+            (cells, cells + 2 * units, embed, att, vocab, width + units),
+        )
+        lower, upper = layers[:2], layers[2:]
+        g_out = g_out.T
     else:
         grad_other = lax.ppermute(grad_other, "role", swap)
         pack = lax.psum(pack.astype(F32), ("role", "dp"))
         small = pack[: 2 * SMALL]
         g_key, g_query = (
             unfold(part, cells) for part in jnp.split(pack[2 * SMALL :], 2, axis=0)
+        )
+        low_bias, up_bias, g_vec, g_out, g_obias, g_table = unpack(
+            small, units, cells, key_proj.shape[1], vocab, embed
         )
         pre = listen_backward(step_lengths, factors, grad_mine, grad_other, w_rec)
         flat = pre.reshape(utts * time_len, 4 * units)
@@ -1326,9 +1497,6 @@
         )
         local = lax.psum(local, ("role", "dp"))
         lower, upper = local[:2], local[2:]
-    low_bias, up_bias, g_vec, g_out, g_obias, g_table = unpack(
-        small, units, cells, key_proj.shape[1], vocab, embed
-    )
     return (
         loss, frame_grad, sum_in[None], sum_rec[None], sum_bias,
         *lower, low_bias, *upper, up_bias,

time: 454 us -> 420 us (0.925)
  other arithmetic: 23.2 us -> 0 us
  local copies, waits for them, and re-layouts: 11.1 us -> 0.89 us
    pallas_call x1, Pallas kernels: 128 us -> 99.4 us  [speller_forward(): pl.pallas_call(functools.partial(speller_forward_kernel, dims), out_shape...]
    pallas_call x0 -> x1, Pallas kernels: none -> 17.7 us  [widen(): pl.pallas_call(functools.partial(widen_kernel, jobs, sizes), out_shape=[j...]
    convert_element_type x5 -> x0, other arithmetic: 15.7 us -> none  [the longest x1 6.19 us: shards(): lower = (sp[0, first:high].astype(F32), sp[0, high:].astype(F32))]
    broadcast_in_dim x2 -> x0, other arithmetic: 6.47 us -> none  [the longest x1 4.34 us: shards(): sum_in[None]]
    pallas_call x1, Pallas kernels: 45.6 us -> 52.1 us  [listen_forward(): pl.pallas_call(functools.partial(listen_forward_kernel, dims), out_shape=...]
  transfers between devices with their start and end apart: 1 -> 1, of which waited for: 0 -> 0; matrix products, arithmetic and copies ran while one was open for 0% -> 0% of each run, Pallas kernels for 22% -> 23%
where the time goes in v4:
time: 420 us
  Pallas kernels  402 us (96%)
  between operations  16.5 us (4%)
    pallas_call x1, Pallas kernels, exchange(): pl.pallas_call(functools.partial(exchange_kernel, dims), out_shape=(shape...  135 us
    pallas_call x1, Pallas kernels, speller_forward(): pl.pallas_call(functools.partial(speller_forward_kernel, dims), out_shape...  99.4 us
    pallas_call x1, Pallas kernels, speller_backward(): pl.pallas_call(speller_backward_kernel, out_shape=outs, in_specs=[vmem] *...  97.9 us
    pallas_call x1, Pallas kernels, listen_forward(): pl.pallas_call(functools.partial(listen_forward_kernel, dims), out_shape=...  52.1 us
    pallas_call x1, Pallas kernels, widen(): pl.pallas_call(functools.partial(widen_kernel, jobs, sizes), out_shape=[j...  17.7 us
  transfers between devices with their start and end apart: 1, of which 0 were waited for; matrix products, arithmetic and copies ran while one was open for 0% of the time, Pallas kernels for 23%

profile of v4, /device:TPU:9, one launch (start us, length us, event | category | flops | bytes accessed | tf_op | source)
XLA Modules:
  0.0 419.9 jit_solution(5489528832103709636)
XLA Ops:
  7.2 0.0 all-gather.2.cloned.1.call-start
  7.9 52.1 %shard_map.314 = (bf16[2,192,1024]{2,1,0:T(8,128)(2,1)}, bf16[384,256]{1,0:T(8,128)(2,1)}, f32[2,192,1536]{2,1,0:T(8,128)}, bf16[192,256]{1,0:T(8,128)(2,1)}, bf...) custom-call(s32[2]{0:T(128)} %lengths.5, bf16[2,384,512]{2,1,0:T(8,128)(2,1)} %frames.1, ...), custom_call_target="tpu_custom_call" | custom-call | tf_op jit(solution)/shard_map/pallas_call | solution.py:347
  60.0 99.4 %shard_map.315 = (f32[1,1]{1,0:T(1,128)}, bf16[72,30]{1,0:T(8,128)(2,1)}, bf16[80,1792]{1,0:T(8,128)(2,1)}, bf16[192,512]{1,0:T(8,128)(2,1)}, f32[192,512]{1,0:T...) custom-call(s32[2]{0:T(128)} %lengths.5, ...), custom_call_target="tpu_custom_call" | custom-call | tf_op jit(solution)/shard_map/pallas_call | solution.py:558
  159.4 0.0 all-gather.2.cloned.1.call-update
  159.5 97.9 %shard_map.316 = (bf16[192,256]{1,0:T(8,128)(2,1)}, bf16[192,256]{1,0:T(8,128)(2,1)}, bf16[80,2048]{1,0:T(8,128)(2,1)}, bf16[80,2048]{1,0:T(8,128)(2,1)}, bf16[320,2048]{1,0:T(8,128)(2,1)}) custom-call(bf16[768,2048]{1,0:T(8,128)(2,1)} %w_lin.3, bf16[512,2048]{1,0:T(8,128)(2,1)} %w_lhid.3, bf16[512,2048]{1,0:T(8,128)(2,1)} %w_uin.3, ...), custom_call_target="tpu_custom_call" | custom-call | tf_op jit(solution)/shard_map/pallas_call | solution.py:726
  257.4 0.0 all-gather.2.cloned.1.call-done.acts_all
  257.4 135.2 %shard_map.317 = (f32[2,192,512]{2,1,0:T(8,128)}, bf16[1344,1024]{1,0:T(8,128)(2,1)}, bf16[2,1344,2048]{2,1,0:T(8,128)(2,1)}) custom-call(s32[2]{0:T(128)} %lengths.5, f32[2,192,1536]{2,1,0:T(8,128)} %get-tuple-element.66.factors, bf16[192,256]{1,0:T(8,128)(2,1)} %get-tuple-element.79.grad_mine, bf16[192,256]{1,0:T(8,128)(2,1)} %get-tuple-element.80.grad_other, ...), custom_call_target="tpu_custom_call" | custom-call | tf_op jit(solution)/shard_map/pallas_call | solution.py:1228
  392.6 0.0 copy-start
  392.6 17.7 %shard_map.318 = (f32[768,2048]{1,0:T(8,128)}, f32[512,2048]{1,0:T(8,128)}, f32[512,2048]{1,0:T(8,128)}, f32[512,2048]{1,0:T(8,128)}, f32[1024,1024]{1,0:T(8,128...) custom-call(bf16[2,1344,2048]{2,1,0:T(8,128)(2,1)} %get-tuple-elemen, ...), custom_call_target="tpu_custom_call" | custom-call | tf_op jit(solution)/shard_map/pallas_call | solution.py:1361
  411.0 0.0 copy-done
  411.0 0.9 copy.40
Async XLA Ops:
  7.2 250.2 %all-gather.2.cloned.1.call-start = ((), (), s32[]{:S(2)}) async-start(), calls=%async_computation | async-start | bytes 9461760 | tf_op jit(solution)/shard_map/all_gather | solution.py:1442
  392.6 18.4 %copy-start = (f32[2,192,512]{2,1,0:T(8,128)S(1)}, f32[2,192,512]{2,1,0:T(8,128)}, u32[]{:S(2)}) copy-start(f32[2,192,512]{2,1,0:T(8,128)} %get-tuple-element.123) | copy-start | bytes 2359300
Sparse Core Ops, SparseCore 0:
  159.6 83.0 all-gather.1
